TPU v7x, 256 devices: a whole 4x4x8 slice. The times are simulated.
256 devices in a mesh: rows: 64 (over x, z, core), pairs: 4 (over y).
Axes of the slice: x: 4, y: 4, z: 8, core: 2. Of those that a mesh axis runs over, the one named last changes fastest.
Arguments:
- embeddings: float32 [32768, 512], P('rows'), may hold values from -5.6 to 5.6
- start_basis: float32 [32768, 64], P('rows'), may hold values from -6 to 6
- pair_mask: int32 [64, 5], P('rows'), may hold values from 0 to 1, as said below
Outputs:
- final_basis: float32 [32768, 64], P('rows')
- projected: float32 [64, 64], replicated
Inputs may be any that keep to these rules, and one draw needn't show every extreme that they name: `pair_mask`: offset 0 is listed for every row block, offsets past the last block never; each row block lists 1 to 4 pairs, the first row block exactly 4.
All inputs are finite; a program needn't handle non-finite values.
Results may differ from a plain program's by a relative error of at most 0.017.
Values may be sent and summed in bfloat16 or wider, within the bound.
No kernel may reach another device: no remote copies, remote signals or barrier semaphores. Data moves between devices by JAX's collectives and lax.ppermute only.
A program may use at most 64 MiB of HBM per device.

v0:
```python
import math

import jax
import jax.numpy as jnp
from jax import lax
from jax.sharding import PartitionSpec as P

WIDTH = 512
BLOCK = 512
ITERS = 2


def shifted(block, axis, distance):
    devices = range(lax.axis_size(axis))
    route = [(i - distance, i) for i in devices if i - distance in devices]
    return lax.ppermute(block, axis, route)


def on_device(embeddings, start_basis, pair_mask):
    block_rows = embeddings.shape[0]
    span_count = pair_mask.shape[1]
    columns = start_basis.shape[1]
    docs_total = block_rows * lax.axis_size("rows")
    pair_count = lax.axis_size("pairs")
    pair_index = lax.axis_index("pairs")
    scale_coef = -math.log(BLOCK / 4) / (2 * WIDTH)
    mask_row = pair_mask[0]
    rounded = embeddings.astype(jnp.bfloat16)
    own_sq = jnp.sum(jnp.square(rounded.astype(jnp.float32)), axis=1)
    assigned = jnp.array(
        [offset * pair_count // span_count for offset in range(span_count)], jnp.int32
    )
    active = [
        (mask_row[offset] == 1) & (assigned[offset] == pair_index) for offset in range(span_count)
    ]
    right_blocks = [rounded]
    for offset in range(1, span_count):
        right_blocks.append(shifted(rounded, "rows", -offset))

    def collect(own_term, col_terms):
        reduced = lax.psum(jnp.stack([own_term] + col_terms), "pairs")
        summed = reduced[0]
        for offset in range(1, span_count):
            summed = summed + shifted(reduced[offset], "rows", offset)
        return summed

    right_sq = [jnp.sum(jnp.square(item.astype(jnp.float32)), axis=1) for item in right_blocks]

    def make_tile(offset):
        inner = lax.dot_general(
            rounded,
            right_blocks[offset],
            (((1,), (1,)), ((), ())),
            preferred_element_type=jnp.float32,
        )
        distance = own_sq[:, None] + right_sq[offset][None, :] - 2.0 * inner
        return jnp.exp(distance * scale_coef).astype(jnp.bfloat16)

    zero_row = jnp.zeros((block_rows,), jnp.float32)
    zero_col = jnp.zeros((block_rows,), jnp.float32)
    own_sum = zero_row
    col_sums = []
    for offset in range(span_count):

        def live_degree(offset=offset):
            weights = make_tile(offset)
            return (
                jnp.sum(weights, axis=1, dtype=jnp.float32),
                jnp.sum(weights, axis=0, dtype=jnp.float32),
            )

        def dead_degree():
            return (zero_row, zero_col)

        row_sum, col_sum = lax.cond(active[offset], live_degree, dead_degree)
        own_sum = own_sum + row_sum
        col_sums.append(col_sum)
    degree = collect(own_sum, col_sums[1:])
    inv_root = lax.rsqrt(degree)[:, None]
    current = start_basis
    projected = jnp.zeros((columns, columns), jnp.float32)
    zero_block = jnp.zeros((block_rows, columns), jnp.float32)
    zero_piece = jnp.zeros((block_rows, columns), jnp.float32)
    for step in range(ITERS):
        scaled = (current * inv_root).astype(jnp.bfloat16)
        found = [scaled]
        for near_offset in range(1, span_count):
            found.append(shifted(scaled, "rows", -near_offset))
        near_vecs = found
        own_term = zero_block
        sends = []
        for offset in range(span_count):

            def live_basis(offset=offset):
                weights = make_tile(offset)
                row_term = jnp.dot(weights, near_vecs[offset], preferred_element_type=jnp.float32)
                if offset > 0:
                    col_term = lax.dot_general(
                        weights,
                        scaled,
                        (((0,), (0,)), ((), ())),
                        preferred_element_type=jnp.float32,
                    )
                else:
                    col_term = zero_piece
                return (row_term, col_term)

            def dead_basis():
                return (zero_block, zero_piece)

            row_term, col_term = lax.cond(active[offset], live_basis, dead_basis)
            own_term = own_term + row_term
            if offset > 0:
                sends.append(col_term)
        image = inv_root * collect(own_term, sends)
        gram_part = lax.dot_general(
            image,
            image,
            (((0,), (0,)), ((), ())),
            precision=lax.Precision.HIGHEST,
            preferred_element_type=jnp.float32,
        )
        proj_part = lax.dot_general(
            current,
            image,
            (((0,), (0,)), ((), ())),
            precision=lax.Precision.HIGHEST,
            preferred_element_type=jnp.float32,
        )
        gram_matrix, projected = lax.psum((gram_part, proj_part), "rows")
        gram_matrix = gram_matrix / docs_total
        projected = projected / docs_total
        factor = jnp.linalg.cholesky(gram_matrix)
        current = jax.scipy.linalg.solve_triangular(factor, image.T, lower=True).T
    return (current, projected)


def solution(mesh):
    in_specs = (P("rows", None), P("rows", None), P("rows", None))
    out_specs = (P("rows", None), P())
    return jax.shard_map(
        on_device, mesh=mesh, in_specs=in_specs, out_specs=out_specs, check_vma=False
    )
```

profile of v0, /device:TPU:32, one launch (start us, length us, event | category | flops | bytes accessed | tf_op | source)
XLA Modules:
  0.0 804.5 jit_solution(8314711075359860527)
XLA Ops:
  11.2 3.8 collective-permute-start.1
  22.1 5.8 collective-permute-done.3
  28.1 21.7 %collective-permute-done.2 = bf16[512,512]{1,0:T(8,128)(2,1)S(1)} collective-permute-done((bf16[512,512]{1,0:T(8,128)(2,1)S(1)}, bf16[512,512]{1,0:T(8,128)(2,1)S(1)}, u32[]{:S(2)}, u32[]{:S(2)}) %collective-permute-start.2) | collective-permute-done | bytes 524320 | tf_op jit(solution)/shard_map/ppermute | solution.py:16
  50.0 13.6 %collective-permute-done.1 = bf16[512,512]{1,0:T(8,128)(2,1)S(1)} collective-permute-done((bf16[512,512]{1,0:T(8,128)(2,1)S(1)}, bf16[512,512]{1,0:T(8,128)(2,1)S(1)}, u32[]{:S(2)}, u32[]{:S(2)}) %collective-permute-start.1) | collective-permute-done | bytes 524320 | tf_op jit(solution)/shard_map/ppermute | solution.py:16
  64.2 17.2 %psum.42 = f32[5,512]{1,0:T(8,128)S(1)} all-reduce(f32[5,512]{1,0:T(8,128)S(1)} %stack.103), channel_id=1, replica_groups=mesh['rows'=64,'pairs'=4] {'pairs'}, use_global_device_ids=true, to_apply=%region_24.25 | all-reduce | flops 2560 | bytes 20480 | tf_op jit(solution)/shard_map/psum | solution.py:41
  81.3 8.3 %collective-permute-start.7 = (f32[512]{0:T(512)S(1)}, f32[512]{0:T(512)S(1)}, u32[]{:S(2)}, u32[]{:S(2)}) collective-permute-start(f32[512]{0:T(512)S(1)} %bitcast.182), channel_id=1, source_target_pairs={{0,16},{4,20},{8,24},{12,28},{16,32},{20,36},{24,40},{28,44},{32,4... | collective-permute-start | bytes 6152 | tf_op jit(solution)/shard_map/ppermute | solution.py:16
  91.6 6.0 collective-permute-start.6
  97.5 3.8 collective-permute-start.5
  113.3 3.6 collective-permute-done.11
  120.8 52.7 %all-reduce.4.cloned.1.call-done = f32[5,512,64]{1,2,0:T(8,128)} async-done(((f32[5,512,64]{1,2,0:T(8,128)}), f32[5,512,64]{1,2,0:T(8,128)}) %all-reduce.4.cloned.1.call-update) | async-done | bytes 655376 | tf_op jit(solution)/shard_map/psum | solution.py:41
  176.6 4.5 collective-permute-start.15
  181.1 4.8 collective-permute-start.14
  191.1 6.2 collective-permute-done.13
  198.5 240.1 %psum.44 = f32[64,64]{0,1:T(8,128)S(1)} all-reduce(f32[64,64]{0,1:T(8,128)S(1)} %fusion.110), channel_id=1, replica_groups=mesh['rows'=64,'pairs'=4] {'rows'}, use_global_device_ids=true, to_apply=%region_36.0 | all-reduce | flops 4096 | bytes 32768 | tf_op jit(solution)/shard_map/psum | solution.py:130
  438.7 5.8 cholesky.44
  445.8 4.9 custom-call.6
  453.7 7.5 collective-permute-start.17
  469.0 49.4 %all-reduce.6.cloned.1.call-done = f32[5,512,64]{1,2,0:T(8,128)} async-done(((f32[5,512,64]{1,2,0:T(8,128)}), f32[5,512,64]{1,2,0:T(8,128)}) %all-reduce.6.cloned.1.call-update) | async-done | bytes 655376 | tf_op jit(solution)/shard_map/psum | solution.py:41
  521.5 4.5 collective-permute-start.23
  526.0 4.8 collective-permute-start.22
  536.0 6.2 collective-permute-done.21
  543.7 240.1 %all-reduce = (f32[64,64]{0,1:T(8,128)S(1)}, f32[64,64]{0,1:T(8,128)S(1)}) all-reduce(f32[64,64]{0,1:T(8,128)S(1)} %fusion.111, f32[64,64]{0,1:T(8,128)S(1)} %fusion.112), channel_id=1, replica_groups=mesh['rows'=64,'pairs'=4] {'rows'}, use_global_device_ids=true, to_apply=%region_50.0 | all-reduce | flops 8192 | bytes 65536 | tf_op jit(solution)/shard_map/psum | solution.py:130
  784.6 5.8 cholesky.55
  791.8 4.9 custom-call.7
  (155 shorter events, 64.3 us)
Async XLA Ops:
  7.2 166.4 %all-reduce.4.cloned.1.call-start = ((), (), s32[]{:S(2)}) async-start(), calls=%async_computation | async-start | bytes 1310720 | tf_op jit(solution)/shard_map/psum | solution.py:41
  8.6 19.3 %collective-permute-start.3 = (bf16[512,512]{1,0:T(8,128)(2,1)S(1)}, bf16[512,512]{1,0:T(8,128)(2,1)S(1)}, u32[]{:S(2)}, u32[]{:S(2)}) collective-permute-start(bf16[512,512]{1,0:T(8,128)(2,1)S(1)} %get-tuple-element.359), channel_id=1, source_target_pairs={{16,0},{20,4},{24,8},{28,12},{32,16},{36,20},{40,24},{44,28},{48,3... | collective-permute-start | bytes 1572872 | tf_op jit(solution)/shard_map/ppermute | solution.py:16
  9.9 39.9 %collective-permute-start.2 = (bf16[512,512]{1,0:T(8,128)(2,1)S(1)}, bf16[512,512]{1,0:T(8,128)(2,1)S(1)}, u32[]{:S(2)}, u32[]{:S(2)}) collective-permute-start(bf16[512,512]{1,0:T(8,128)(2,1)S(1)} %get-tuple-element.359), channel_id=1, source_target_pairs={{12,0},{16,4},{20,8},{24,12},{28,16},{32,20},{36,24},{40,28},{44,3... | collective-permute-start | bytes 1572872 | tf_op jit(solution)/shard_map/ppermute | solution.py:16
  11.2 52.5 %collective-permute-start.1 = (bf16[512,512]{1,0:T(8,128)(2,1)S(1)}, bf16[512,512]{1,0:T(8,128)(2,1)S(1)}, u32[]{:S(2)}, u32[]{:S(2)}) collective-permute-start(bf16[512,512]{1,0:T(8,128)(2,1)S(1)} %get-tuple-element.359), channel_id=1, source_target_pairs={{8,0},{12,4},{16,8},{20,12},{24,16},{28,20},{32,24},{36,28},{40,32... | collective-permute-start | bytes 1572872 | tf_op jit(solution)/shard_map/ppermute | solution.py:16
  15.0 48.9 %collective-permute-start = (bf16[512,512]{1,0:T(8,128)(2,1)S(1)}, bf16[512,512]{1,0:T(8,128)(2,1)S(1)}, u32[]{:S(2)}, u32[]{:S(2)}) collective-permute-start(bf16[512,512]{1,0:T(8,128)(2,1)S(1)} %get-tuple-element.359), channel_id=1, source_target_pairs={{4,0},{8,4},{12,8},{16,12},{20,16},{24,20},{28,24},{32,28},{36,32}... | collective-permute-start | bytes 1572872 | tf_op jit(solution)/shard_map/ppermute | solution.py:16
  81.3 20.0 %collective-permute-start.7 = (f32[512]{0:T(512)S(1)}, f32[512]{0:T(512)S(1)}, u32[]{:S(2)}, u32[]{:S(2)}) collective-permute-start(f32[512]{0:T(512)S(1)} %bitcast.182), channel_id=1, source_target_pairs={{0,16},{4,20},{8,24},{12,28},{16,32},{20,36},{24,40},{28,44},{32,4... | collective-permute-start | bytes 6152 | tf_op jit(solution)/shard_map/ppermute | solution.py:16
  89.6 11.8 %collective-permute-start.4 = (f32[512]{0:T(512)S(1)}, f32[512]{0:T(512)S(1)}, u32[]{:S(2)}, u32[]{:S(2)}) collective-permute-start(f32[512]{0:T(512)S(1)} %bitcast.181), channel_id=1, source_target_pairs={{0,4},{4,8},{8,12},{12,16},{16,20},{20,24},{24,28},{28,32},{32,36}... | collective-permute-start | bytes 6152 | tf_op jit(solution)/shard_map/ppermute | solution.py:16
  91.6 9.9 %collective-permute-start.6 = (f32[512]{0:T(512)S(1)}, f32[512]{0:T(512)S(1)}, u32[]{:S(2)}, u32[]{:S(2)}) collective-permute-start(f32[512]{0:T(512)S(1)} %bitcast.180), channel_id=1, source_target_pairs={{0,12},{4,16},{8,20},{12,24},{16,28},{20,32},{24,36},{28,40},{32,4... | collective-permute-start | bytes 6152 | tf_op jit(solution)/shard_map/ppermute | solution.py:16
  103.1 7.3 collective-permute-start.8
  105.0 6.6 collective-permute-start.9
  106.9 6.3 collective-permute-start.10
  108.2 8.7 %collective-permute-start.11 = (bf16[512,64]{0,1:T(8,128)(2,1)S(1)}, bf16[512,64]{0,1:T(8,128)(2,1)S(1)}, u32[]{:S(2)}, u32[]{:S(2)}) collective-permute-start(bf16[512,64]{0,1:T(8,128)(2,1)S(1)} %multiply_convert_fusion.1), channel_id=1, source_target_pairs={{16,0},{20,4},{24,8},{28,12},{32,16},{36,20},{40,24},{44,28},{48,3... | collective-permute-start | bytes 196616 | tf_op jit(solution)/shard_map/ppermute | solution.py:16
  120.8 397.7 %all-reduce.6.cloned.1.call-start = ((), (), s32[]{:S(2)}) async-start(), calls=%async_computation.1 | async-start | bytes 1310720 | tf_op jit(solution)/shard_map/psum | solution.py:41
  174.7 13.7 %collective-permute-start.12 = (f32[512,64]{0,1:T(8,128)S(1)}, f32[512,64]{0,1:T(8,128)S(1)}, u32[]{:S(2)}, u32[]{:S(2)}) collective-permute-start(f32[512,64]{0,1:T(8,128)S(1)} %get-tuple-element.364), channel_id=1, source_target_pairs={{0,4},{4,8},{8,12},{12,16},{16,20},{20,24},{24,28},{28,32},{32,36}... | collective-permute-start | bytes 393224 | tf_op jit(solution)/shard_map/ppermute | solution.py:16
  176.6 11.8 %collective-permute-start.15 = (f32[512,64]{0,1:T(8,128)S(1)}, f32[512,64]{0,1:T(8,128)S(1)}, u32[]{:S(2)}, u32[]{:S(2)}) collective-permute-start(f32[512,64]{0,1:T(8,128)S(1)} %get-tuple-element.365), channel_id=1, source_target_pairs={{0,16},{4,20},{8,24},{12,28},{16,32},{20,36},{24,40},{28,44},{32,4... | collective-permute-start | bytes 393224 | tf_op jit(solution)/shard_map/ppermute | solution.py:16
  181.1 10.0 %collective-permute-start.14 = (f32[512,64]{0,1:T(8,128)S(1)}, f32[512,64]{0,1:T(8,128)S(1)}, u32[]{:S(2)}, u32[]{:S(2)}) collective-permute-start(f32[512,64]{0,1:T(8,128)S(1)} %get-tuple-element.366), channel_id=1, source_target_pairs={{0,12},{4,16},{8,20},{12,24},{16,28},{20,32},{24,36},{28,40},{32,4... | collective-permute-start | bytes 393224 | tf_op jit(solution)/shard_map/ppermute | solution.py:16
  185.8 11.4 %collective-permute-start.13 = (f32[512,64]{0,1:T(8,128)S(1)}, f32[512,64]{0,1:T(8,128)S(1)}, u32[]{:S(2)}, u32[]{:S(2)}) collective-permute-start(f32[512,64]{0,1:T(8,128)S(1)} %get-tuple-element.367), channel_id=1, source_target_pairs={{0,8},{4,12},{8,16},{12,20},{16,24},{20,28},{24,32},{28,36},{32,40... | collective-permute-start | bytes 393224 | tf_op jit(solution)/shard_map/ppermute | solution.py:16
  451.1 13.0 %collective-permute-start.19 = (bf16[512,64]{0,1:T(8,128)(2,1)S(1)}, bf16[512,64]{0,1:T(8,128)(2,1)S(1)}, u32[]{:S(2)}, u32[]{:S(2)}) collective-permute-start(bf16[512,64]{0,1:T(8,128)(2,1)S(1)} %fusion.91), channel_id=1, source_target_pairs={{16,0},{20,4},{24,8},{28,12},{32,16},{36,20},{40,24},{44,28},{48,3... | collective-permute-start | bytes 196616 | tf_op jit(solution)/shard_map/ppermute | solution.py:16
  452.4 12.4 %collective-permute-start.18 = (bf16[512,64]{0,1:T(8,128)(2,1)S(1)}, bf16[512,64]{0,1:T(8,128)(2,1)S(1)}, u32[]{:S(2)}, u32[]{:S(2)}) collective-permute-start(bf16[512,64]{0,1:T(8,128)(2,1)S(1)} %fusion.91), channel_id=1, source_target_pairs={{12,0},{16,4},{20,8},{24,12},{28,16},{32,20},{36,24},{40,28},{44,3... | collective-permute-start | bytes 196616 | tf_op jit(solution)/shard_map/ppermute | solution.py:16
  453.7 12.4 %collective-permute-start.17 = (bf16[512,64]{0,1:T(8,128)(2,1)S(1)}, bf16[512,64]{0,1:T(8,128)(2,1)S(1)}, u32[]{:S(2)}, u32[]{:S(2)}) collective-permute-start(bf16[512,64]{0,1:T(8,128)(2,1)S(1)} %fusion.91), channel_id=1, source_target_pairs={{8,0},{12,4},{16,8},{20,12},{24,16},{28,20},{32,24},{36,28},{40,32... | collective-permute-start | bytes 196616 | tf_op jit(solution)/shard_map/ppermute | solution.py:16
  519.6 13.7 %collective-permute-start.20 = (f32[512,64]{0,1:T(8,128)S(1)}, f32[512,64]{0,1:T(8,128)S(1)}, u32[]{:S(2)}, u32[]{:S(2)}) collective-permute-start(f32[512,64]{0,1:T(8,128)S(1)} %get-tuple-element.360), channel_id=1, source_target_pairs={{0,4},{4,8},{8,12},{12,16},{16,20},{20,24},{24,28},{28,32},{32,36}... | collective-permute-start | bytes 393224 | tf_op jit(solution)/shard_map/ppermute | solution.py:16
  521.5 11.8 %collective-permute-start.23 = (f32[512,64]{0,1:T(8,128)S(1)}, f32[512,64]{0,1:T(8,128)S(1)}, u32[]{:S(2)}, u32[]{:S(2)}) collective-permute-start(f32[512,64]{0,1:T(8,128)S(1)} %get-tuple-element.361), channel_id=1, source_target_pairs={{0,16},{4,20},{8,24},{12,28},{16,32},{20,36},{24,40},{28,44},{32,4... | collective-permute-start | bytes 393224 | tf_op jit(solution)/shard_map/ppermute | solution.py:16
  526.0 10.0 %collective-permute-start.22 = (f32[512,64]{0,1:T(8,128)S(1)}, f32[512,64]{0,1:T(8,128)S(1)}, u32[]{:S(2)}, u32[]{:S(2)}) collective-permute-start(f32[512,64]{0,1:T(8,128)S(1)} %get-tuple-element.362), channel_id=1, source_target_pairs={{0,12},{4,16},{8,20},{12,24},{16,28},{20,32},{24,36},{28,40},{32,4... | collective-permute-start | bytes 393224 | tf_op jit(solution)/shard_map/ppermute | solution.py:16
  530.7 11.4 %collective-permute-start.21 = (f32[512,64]{0,1:T(8,128)S(1)}, f32[512,64]{0,1:T(8,128)S(1)}, u32[]{:S(2)}, u32[]{:S(2)}) collective-permute-start(f32[512,64]{0,1:T(8,128)S(1)} %get-tuple-element.363), channel_id=1, source_target_pairs={{0,8},{4,12},{8,16},{12,20},{16,24},{20,28},{24,32},{28,36},{32,40... | collective-permute-start | bytes 393224 | tf_op jit(solution)/shard_map/ppermute | solution.py:16
  (18 other events, 67.1 us)
Sparse Core Ops, SparseCore 0:
  120.9 52.5 all-reduce.3
  469.2 49.2 all-reduce.5
where the time goes:
time: 810 us; the launch traced here: 804 us
  blocking collectives  497 us (61%)
  waiting for transfers between devices  168 us (21%)
  starting transfers between devices  74.1 us (9%)
  other arithmetic  29.4 us (4%)
  between operations  18 us (2%)
  local copies, waits for them, and re-layouts  13.2 us (2%)
    psum x2, blocking collectives, on_device(): gram_matrix, projected = lax.psum((gram_part, proj_part), 'rows')  480 us
    psum x2, waiting for transfers between devices, collect(): reduced = lax.psum(jnp.stack([own_term] + col_terms), 'pairs')  102 us
    ppermute x24, starting transfers between devices, shifted(): return lax.ppermute(block, axis, route)  74.1 us
    ppermute x24, waiting for transfers between devices, shifted(): return lax.ppermute(block, axis, route)  65.5 us
    psum x1, blocking collectives, collect(): reduced = lax.psum(jnp.stack([own_term] + col_terms), 'pairs')  17.2 us
  transfers between devices with their start and end apart: 26, of which 13 were waited for; matrix products, arithmetic and copies ran while one was open for 1% of the time, Pallas kernels for 0%

commit v1 on v0

v1 whole, which is shorter than its diff:
```python
import math

import jax
import jax.numpy as jnp
from jax import lax
from jax.sharding import Mesh
from jax.sharding import PartitionSpec as P

WIDTH = 512
BLOCK = 512
CHIPS = 32
CORES = 2
PAIRS = 4
REACHES = ((1, -2), (-1, 2))
ALL_AXES = ("chip", "core", "pairs")


def route(step):
    moves = []
    for chip in range(CHIPS):
        for core in range(CORES):
            for pair in range(PAIRS):
                to_chip, to_core, to_pair = step(chip, core, pair)
                source = (chip * CORES + core) * PAIRS + pair
                target = ((to_chip % CHIPS) * CORES + to_core) * PAIRS + to_pair
                moves.append((source, target))
    return moves


def swap_core(array):
    return lax.ppermute(array, "core", [(0, 1), (1, 0)])


def swap_pair(array):
    return lax.ppermute(array, "pairs", [(i, i ^ 1) for i in range(PAIRS)])


def fetch(array, which):
    moves = route(lambda chip, core, pair: (chip - REACHES[pair % 2][which], core, pair))
    return lax.ppermute(array, ALL_AXES, moves)


def deliver(array, which):
    moves = route(lambda chip, core, pair: (chip + REACHES[pair % 2][which], core, pair))
    return lax.ppermute(array, ALL_AXES, moves)


def listed(reach, own_mask, other_mask, core, row_core):
    offset = 2 * reach + core - row_core
    ahead = jnp.sum(jnp.where(jnp.arange(5) == offset, own_mask, 0.0))
    behind = jnp.sum(jnp.where(jnp.arange(5) == -offset, other_mask, 0.0))
    return jnp.where(offset >= 0, ahead, behind)


def on_device(embeddings, start_basis, pair_mask):
    scale_coef = -math.log(BLOCK / 4) / (2 * WIDTH)
    core = lax.axis_index("core")
    pair = lax.axis_index("pairs")
    parity = pair % 2
    docs_total = BLOCK * CHIPS * CORES

    rounded = embeddings.astype(jnp.bfloat16)
    mask_rows = jnp.pad(pair_mask.astype(jnp.bfloat16), ((0, 15), (0, WIDTH - 5)))
    packed = jnp.concatenate([rounded, mask_rows])
    near = fetch(packed, 0)
    far = fetch(packed, 1)
    mate = swap_core(packed)
    mate_basis = swap_core(start_basis)

    half = BLOCK // 2
    own_half = lax.dynamic_slice_in_dim(rounded, parity * half, half, 0)
    rows = jnp.concatenate([rounded, mate[:BLOCK]])
    cols = jnp.concatenate([near[:BLOCK], far[:BLOCK], own_half])

    def mask_of(array):
        return array[BLOCK, :5].astype(jnp.float32)

    own_mask = pair_mask[0].astype(jnp.float32)
    mate_mask = mask_of(mate)
    flags = []
    for which, source in ((0, near), (1, far), (2, packed)):
        reach = 0 if which == 2 else jnp.where(parity == 0, REACHES[0][which], REACHES[1][which])
        flags.append(
            [
                listed(reach, own_mask, mask_of(source), core, core),
                listed(reach, mate_mask, mask_of(source), core, 1 - core),
            ]
        )
    flag_rows = [jnp.repeat(jnp.stack(f), BLOCK)[None, :] for f in flags]

    def norms(array):
        return jnp.sum(jnp.square(array.astype(jnp.float32)), axis=1)

    rows_sq = norms(rows)
    cols_sq = norms(cols)
    inner = lax.dot_general(
        cols, rows, (((1,), (1,)), ((), ())), preferred_element_type=jnp.float32
    )
    weights = jnp.exp((cols_sq[:, None] + rows_sq[None, :] - 2.0 * inner) * scale_coef)
    flag = jnp.concatenate(
        [
            jnp.broadcast_to(flag_rows[0], (BLOCK, 2 * BLOCK)),
            jnp.broadcast_to(flag_rows[1], (BLOCK, 2 * BLOCK)),
            jnp.broadcast_to(flag_rows[2], (half, 2 * BLOCK)),
        ]
    )
    weights = jnp.where(flag > 0, weights, 0.0).astype(jnp.bfloat16)
    partial_degree = jnp.sum(weights, axis=0, dtype=jnp.float32)
    swapped = swap_core(partial_degree)
    partial_degree = partial_degree + jnp.concatenate([swapped[BLOCK:], swapped[:BLOCK]])
    degree = partial_degree + swap_pair(partial_degree)
    inv_root = lax.rsqrt(degree)[:, None]
    own_root = inv_root[:BLOCK]

    def apply(vectors):
        terms = jnp.dot(weights, vectors, preferred_element_type=jnp.float32)
        if terms.shape[1] == 128:
            terms = terms[:, :64] + terms[:, 64:]
        got = deliver(terms[:BLOCK], 0) + deliver(terms[BLOCK : 2 * BLOCK], 1)
        own = terms[2 * BLOCK :]
        blank = jnp.zeros_like(own)
        own = jnp.where(parity == 0, jnp.concatenate([own, blank]), jnp.concatenate([blank, own]))
        got = got + own
        return got + swap_pair(got)

    scaled = (jnp.concatenate([start_basis, mate_basis]) * inv_root).astype(jnp.bfloat16)
    first = own_root * apply(scaled)
    scaled = own_root * first
    scaled = jnp.concatenate([scaled, swap_core(scaled)])
    high = scaled.astype(jnp.bfloat16)
    low = (scaled - high.astype(jnp.float32)).astype(jnp.bfloat16)
    second = own_root * apply(jnp.concatenate([high, low], axis=1))

    def inner_product(left, right):
        return lax.dot_general(
            left,
            right,
            (((0,), (0,)), ((), ())),
            precision=lax.Precision.HIGHEST,
            preferred_element_type=jnp.float32,
        )

    cross = inner_product(first, second)
    products = jnp.concatenate(
        [
            jnp.concatenate([inner_product(first, first), inner_product(second, second)], axis=1),
            jnp.concatenate([cross[:32], cross[32:]], axis=1),
        ]
    )
    share = 96 // (CORES * PAIRS)
    mine = lax.dynamic_slice_in_dim(products, (core * PAIRS + pair) * share, share, 0)
    theirs = lax.dynamic_slice_in_dim(products, ((1 - core) * PAIRS + pair) * share, share, 0)
    mine = mine + swap_core(theirs)
    gathered = lax.all_to_all(jnp.tile(mine, (CHIPS, 1)), "chip", 0, 0, tiled=True)
    mine = jnp.sum(gathered.reshape(CHIPS, share, 128), axis=0)
    products = lax.all_to_all(
        jnp.tile(mine, (CORES * PAIRS, 1)), ("core", "pairs"), 0, 0, tiled=True
    )
    products = products / docs_total
    gram_first = products[:64, :64]
    gram_second = products[:64, 64:]
    cross = jnp.concatenate([products[64:, :64], products[64:, 64:]])

    eye = jnp.eye(64, dtype=jnp.float32)
    factors = jnp.linalg.cholesky(jnp.stack([gram_first, gram_second]))
    inverses = jax.scipy.linalg.solve_triangular(factors, jnp.stack([eye, eye]), lower=True)
    exact = lax.Precision.HIGHEST
    basis = jnp.dot(second, inverses[1].T, precision=exact)
    projected = jnp.dot(jnp.dot(inverses[0], cross, precision=exact), inverses[0].T, precision=exact)
    return basis, projected


def solution(mesh):
    grid = Mesh(mesh.devices.reshape(CHIPS, CORES, PAIRS), ALL_AXES)
    rows = P(("chip", "core"), None)
    return jax.shard_map(
        on_device, mesh=grid, in_specs=(rows, rows, rows), out_specs=(rows, P()), check_vma=False
    )
```

time: 810 us -> 153 us (0.19)
  blocking collectives: 497 us -> 0 us
  waiting for transfers between devices: 168 us -> 51.4 us
  starting transfers between devices: 74.1 us -> 51.4 us
  between operations: 18 us -> 7.11 us
  local copies, waits for them, and re-layouts: 13.2 us -> 2.79 us
    psum x3 -> x0, blocking collectives: 497 us -> none  [the longest x2 480 us: on_device(): gram_matrix, projected = lax.psum((gram_part, proj_part), 'rows')]
    psum x2 -> x0, waiting for transfers between devices: 102 us -> none  [collect(): reduced = lax.psum(jnp.stack([own_term] + col_terms), 'pairs')]
    ppermute x24 -> x14, starting transfers between devices: 74.1 us -> 40.1 us  [the longest x4 18.3 us: deliver(): return lax.ppermute(array, ALL_AXES, moves)]
    ppermute x24 -> x14, waiting for transfers between devices: 65.5 us -> 33.5 us  [the longest x2 13.8 us: fetch(): return lax.ppermute(array, ALL_AXES, moves)]
    all_to_all x0 -> x2, waiting for transfers between devices: none -> 17.9 us  [the longest x1 12.6 us: on_device(): lax.all_to_all(jnp.tile(mine, (CHIPS, 1)), 'chip', 0, 0, tiled=True)]
    all_to_all x0 -> x2, starting transfers between devices: none -> 11.3 us  [the longest x1 6.79 us: on_device(): lax.all_to_all(jnp.tile(mine, (CHIPS, 1)), 'chip', 0, 0, tiled=True)]
    unnamed x39 -> x12, local copies, waits for them, and re-layouts: 8.62 us -> 0.4 us
    another operation x10 -> x11, other arithmetic: 24.1 us -> 22.7 us  [the longest x5 11.9 us: on_device(): factors = jnp.linalg.cholesky(jnp.stack([gram_first, gram_second]))]
  transfers between devices with their start and end apart: 26 -> 16, of which waited for: 13 -> 13; matrix products, arithmetic and copies ran while one was open for 1% -> 2% of each run, Pallas kernels for 0% -> 0%
where the time goes in v1:
time: 153 us; the launch traced here: 151 us
  starting transfers between devices  51.4 us (34%)
  waiting for transfers between devices  51.4 us (34%)
  other arithmetic  28.3 us (18%)
  matrix products  10.2 us (7%)
  between operations  7.11 us (5%)
  local copies, waits for them, and re-layouts  2.79 us (2%)
    ppermute x4, starting transfers between devices, deliver(): return lax.ppermute(array, ALL_AXES, moves)  18.3 us
    ppermute x3, starting transfers between devices, swap_pair(): return lax.ppermute(array, 'pairs', [(i, i ^ 1) for i in range(PAIRS)])  18 us
    ppermute x2, waiting for transfers between devices, fetch(): return lax.ppermute(array, ALL_AXES, moves)  13.8 us
    all_to_all x1, waiting for transfers between devices, on_device(): lax.all_to_all(jnp.tile(mine, (CHIPS, 1)), 'chip', 0, 0, tiled=True)  12.6 us
    another operation x5, other arithmetic, on_device(): factors = jnp.linalg.cholesky(jnp.stack([gram_first, gram_second]))  11.9 us
    another operation x3, other arithmetic, on_device(): jax.scipy.linalg.solve_triangular(factors, jnp.stack([eye, eye]), lower=T...  9.92 us
    ppermute x4, waiting for transfers between devices, deliver(): return lax.ppermute(array, ALL_AXES, moves)  8.29 us
    ppermute x3, waiting for transfers between devices, swap_pair(): return lax.ppermute(array, 'pairs', [(i, i ^ 1) for i in range(PAIRS)])  7.81 us
  transfers between devices with their start and end apart: 16, of which 13 were waited for; matrix products, arithmetic and copies ran while one was open for 2% of the time, Pallas kernels for 0%

profile of v1, /device:TPU:32, one launch (start us, length us, event | category | flops | bytes accessed | tf_op | source)
XLA Modules:
  0.0 151.2 jit_solution(6276348293414456067)
XLA Ops:
  2.6 1.9 %collective-permute-start = (bf16[528,512]{1,0:T(8,128)(2,1)S(1)}, bf16[528,512]{1,0:T(8,128)(2,1)S(1)}, u32[]{:S(2)}, u32[]{:S(2)}) collective-permute-start(bf16[528,512]{1,0:T(8,128)(2,1)S(1)} %fusion.1), channel_id=1, source_target_pairs={{0,248},{1,9},{2,250},{3,11},{4,252},{5,13},{6,254},{7,15},{8,0},{... | collective-permute-start | bytes 1622024 | tf_op jit(solution)/shard_map/ppermute | solution.py:40
  4.6 1.6 %collective-permute-start.2 = (bf16[528,512]{1,0:T(8,128)(2,1)S(1)}, bf16[528,512]{1,0:T(8,128)(2,1)S(1)}, u32[]{:S(2)}, u32[]{:S(2)}) collective-permute-start(bf16[528,512]{1,0:T(8,128)(2,1)S(1)} %fusion.1), channel_id=1, source_target_pairs={{0,16},{1,241},{2,18},{3,243},{4,20},{5,245},{6,22},{7,247},{8,24}... | collective-permute-start | bytes 1622024 | tf_op jit(solution)/shard_map/ppermute | solution.py:40
  6.9 10.0 %collective-permute-done = bf16[528,512]{1,0:T(8,128)(2,1)S(1)} collective-permute-done((bf16[528,512]{1,0:T(8,128)(2,1)S(1)}, bf16[528,512]{1,0:T(8,128)(2,1)S(1)}, u32[]{:S(2)}, u32[]{:S(2)}) %collective-permute-start) | collective-permute-done | bytes 540704 | tf_op jit(solution)/shard_map/ppermute | solution.py:40
  20.8 3.8 %collective-permute-done.2 = bf16[528,512]{1,0:T(8,128)(2,1)S(1)} collective-permute-done((bf16[528,512]{1,0:T(8,128)(2,1)S(1)}, bf16[528,512]{1,0:T(8,128)(2,1)S(1)}, u32[]{:S(2)}, u32[]{:S(2)}) %collective-permute-start.2) | collective-permute-done | bytes 540704 | tf_op jit(solution)/shard_map/ppermute | solution.py:40
  31.3 5.4 %convert_reduce_fusion = (f32[1024]{0:T(1024)S(1)}, bf16[1280,1024]{1,0:T(8,128)(2,1)S(1)}) fusion(bf16[512,512]{1,0:T(8,128)(2,1)S(1)} %slice.123, bf16[512,512]{1,0:T(8,128)(2,1)S(1)} %convert_element_type.75, bf16[256,512]{1,0:T(8,128)(2,1)S(1)} %constant_dynamic-slice_fusion.1, bf16[512,512]{1,0:T(8,128)(2,1)S(1)} %slice.122, ...), kind=kOutput, calls=%fused_computation.1 | convolution fusion | flops 1362623488 | bytes 10236928 | tf_op jit(solution)/shard_map/dot_general | solution.py:96
  37.9 8.2 %collective-permute-start.4 = (f32[1024]{0:T(1024)S(1)}, f32[1024]{0:T(1024)S(1)}, u32[]{:S(2)}, u32[]{:S(2)}) collective-permute-start(f32[1024]{0:T(1024)S(1)} %maximum_add_fusion), channel_id=1, source_target_pairs={{0,1},{1,0},{2,3},{3,2},{4,5},{5,4},{6,7},{7,6},{8,9},{9,8},{10,11... | collective-permute-start | bytes 12296 | tf_op jit(solution)/shard_map/ppermute | solution.py:35
  46.1 1.6 %collective-permute-done.4 = f32[1024]{0:T(1024)S(1)} collective-permute-done((f32[1024]{0:T(1024)S(1)}, f32[1024]{0:T(1024)S(1)}, u32[]{:S(2)}, u32[]{:S(2)}) %collective-permute-start.4) | collective-permute-done | bytes 4128 | tf_op jit(solution)/shard_map/ppermute | solution.py:35
  48.6 4.6 %collective-permute-start.6 = (f32[512,64]{0,1:T(8,128)S(1)}, f32[512,64]{0,1:T(8,128)S(1)}, u32[]{:S(2)}, u32[]{:S(2)}) collective-permute-start(f32[512,64]{0,1:T(8,128)S(1)} %get-tuple-element.18), channel_id=1, source_target_pairs={{0,8},{1,249},{2,10},{3,251},{4,12},{5,253},{6,14},{7,255},{8,16},... | collective-permute-start | bytes 393224 | tf_op jit(solution)/shard_map/ppermute | solution.py:45
  53.3 9.9 %collective-permute-start.7 = (f32[512,64]{0,1:T(8,128)S(1)}, f32[512,64]{0,1:T(8,128)S(1)}, u32[]{:S(2)}, u32[]{:S(2)}) collective-permute-start(f32[512,64]{0,1:T(8,128)S(1)} %get-tuple-element.17), channel_id=1, source_target_pairs={{0,240},{1,17},{2,242},{3,19},{4,244},{5,21},{6,246},{7,23},{8,248... | collective-permute-start | bytes 393224 | tf_op jit(solution)/shard_map/ppermute | solution.py:45
  63.1 2.5 %collective-permute-done.7 = f32[512,64]{0,1:T(8,128)S(1)} collective-permute-done((f32[512,64]{0,1:T(8,128)S(1)}, f32[512,64]{0,1:T(8,128)S(1)}, u32[]{:S(2)}, u32[]{:S(2)}) %collective-permute-start.7) | collective-permute-done | bytes 131104 | tf_op jit(solution)/shard_map/ppermute | solution.py:45
  65.7 4.7 %collective-permute-start.8 = (f32[512,64]{0,1:T(8,128)S(1)}, f32[512,64]{0,1:T(8,128)S(1)}, u32[]{:S(2)}, u32[]{:S(2)}) collective-permute-start(f32[512,64]{0,1:T(8,128)S(1)} %select_add_fusion.1), channel_id=1, source_target_pairs={{0,1},{1,0},{2,3},{3,2},{4,5},{5,4},{6,7},{7,6},{8,9},{9,8},{10,11... | collective-permute-start | bytes 393224 | tf_op jit(solution)/shard_map/ppermute | solution.py:35
  70.4 3.5 %collective-permute-done.8 = f32[512,64]{0,1:T(8,128)S(1)} collective-permute-done((f32[512,64]{0,1:T(8,128)S(1)}, f32[512,64]{0,1:T(8,128)S(1)}, u32[]{:S(2)}, u32[]{:S(2)}) %collective-permute-start.8) | collective-permute-done | bytes 131104 | tf_op jit(solution)/shard_map/ppermute | solution.py:35
  74.1 1.3 collective-permute-done.9
  76.8 3.6 %collective-permute-start.11 = (f32[512,64]{0,1:T(8,128)S(1)}, f32[512,64]{0,1:T(8,128)S(1)}, u32[]{:S(2)}, u32[]{:S(2)}) collective-permute-start(f32[512,64]{0,1:T(8,128)S(1)} %get-tuple-element.15), channel_id=1, source_target_pairs={{0,240},{1,17},{2,242},{3,19},{4,244},{5,21},{6,246},{7,23},{8,248... | collective-permute-start | bytes 393224 | tf_op jit(solution)/shard_map/ppermute | solution.py:45
  80.3 2.0 %collective-permute-done.10 = f32[512,64]{0,1:T(8,128)S(1)} collective-permute-done((f32[512,64]{0,1:T(8,128)S(1)}, f32[512,64]{0,1:T(8,128)S(1)}, u32[]{:S(2)}, u32[]{:S(2)}) %collective-permute-start.10) | collective-permute-done | bytes 131104 | tf_op jit(solution)/shard_map/ppermute | solution.py:45
  82.3 3.8 %collective-permute-done.11 = f32[512,64]{0,1:T(8,128)S(1)} collective-permute-done((f32[512,64]{0,1:T(8,128)S(1)}, f32[512,64]{0,1:T(8,128)S(1)}, u32[]{:S(2)}, u32[]{:S(2)}) %collective-permute-start.11) | collective-permute-done | bytes 131104 | tf_op jit(solution)/shard_map/ppermute | solution.py:45
  86.1 5.1 %collective-permute-start.12 = (f32[512,64]{0,1:T(8,128)S(1)}, f32[512,64]{0,1:T(8,128)S(1)}, u32[]{:S(2)}, u32[]{:S(2)}) collective-permute-start(f32[512,64]{0,1:T(8,128)S(1)} %select_add_fusion), channel_id=1, source_target_pairs={{0,1},{1,0},{2,3},{3,2},{4,5},{5,4},{6,7},{7,6},{8,9},{9,8},{10,11... | collective-permute-start | bytes 393224 | tf_op jit(solution)/shard_map/ppermute | solution.py:35
  91.6 2.7 %collective-permute-done.12 = f32[512,64]{0,1:T(8,128)S(1)} collective-permute-done((f32[512,64]{0,1:T(8,128)S(1)}, f32[512,64]{0,1:T(8,128)S(1)}, u32[]{:S(2)}, u32[]{:S(2)}) %collective-permute-start.12) | collective-permute-done | bytes 131104 | tf_op jit(solution)/shard_map/ppermute | solution.py:35
  96.9 6.8 %all-to-all-start = ((f32[32,12,128]{2,1,0:T(8,128)}), f32[32,12,128]{2,1,0:T(8,128)S(1)}, u32[]{:S(2)}, u32[]{:S(2)}) async-start(f32[32,12,128]{2,1,0:T(8,128)} %tile.4), calls=%async_computation | async-start | bytes 524288 | tf_op jit(solution)/shard_map/all_to_all | solution.py:154
  103.7 12.6 %all-to-all-done = f32[32,12,128]{2,1,0:T(8,128)S(1)} async-done(((f32[32,12,128]{2,1,0:T(8,128)}), f32[32,12,128]{2,1,0:T(8,128)S(1)}, u32[]{:S(2)}, u32[]{:S(2)}) %all-to-all-start) | async-done | bytes 196640 | tf_op jit(solution)/shard_map/all_to_all | solution.py:154
  117.0 4.5 %all-to-all-start.1 = ((f32[8,12,128]{2,1,0:T(8,128)}), f32[8,12,128]{2,1,0:T(8,128)S(1)}, u32[]{:S(2)}, u32[]{:S(2)}) async-start(f32[8,12,128]{2,1,0:T(8,128)} %tile.5), calls=%async_computation.1 | async-start | bytes 131072 | tf_op jit(solution)/shard_map/all_to_all | solution.py:156
  121.5 5.3 %all-to-all-done.1 = f32[8,12,128]{2,1,0:T(8,128)S(1)} async-done(((f32[8,12,128]{2,1,0:T(8,128)}), f32[8,12,128]{2,1,0:T(8,128)S(1)}, u32[]{:S(2)}, u32[]{:S(2)}) %all-to-all-start.1) | async-done | bytes 49184 | tf_op jit(solution)/shard_map/all_to_all | solution.py:156
  127.3 11.7 %custom-call.8 = f32[2,64,64]{2,1,0:T(8,128)S(1)} custom-call(f32[2,64,64]{2,1,0:T(8,128)S(1)} %fusion.13), custom_call_target="Cholesky" | custom-call | tf_op jit(solution)/shard_map/jit(cholesky)/cholesky | solution.py:165
  139.2 9.8 %custom-call.9 = f32[2,1,64,64]{2,3,1,0:T(8,128)S(1)} custom-call(f32[2,1,64,64]{3,2,1,0:T(8,128)S(1)} %select_bitcast_fusion), custom_call_target="InvertDiagBlocksLowerTriangular" | custom-call | tf_op jit(solution)/shard_map/jit(_solve_triangular)/vmap()/triangular_solve | solution.py:166
  (86 shorter events, 17.2 us)
Async XLA Ops:
  0.6 5.6 %copy-start.1 = (s32[1,5]{1,0:T(1,128)S(1)}, s32[1,5]{1,0:T(1,128)}, u32[]{:S(2)}) copy-start(s32[1,5]{1,0:T(1,128)} %param.5) | copy-start | bytes 64
  2.6 14.3 %collective-permute-start = (bf16[528,512]{1,0:T(8,128)(2,1)S(1)}, bf16[528,512]{1,0:T(8,128)(2,1)S(1)}, u32[]{:S(2)}, u32[]{:S(2)}) collective-permute-start(bf16[528,512]{1,0:T(8,128)(2,1)S(1)} %fusion.1), channel_id=1, source_target_pairs={{0,248},{1,9},{2,250},{3,11},{4,252},{5,13},{6,254},{7,15},{8,0},{... | collective-permute-start | bytes 1622024 | tf_op jit(solution)/shard_map/ppermute | solution.py:40
  4.6 13.0 %collective-permute-start.1 = (bf16[528,512]{1,0:T(8,128)(2,1)S(1)}, bf16[528,512]{1,0:T(8,128)(2,1)S(1)}, u32[]{:S(2)}, u32[]{:S(2)}) collective-permute-start(bf16[528,512]{1,0:T(8,128)(2,1)S(1)} %fusion.1), channel_id=1, source_target_pairs={{0,4},{4,0},{1,5},{5,1},{2,6},{6,2},{3,7},{7,3},{8,12},{12,8},{9,1... | collective-permute-start | bytes 1622024 | tf_op jit(solution)/shard_map/ppermute | solution.py:31
  4.6 20.0 %collective-permute-start.2 = (bf16[528,512]{1,0:T(8,128)(2,1)S(1)}, bf16[528,512]{1,0:T(8,128)(2,1)S(1)}, u32[]{:S(2)}, u32[]{:S(2)}) collective-permute-start(bf16[528,512]{1,0:T(8,128)(2,1)S(1)} %fusion.1), channel_id=1, source_target_pairs={{0,16},{1,241},{2,18},{3,243},{4,20},{5,245},{6,22},{7,247},{8,24}... | collective-permute-start | bytes 1622024 | tf_op jit(solution)/shard_map/ppermute | solution.py:40
  31.3 14.8 %copy-start = (f32[512,64]{0,1:T(8,128)S(1)}, f32[512,64]{0,1:T(8,128)}, u32[]{:S(2)}) copy-start(f32[512,64]{0,1:T(8,128)} %param.4) | copy-start | bytes 393220
  36.7 1.3 collective-permute-start.3
  37.9 9.8 %collective-permute-start.4 = (f32[1024]{0:T(1024)S(1)}, f32[1024]{0:T(1024)S(1)}, u32[]{:S(2)}, u32[]{:S(2)}) collective-permute-start(f32[1024]{0:T(1024)S(1)} %maximum_add_fusion), channel_id=1, source_target_pairs={{0,1},{1,0},{2,3},{3,2},{4,5},{5,4},{6,7},{7,6},{8,9},{9,8},{10,11... | collective-permute-start | bytes 12296 | tf_op jit(solution)/shard_map/ppermute | solution.py:35
  46.1 1.6 %collective-permute-start.5 = (f32[512,64]{0,1:T(8,128)S(1)}, f32[512,64]{0,1:T(8,128)S(1)}, u32[]{:S(2)}, u32[]{:S(2)}) collective-permute-start(f32[512,64]{0,1:T(8,128)S(1)} %copy-done), channel_id=1, source_target_pairs={{0,4},{4,0},{1,5},{5,1},{2,6},{6,2},{3,7},{7,3},{8,12},{12,8},{9,1... | collective-permute-start | bytes 393224 | tf_op jit(solution)/shard_map/ppermute | solution.py:31
  48.6 14.5 %collective-permute-start.6 = (f32[512,64]{0,1:T(8,128)S(1)}, f32[512,64]{0,1:T(8,128)S(1)}, u32[]{:S(2)}, u32[]{:S(2)}) collective-permute-start(f32[512,64]{0,1:T(8,128)S(1)} %get-tuple-element.18), channel_id=1, source_target_pairs={{0,8},{1,249},{2,10},{3,251},{4,12},{5,253},{6,14},{7,255},{8,16},... | collective-permute-start | bytes 393224 | tf_op jit(solution)/shard_map/ppermute | solution.py:45
  53.3 12.4 %collective-permute-start.7 = (f32[512,64]{0,1:T(8,128)S(1)}, f32[512,64]{0,1:T(8,128)S(1)}, u32[]{:S(2)}, u32[]{:S(2)}) collective-permute-start(f32[512,64]{0,1:T(8,128)S(1)} %get-tuple-element.17), channel_id=1, source_target_pairs={{0,240},{1,17},{2,242},{3,19},{4,244},{5,21},{6,246},{7,23},{8,248... | collective-permute-start | bytes 393224 | tf_op jit(solution)/shard_map/ppermute | solution.py:45
  65.7 8.3 %collective-permute-start.8 = (f32[512,64]{0,1:T(8,128)S(1)}, f32[512,64]{0,1:T(8,128)S(1)}, u32[]{:S(2)}, u32[]{:S(2)}) collective-permute-start(f32[512,64]{0,1:T(8,128)S(1)} %select_add_fusion.1), channel_id=1, source_target_pairs={{0,1},{1,0},{2,3},{3,2},{4,5},{5,4},{6,7},{7,6},{8,9},{9,8},{10,11... | collective-permute-start | bytes 393224 | tf_op jit(solution)/shard_map/ppermute | solution.py:35
  74.0 1.4 collective-permute-start.9
  76.5 5.8 %collective-permute-start.10 = (f32[512,64]{0,1:T(8,128)S(1)}, f32[512,64]{0,1:T(8,128)S(1)}, u32[]{:S(2)}, u32[]{:S(2)}) collective-permute-start(f32[512,64]{0,1:T(8,128)S(1)} %get-tuple-element.16), channel_id=1, source_target_pairs={{0,8},{1,249},{2,10},{3,251},{4,12},{5,253},{6,14},{7,255},{8,16},... | collective-permute-start | bytes 393224 | tf_op jit(solution)/shard_map/ppermute | solution.py:45
  76.8 9.3 %collective-permute-start.11 = (f32[512,64]{0,1:T(8,128)S(1)}, f32[512,64]{0,1:T(8,128)S(1)}, u32[]{:S(2)}, u32[]{:S(2)}) collective-permute-start(f32[512,64]{0,1:T(8,128)S(1)} %get-tuple-element.15), channel_id=1, source_target_pairs={{0,240},{1,17},{2,242},{3,19},{4,244},{5,21},{6,246},{7,23},{8,248... | collective-permute-start | bytes 393224 | tf_op jit(solution)/shard_map/ppermute | solution.py:45
  86.1 8.1 %collective-permute-start.12 = (f32[512,64]{0,1:T(8,128)S(1)}, f32[512,64]{0,1:T(8,128)S(1)}, u32[]{:S(2)}, u32[]{:S(2)}) collective-permute-start(f32[512,64]{0,1:T(8,128)S(1)} %select_add_fusion), channel_id=1, source_target_pairs={{0,1},{1,0},{2,3},{3,2},{4,5},{5,4},{6,7},{7,6},{8,9},{9,8},{10,11... | collective-permute-start | bytes 393224 | tf_op jit(solution)/shard_map/ppermute | solution.py:35
  94.9 1.3 collective-permute-start.13
  96.9 19.4 %all-to-all-start = ((f32[32,12,128]{2,1,0:T(8,128)}), f32[32,12,128]{2,1,0:T(8,128)S(1)}, u32[]{:S(2)}, u32[]{:S(2)}) async-start(f32[32,12,128]{2,1,0:T(8,128)} %tile.4), calls=%async_computation | async-start | bytes 524288 | tf_op jit(solution)/shard_map/all_to_all | solution.py:154
  117.0 9.8 %all-to-all-start.1 = ((f32[8,12,128]{2,1,0:T(8,128)}), f32[8,12,128]{2,1,0:T(8,128)S(1)}, u32[]{:S(2)}, u32[]{:S(2)}) async-start(f32[8,12,128]{2,1,0:T(8,128)} %tile.5), calls=%async_computation.1 | async-start | bytes 131072 | tf_op jit(solution)/shard_map/all_to_all | solution.py:156

commit v2 on v1

v2 whole, which is shorter than its diff:
```python
import math

import jax
import jax.numpy as jnp
from jax import lax
from jax.experimental import pallas as pl
from jax.experimental.pallas import tpu as pltpu
from jax.sharding import Mesh
from jax.sharding import PartitionSpec as P

WIDTH = 512
BASIS = 64
BLOCK = 512
HALF = BLOCK // 2
QUARTER = BLOCK // 4
DOCS = 32768
REACH = 5
CHUNK = 256
EXPONENT = -math.log(BLOCK / 4) / (2 * WIDTH) * math.log2(math.e)
UNLISTED = -1e30
CHIPS = 32
CORES = 2
PAIRS = 4
PARITIES = (0, 1, 1, 0)
HALVES = (0, 0, 1, 1)
NEAR = (1, -1)
FAR = (-2, 2)
ALL_AXES = ("chip", "core", "pairs")
NT = (((1,), (1,)), ((), ()))
EXACT = lax.Precision.HIGHEST


def move(array, reaches, sign):
    moves = []
    for chip in range(CHIPS):
        for core in range(CORES):
            for pair in range(PAIRS):
                to_chip = (chip + sign * reaches[PARITIES[pair]]) % CHIPS
                source = (chip * CORES + core) * PAIRS + pair
                target = (to_chip * CORES + core) * PAIRS + pair
                moves.append((source, target))
    return lax.ppermute(array, ALL_AXES, moves)


def swap_core(array):
    return lax.ppermute(array, "core", [(0, 1), (1, 0)])


def swap_parity(array):
    return lax.ppermute(array, "pairs", [(i, i ^ 1) for i in range(PAIRS)])


def swap_half(array):
    return lax.ppermute(array, "pairs", [(i, PAIRS - 1 - i) for i in range(PAIRS)])


def pack_kernel(place_ref, mask_ref, embeddings_ref, start_ref, full_out, half_out, start_out):
    half = place_ref[2]
    lane = lax.broadcasted_iota(jnp.int32, (16, WIDTH), 1)
    row = jnp.zeros((16, WIDTH), jnp.float32)
    for offset in range(REACH):
        row = jnp.where(lane == offset, mask_ref[0, offset].astype(jnp.float32), row)
    row = row.astype(jnp.bfloat16)
    full_out[:BLOCK, :] = embeddings_ref[...].astype(jnp.bfloat16)
    full_out[BLOCK:, :] = row
    sent = embeddings_ref[pl.ds(pl.multiple_of(half * HALF, HALF), HALF), :]
    half_out[:HALF, :] = sent.astype(jnp.bfloat16)
    half_out[HALF:, :] = row
    start_out[...] = start_ref[...].T


def column_bias(reach, own_mask, mate_mask, other_mask, core):
    lane = lax.broadcasted_iota(jnp.int32, (1, 128), 1)
    found = []
    for mask, row_core in ((own_mask, core), (mate_mask, 1 - core)):
        offset = 2 * reach + core - row_core
        ahead = jnp.where((lane == offset) & (lane < REACH), mask, 0.0)
        behind = jnp.where((lane == -offset) & (lane > 0) & (lane < REACH), other_mask, 0.0)
        flag = jnp.sum(ahead + behind, axis=1, keepdims=True)
        found.append(jnp.where(flag > 0, 0.0, UNLISTED))
    return found


def mask_row(ref):
    return ref[ref.shape[0] - 16 :, :128].astype(jnp.float32)[:1]


def norms(array):
    return EXPONENT * jnp.sum(jnp.square(array.astype(jnp.float32)), axis=1, keepdims=True)


def write_tiles(row_refs, biases, cols, out_ref):
    count = cols.shape[0]
    cols_sq = jnp.broadcast_to(norms(cols), (count, 128)).T[:1]
    for part, (row_ref, bias) in enumerate(zip(row_refs, biases)):
        shift = cols_sq + bias
        for first in range(0, BLOCK, CHUNK):
            rows = row_ref[first : first + CHUNK, :]
            inner = lax.dot_general(rows, cols, NT, preferred_element_type=jnp.float32)
            tile = jnp.exp2(inner * (-2.0 * EXPONENT) + norms(rows) + shift)
            start = part * BLOCK + first
            out_ref[start : start + CHUNK, :] = tile.astype(jnp.bfloat16)
    ones = jnp.ones((8, count), jnp.bfloat16)
    return lax.dot_general(ones, out_ref[...], NT, preferred_element_type=jnp.float32)[:1]


def near_kernel(place_ref, own_ref, mate_ref, near_ref, near_out, own_out, sum_out):
    core, parity, half = place_ref[0], place_ref[1], place_ref[2]
    reach = jnp.where(parity == 0, NEAR[0], NEAR[1])
    masks = mask_row(own_ref), mask_row(mate_ref)
    rows = (own_ref, mate_ref)
    start = pl.multiple_of((2 * half + parity) * QUARTER, QUARTER)
    bias = column_bias(0, *masks, masks[0], core)
    total = write_tiles(rows, bias, own_ref[pl.ds(start, QUARTER), :], own_out)
    bias = column_bias(reach, *masks, mask_row(near_ref), core)
    sum_out[...] = total + write_tiles(rows, bias, near_ref[:HALF, :], near_out)


def far_kernel(place_ref, own_ref, mate_ref, far_ref, sum_ref, far_out, sum_out):
    core, parity = place_ref[0], place_ref[1]
    reach = jnp.where(parity == 0, FAR[0], FAR[1])
    masks = mask_row(own_ref), mask_row(mate_ref)
    bias = column_bias(reach, *masks, mask_row(far_ref), core)
    rows = (own_ref, mate_ref)
    sum_out[...] = sum_ref[...] + write_tiles(rows, bias, far_ref[:HALF, :], far_out)


def multiply(vectors, far_ref, near_ref, own_ref, far_out, near_out, own_out):
    for weights_ref, out_ref in ((far_ref, far_out), (near_ref, near_out), (own_ref, own_out)):
        found = jnp.dot(vectors, weights_ref[...], preferred_element_type=jnp.float32)
        if found.shape[0] > BASIS:
            found = found[:BASIS] + found[BASIS:]
        out_ref[...] = found


def first_kernel(
    degree_ref, other_ref, own_start, mate_start, far, near, own, far_out, near_out, own_out, root_out
):
    root = lax.rsqrt(degree_ref[...] + other_ref[...])
    root_out[...] = root
    scaled = jnp.concatenate(
        [own_start[...] * root[:, :BLOCK], mate_start[...] * root[:, BLOCK:]], axis=1
    )
    multiply(scaled.astype(jnp.bfloat16), far, near, own, far_out, near_out, own_out)


def second_kernel(root_ref, own_ref, mate_ref, far, near, own, far_out, near_out, own_out):
    root = root_ref[...]
    scaled = jnp.concatenate([own_ref[...], mate_ref[...]], axis=1) * root * root
    high = scaled.astype(jnp.bfloat16)
    low = (scaled - high.astype(jnp.float32)).astype(jnp.bfloat16)
    multiply(jnp.concatenate([high, low]), far, near, own, far_out, near_out, own_out)


def products_kernel(root_ref, first_ref, second_ref, image_out, products_out):
    root = root_ref[:, :BLOCK]
    image = second_ref[...] * root
    image_out[...] = image
    both = jnp.concatenate([first_ref[...] * root, image])
    found = lax.dot_general(both, both, NT, precision=EXACT, preferred_element_type=jnp.float32)
    left = lax.broadcasted_iota(jnp.int32, (BASIS, 128), 1) < BASIS
    products_out[:BASIS, :] = jnp.where(left, found[:BASIS], found[BASIS:])
    products_out[BASIS:, :] = jnp.concatenate([found[:32, BASIS:], found[32:64, BASIS:]], axis=1)


def finish_kernel(products_ref, image_ref, basis_ref, projected_ref):
    work = products_ref[:BASIS, :] * (1.0 / DOCS)
    row = lax.broadcasted_iota(jnp.int32, (BASIS, 128), 0)
    lane = lax.broadcasted_iota(jnp.int32, (BASIS, 128), 1)
    left = lane < BASIS
    for j in range(BASIS):
        column = jnp.where(left, work[:, j : j + 1], work[:, BASIS + j : BASIS + j + 1])
        pivot_row = work[j : j + 1, :] + jnp.where(lane[:1] % BASIS == j, 1.0, 0.0)
        factor = jnp.where(row > j, column / column[j : j + 1, :], 0.0)
        work = work - factor * pivot_row
    diagonal = lane % BASIS == row
    pivots = jnp.where(diagonal, work, 0.0)
    scale = jnp.where(
        left,
        jnp.sum(pivots[:, :BASIS], axis=1, keepdims=True),
        jnp.sum(pivots[:, BASIS:], axis=1, keepdims=True),
    )
    inverse = jnp.where(diagonal, 1.0, jnp.where(lane % BASIS < row, work, 0.0)) * lax.rsqrt(scale)
    cross = jnp.concatenate([products_ref[BASIS:, :BASIS], products_ref[BASIS:, BASIS:]])
    first = inverse[:, :BASIS]
    half = jnp.dot(
        first, cross * (1.0 / DOCS), precision=EXACT, preferred_element_type=jnp.float32
    )
    projected_ref[...] = lax.dot_general(
        half, first, NT, precision=EXACT, preferred_element_type=jnp.float32
    )
    basis = jnp.dot(
        inverse[:, BASIS:], image_ref[...], precision=EXACT, preferred_element_type=jnp.float32
    )
    basis_ref[...] = basis.T


def call(kernel, outs, operands, scalars=0):
    vmem = pl.BlockSpec(memory_space=pltpu.VMEM)
    smem = pl.BlockSpec(memory_space=pltpu.SMEM)
    return pl.pallas_call(
        kernel,
        out_shape=[jax.ShapeDtypeStruct(shape, dtype) for shape, dtype in outs],
        in_specs=[smem] * scalars + [vmem] * (len(operands) - scalars),
        out_specs=[vmem] * len(outs),
        compiler_params=pltpu.CompilerParams(vmem_limit_bytes=32 * 2**20),
    )(*operands)


def on_device(embeddings, start_basis, pair_mask):
    f32, bf16 = jnp.float32, jnp.bfloat16
    wide = 2 * BLOCK
    core = lax.axis_index("core")
    pair = lax.axis_index("pairs")
    parity = jnp.where((pair == 1) | (pair == 2), 1, 0)
    half = jnp.where(pair >= 2, 1, 0)
    place = jnp.stack([core, parity, half]).astype(jnp.int32)

    packed, sent, own_start = call(
        pack_kernel,
        [((BLOCK + 16, WIDTH), bf16), ((HALF + 16, WIDTH), bf16), ((BASIS, BLOCK), f32)],
        (place, pair_mask, embeddings, start_basis),
        scalars=2,
    )
    far = move(sent, FAR, -1)
    near = move(sent, NEAR, -1)
    mate = swap_core(packed)
    mate_start = swap_core(own_start)
    near_weights, own_weights, sums = call(
        near_kernel,
        [((wide, HALF), bf16), ((wide, QUARTER), bf16), ((1, wide), f32)],
        (place, packed, mate, near),
        scalars=1,
    )
    far_weights, sums = call(
        far_kernel,
        [((wide, HALF), bf16), ((1, wide), f32)],
        (place, packed, mate, far, sums),
        scalars=1,
    )
    other = swap_core(sums)
    sums = sums + jnp.concatenate([other[:, BLOCK:], other[:, :BLOCK]], axis=1)
    sums = sums + swap_parity(sums)
    weights = (far_weights, near_weights, own_weights)
    terms = [((BASIS, HALF), f32), ((BASIS, HALF), f32), ((BASIS, QUARTER), f32)]

    def collect(far_term, near_term, own_term):
        total = move(far_term, FAR, 1) + move(near_term, NEAR, 1)
        blank = jnp.zeros_like(own_term)
        total = total + jnp.where(
            parity == 0,
            jnp.concatenate([own_term, blank], axis=1),
            jnp.concatenate([blank, own_term], axis=1),
        )
        total = total + swap_parity(total)
        other = swap_half(total)
        return jnp.where(
            half == 0,
            jnp.concatenate([total, other], axis=1),
            jnp.concatenate([other, total], axis=1),
        )

    far_term, near_term, own_term, root = call(
        first_kernel,
        terms + [((1, wide), f32)],
        (sums, swap_half(sums), own_start, mate_start, *weights),
    )
    first = collect(far_term, near_term, own_term)
    second = collect(*call(second_kernel, terms, (root, first, swap_core(first), *weights)))
    image, products = call(
        products_kernel, [((BASIS, BLOCK), f32), ((96, 128), f32)], (root, first, second)
    )
    products = products + swap_core(products)
    for bit in (1, 2, 4, 8, 16):
        other = lax.ppermute(products, "chip", [(i, i ^ bit) for i in range(CHIPS)])
        products = products + other
    return call(
        finish_kernel, [((BLOCK, BASIS), f32), ((BASIS, BASIS), f32)], (products, image)
    )


def solution(mesh):
    grid = Mesh(mesh.devices.reshape(CHIPS, CORES, PAIRS), ALL_AXES)
    rows = P(("chip", "core"), None)
    return jax.shard_map(
        on_device, mesh=grid, in_specs=(rows, rows, rows), out_specs=(rows, P()), check_vma=False
    )
```

time: 153 us -> 118 us (0.77)
  other arithmetic: 28.3 us -> 0.21 us
  starting transfers between devices: 51.4 us -> 37.5 us
  waiting for transfers between devices: 51.4 us -> 63.3 us
  Pallas kernels: 0 us -> 11.3 us
  matrix products: 10.2 us -> 0 us
  between operations: 7.11 us -> 0.81 us
    ppermute x9 -> x17, waiting for transfers between devices: 29.9 us -> 60.1 us  [the longest x5 25.3 us: on_device(): other = lax.ppermute(products, 'chip', [(i, i ^ bit) for i in range(CHIPS)])]
    another operation x11 -> x1, other arithmetic: 22.7 us -> 0.08 us  [on_device(): place = jnp.stack([core, parity, half]).astype(jnp.int32)]
    all_to_all x2 -> x0, waiting for transfers between devices: 17.9 us -> none  [the longest x1 12.6 us: on_device(): lax.all_to_all(jnp.tile(mine, (CHIPS, 1)), 'chip', 0, 0, tiled=True)]
    pallas_call x0 -> x7, Pallas kernels: none -> 11.3 us  [call(): pl.pallas_call(kernel, out_shape=[jax.ShapeDtypeStruct(shape, dtype) for...]
    all_to_all x2 -> x0, starting transfers between devices: 11.3 us -> none  [the longest x1 6.79 us: on_device(): lax.all_to_all(jnp.tile(mine, (CHIPS, 1)), 'chip', 0, 0, tiled=True)]
    dot_general x9 -> x0, matrix products: 9.94 us -> none  [the longest x1 5.37 us: on_device(): lax.dot_general(cols, rows, (((1,), (1,)), ((), ())), preferred_element_t...]
    reduce_sum x7 -> x0, other arithmetic: 3.24 us -> none  [the longest x2 1.36 us: listed(): ahead = jnp.sum(jnp.where(jnp.arange(5) == offset, own_mask, 0.0))]
    ppermute x9 -> x17, starting transfers between devices: 39.9 us -> 36.8 us  [the longest x6 20.5 us: move(): return lax.ppermute(array, ALL_AXES, moves)]
  transfers between devices with their start and end apart: 16 -> 22, of which waited for: 13 -> 18; matrix products, arithmetic and copies ran while one was open for 2% -> 0% of each run, Pallas kernels for 0% -> 2%
where the time goes in v2:
time: 118 us; the launch traced here: 117 us
  waiting for transfers between devices  63.3 us (54%)
  starting transfers between devices  37.5 us (32%)
  Pallas kernels  11.3 us (10%)
  local copies, waits for them, and re-layouts  3.6 us (3%)
    ppermute x5, waiting for transfers between devices, on_device(): other = lax.ppermute(products, 'chip', [(i, i ^ bit) for i in range(CHIPS)])  25.3 us
    ppermute x6, starting transfers between devices, move(): return lax.ppermute(array, ALL_AXES, moves)  20.5 us
    ppermute x6, waiting for transfers between devices, move(): return lax.ppermute(array, ALL_AXES, moves)  15.4 us
    pallas_call x7, Pallas kernels, call(): pl.pallas_call(kernel, out_shape=[jax.ShapeDtypeStruct(shape, dtype) for...  11.3 us
    ppermute x3, waiting for transfers between devices, swap_parity(): return lax.ppermute(array, 'pairs', [(i, i ^ 1) for i in range(PAIRS)])  10.1 us
    ppermute x3, waiting for transfers between devices, swap_half(): lax.ppermute(array, 'pairs', [(i, PAIRS - 1 - i) for i in range(PAIRS)])  9.22 us
    ppermute x3, starting transfers between devices, swap_half(): lax.ppermute(array, 'pairs', [(i, PAIRS - 1 - i) for i in range(PAIRS)])  6.9 us
    ppermute x5, starting transfers between devices, on_device(): other = lax.ppermute(products, 'chip', [(i, i ^ bit) for i in range(CHIPS)])  5.55 us
  transfers between devices with their start and end apart: 22, of which 18 were waited for; matrix products, arithmetic and copies ran while one was open for 0% of the time, Pallas kernels for 2%

profile of v2, /device:TPU:32, one launch (start us, length us, event | category | flops | bytes accessed | tf_op | source)
XLA Modules:
  0.0 116.8 jit_solution(4303948620447124739)
XLA Ops:
  4.3 1.9 %collective-permute-start.2 = (bf16[272,512]{1,0:T(8,128)(2,1)S(1)}, bf16[272,512]{1,0:T(8,128)(2,1)S(1)}, u32[]{:S(2)}, u32[]{:S(2)}) collective-permute-start(bf16[272,512]{1,0:T(8,128)(2,1)S(1)} %get-tuple-element.20), channel_id=1, source_target_pairs={{0,248},{1,9},{2,10},{3,251},{4,252},{5,13},{6,14},{7,255},{8,0},{... | collective-permute-start | bytes 835592 | tf_op jit(solution)/shard_map/ppermute | solution.py:42
  7.8 5.8 %collective-permute-done.2.near_ref = bf16[272,512]{1,0:T(8,128)(2,1)S(1)} collective-permute-done((bf16[272,512]{1,0:T(8,128)(2,1)S(1)}, bf16[272,512]{1,0:T(8,128)(2,1)S(1)}, u32[]{:S(2)}, u32[]{:S(2)}) %collective-permute-start.2) | collective-permute-done | bytes 278560 | tf_op jit(solution)/shard_map/ppermute | solution.py:42
  15.4 4.8 %collective-permute-done.1.far_ref = bf16[272,512]{1,0:T(8,128)(2,1)S(1)} collective-permute-done((bf16[272,512]{1,0:T(8,128)(2,1)S(1)}, bf16[272,512]{1,0:T(8,128)(2,1)S(1)}, u32[]{:S(2)}, u32[]{:S(2)}) %collective-permute-start.1) | collective-permute-done | bytes 278560 | tf_op jit(solution)/shard_map/ppermute | solution.py:42
  22.6 3.6 %collective-permute-start.4 = (f32[1,1024]{1,0:T(1,128)S(1)}, f32[1,1024]{1,0:T(1,128)S(1)}, u32[]{:S(2)}, u32[]{:S(2)}) collective-permute-start(f32[1,1024]{1,0:T(1,128)S(1)} %maximum_add_fusion), channel_id=1, source_target_pairs={{0,1},{1,0},{2,3},{3,2},{4,5},{5,4},{6,7},{7,6},{8,9},{9,8},{10,11... | collective-permute-start | bytes 12296 | tf_op jit(solution)/shard_map/ppermute | solution.py:50
  27.8 2.2 %collective-permute-start.5 = (f32[1,1024]{1,0:T(1,128)S(1)}, f32[1,1024]{1,0:T(1,128)S(1)}, u32[]{:S(2)}, u32[]{:S(2)}) collective-permute-start(f32[1,1024]{1,0:T(1,128)S(1)} %add.51.degree_ref), channel_id=1, source_target_pairs={{0,3},{1,2},{2,1},{3,0},{4,7},{5,6},{6,5},{7,4},{8,11},{9,10},{10,... | collective-permute-start | bytes 12296 | tf_op jit(solution)/shard_map/ppermute | solution.py:54
  30.0 2.6 %collective-permute-done.5.other_ref = f32[1,1024]{1,0:T(1,128)S(1)} collective-permute-done((f32[1,1024]{1,0:T(1,128)S(1)}, f32[1,1024]{1,0:T(1,128)S(1)}, u32[]{:S(2)}, u32[]{:S(2)}) %collective-permute-start.5) | collective-permute-done | bytes 4128 | tf_op jit(solution)/shard_map/ppermute | solution.py:54
  33.0 7.1 %collective-permute-start.7 = (f32[64,256]{1,0:T(8,128)S(1)}, f32[64,256]{1,0:T(8,128)S(1)}, u32[]{:S(2)}, u32[]{:S(2)}) collective-permute-start(f32[64,256]{1,0:T(8,128)S(1)} %get-tuple-element.28), channel_id=1, source_target_pairs={{0,240},{1,17},{2,18},{3,243},{4,244},{5,21},{6,22},{7,247},{8,248... | collective-permute-start | bytes 196616 | tf_op jit(solution)/shard_map/ppermute | solution.py:42
  40.1 3.1 %collective-permute-start.8 = (f32[64,256]{1,0:T(8,128)S(1)}, f32[64,256]{1,0:T(8,128)S(1)}, u32[]{:S(2)}, u32[]{:S(2)}) collective-permute-start(f32[64,256]{1,0:T(8,128)S(1)} %get-tuple-element.29), channel_id=1, source_target_pairs={{0,8},{1,249},{2,250},{3,11},{4,12},{5,253},{6,254},{7,15},{8,16},... | collective-permute-start | bytes 196616 | tf_op jit(solution)/shard_map/ppermute | solution.py:42
  43.2 2.9 %collective-permute-done.8 = f32[64,256]{1,0:T(8,128)S(1)} collective-permute-done((f32[64,256]{1,0:T(8,128)S(1)}, f32[64,256]{1,0:T(8,128)S(1)}, u32[]{:S(2)}, u32[]{:S(2)}) %collective-permute-start.8) | collective-permute-done | bytes 65568 | tf_op jit(solution)/shard_map/ppermute | solution.py:42
  46.2 4.3 %collective-permute-done.9 = f32[64,256]{1,0:T(8,128)S(1)} collective-permute-done((f32[64,256]{1,0:T(8,128)S(1)}, f32[64,256]{1,0:T(8,128)S(1)}, u32[]{:S(2)}, u32[]{:S(2)}) %collective-permute-start.9) | collective-permute-done | bytes 65568 | tf_op jit(solution)/shard_map/ppermute | solution.py:50
  50.5 2.3 %collective-permute-start.10 = (f32[64,256]{1,0:T(8,128)S(1)}, f32[64,256]{1,0:T(8,128)S(1)}, u32[]{:S(2)}, u32[]{:S(2)}) collective-permute-start(f32[64,256]{1,0:T(8,128)S(1)} %add.54), channel_id=1, source_target_pairs={{0,3},{1,2},{2,1},{3,0},{4,7},{5,6},{6,5},{7,4},{8,11},{9,10},{10,... | collective-permute-start | bytes 196616 | tf_op jit(solution)/shard_map/ppermute | solution.py:54
  52.8 3.3 %collective-permute-done.10 = f32[64,256]{1,0:T(8,128)S(1)} collective-permute-done((f32[64,256]{1,0:T(8,128)S(1)}, f32[64,256]{1,0:T(8,128)S(1)}, u32[]{:S(2)}, u32[]{:S(2)}) %collective-permute-start.10) | collective-permute-done | bytes 65568 | tf_op jit(solution)/shard_map/ppermute | solution.py:54
  57.9 4.5 %collective-permute-start.12 = (f32[64,256]{1,0:T(8,128)S(1)}, f32[64,256]{1,0:T(8,128)S(1)}, u32[]{:S(2)}, u32[]{:S(2)}) collective-permute-start(f32[64,256]{1,0:T(8,128)S(1)} %get-tuple-element.31), channel_id=1, source_target_pairs={{0,240},{1,17},{2,18},{3,243},{4,244},{5,21},{6,22},{7,247},{8,248... | collective-permute-start | bytes 196616 | tf_op jit(solution)/shard_map/ppermute | solution.py:42
  62.4 2.4 %collective-permute-start.13 = (f32[64,256]{1,0:T(8,128)S(1)}, f32[64,256]{1,0:T(8,128)S(1)}, u32[]{:S(2)}, u32[]{:S(2)}) collective-permute-start(f32[64,256]{1,0:T(8,128)S(1)} %get-tuple-element.32), channel_id=1, source_target_pairs={{0,8},{1,249},{2,250},{3,11},{4,12},{5,253},{6,254},{7,15},{8,16},... | collective-permute-start | bytes 196616 | tf_op jit(solution)/shard_map/ppermute | solution.py:42
  66.8 4.3 %collective-permute-done.14 = f32[64,256]{1,0:T(8,128)S(1)} collective-permute-done((f32[64,256]{1,0:T(8,128)S(1)}, f32[64,256]{1,0:T(8,128)S(1)}, u32[]{:S(2)}, u32[]{:S(2)}) %collective-permute-start.14) | collective-permute-done | bytes 65568 | tf_op jit(solution)/shard_map/ppermute | solution.py:50
  71.1 2.4 %collective-permute-start.15 = (f32[64,256]{1,0:T(8,128)S(1)}, f32[64,256]{1,0:T(8,128)S(1)}, u32[]{:S(2)}, u32[]{:S(2)}) collective-permute-start(f32[64,256]{1,0:T(8,128)S(1)} %add.57), channel_id=1, source_target_pairs={{0,3},{1,2},{2,1},{3,0},{4,7},{5,6},{6,5},{7,4},{8,11},{9,10},{10,... | collective-permute-start | bytes 196616 | tf_op jit(solution)/shard_map/ppermute | solution.py:54
  73.5 3.3 %collective-permute-done.15 = f32[64,256]{1,0:T(8,128)S(1)} collective-permute-done((f32[64,256]{1,0:T(8,128)S(1)}, f32[64,256]{1,0:T(8,128)S(1)}, u32[]{:S(2)}, u32[]{:S(2)}) %collective-permute-start.15) | collective-permute-done | bytes 65568 | tf_op jit(solution)/shard_map/ppermute | solution.py:54
  78.6 5.2 %collective-permute-start.17 = (f32[96,128]{1,0:T(8,128)S(1)}, f32[96,128]{1,0:T(8,128)S(1)}, u32[]{:S(2)}, u32[]{:S(2)}) collective-permute-start(f32[96,128]{1,0:T(8,128)S(1)} %add.58), channel_id=1, source_target_pairs={{0,8},{8,0},{16,24},{24,16},{32,40},{40,32},{48,56},{56,48},{64,72... | collective-permute-start | bytes 147464 | tf_op jit(solution)/shard_map/ppermute | solution.py:275
  83.8 2.1 %collective-permute-done.17 = f32[96,128]{1,0:T(8,128)S(1)} collective-permute-done((f32[96,128]{1,0:T(8,128)S(1)}, f32[96,128]{1,0:T(8,128)S(1)}, u32[]{:S(2)}, u32[]{:S(2)}) %collective-permute-start.17) | collective-permute-done | bytes 49184 | tf_op jit(solution)/shard_map/ppermute | solution.py:275
  85.9 5.4 %collective-permute-done.18 = f32[96,128]{1,0:T(8,128)S(1)} collective-permute-done((f32[96,128]{1,0:T(8,128)S(1)}, f32[96,128]{1,0:T(8,128)S(1)}, u32[]{:S(2)}, u32[]{:S(2)}) %collective-permute-start.18) | collective-permute-done | bytes 49184 | tf_op jit(solution)/shard_map/ppermute | solution.py:275
  91.4 8.3 %collective-permute-done.19 = f32[96,128]{1,0:T(8,128)S(1)} collective-permute-done((f32[96,128]{1,0:T(8,128)S(1)}, f32[96,128]{1,0:T(8,128)S(1)}, u32[]{:S(2)}, u32[]{:S(2)}) %collective-permute-start.19) | collective-permute-done | bytes 49184 | tf_op jit(solution)/shard_map/ppermute | solution.py:275
  99.7 4.1 %collective-permute-done.20 = f32[96,128]{1,0:T(8,128)S(1)} collective-permute-done((f32[96,128]{1,0:T(8,128)S(1)}, f32[96,128]{1,0:T(8,128)S(1)}, u32[]{:S(2)}, u32[]{:S(2)}) %collective-permute-start.20) | collective-permute-done | bytes 49184 | tf_op jit(solution)/shard_map/ppermute | solution.py:275
  103.9 5.6 %collective-permute-done.21 = f32[96,128]{1,0:T(8,128)S(1)} collective-permute-done((f32[96,128]{1,0:T(8,128)S(1)}, f32[96,128]{1,0:T(8,128)S(1)}, u32[]{:S(2)}, u32[]{:S(2)}) %collective-permute-start.21) | collective-permute-done | bytes 49184 | tf_op jit(solution)/shard_map/ppermute | solution.py:275
  109.5 6.5 %shard_map.56 = (f32[512,64]{1,0:T(8,128)S(1)}, f32[64,64]{1,0:T(8,128)}) custom-call(f32[96,128]{1,0:T(8,128)S(1)} %add.63.products_ref, f32[64,512]{1,0:T(8,128)S(1)} %get-tuple-element.35.image_ref), custom_call_target="tpu_custom_call" | custom-call | tf_op jit(solution)/shard_map/pallas_call | solution.py:201
  (49 shorter events, 18.2 us)
Async XLA Ops:
  1.7 0.7 copy-start.1
  2.3 1.2 %copy-start = (f32[512,512]{1,0:T(8,128)S(1)}, f32[512,512]{1,0:T(8,128)}, u32[]{:S(2)}) copy-start(f32[512,512]{1,0:T(8,128)} %embeddings_ref.1) | copy-start | bytes 3145732
  4.2 9.3 %collective-permute-start = (bf16[528,512]{1,0:T(8,128)(2,1)S(1)}, bf16[528,512]{1,0:T(8,128)(2,1)S(1)}, u32[]{:S(2)}, u32[]{:S(2)}) collective-permute-start(bf16[528,512]{1,0:T(8,128)(2,1)S(1)} %get-tuple-element.19.own_ref), channel_id=1, source_target_pairs={{0,4},{4,0},{1,5},{5,1},{2,6},{6,2},{3,7},{7,3},{8,12},{12,8},{9,1... | collective-permute-start | bytes 1622024 | tf_op jit(solution)/shard_map/ppermute | solution.py:46
  4.3 9.2 %collective-permute-start.2 = (bf16[272,512]{1,0:T(8,128)(2,1)S(1)}, bf16[272,512]{1,0:T(8,128)(2,1)S(1)}, u32[]{:S(2)}, u32[]{:S(2)}) collective-permute-start(bf16[272,512]{1,0:T(8,128)(2,1)S(1)} %get-tuple-element.20), channel_id=1, source_target_pairs={{0,248},{1,9},{2,10},{3,251},{4,252},{5,13},{6,14},{7,255},{8,0},{... | collective-permute-start | bytes 835592 | tf_op jit(solution)/shard_map/ppermute | solution.py:42
  6.3 13.9 %collective-permute-start.1 = (bf16[272,512]{1,0:T(8,128)(2,1)S(1)}, bf16[272,512]{1,0:T(8,128)(2,1)S(1)}, u32[]{:S(2)}, u32[]{:S(2)}) collective-permute-start(bf16[272,512]{1,0:T(8,128)(2,1)S(1)} %get-tuple-element.20), channel_id=1, source_target_pairs={{0,16},{1,241},{2,242},{3,19},{4,20},{5,245},{6,246},{7,23},{8,24}... | collective-permute-start | bytes 835592 | tf_op jit(solution)/shard_map/ppermute | solution.py:42
  21.4 1.2 %collective-permute-start.3 = (f32[1,1024]{1,0:T(1,128)S(1)}, f32[1,1024]{1,0:T(1,128)S(1)}, u32[]{:S(2)}, u32[]{:S(2)}) collective-permute-start(f32[1,1024]{1,0:T(1,128)S(1)} %get-tuple-element.22), channel_id=1, source_target_pairs={{0,4},{4,0},{1,5},{5,1},{2,6},{6,2},{3,7},{7,3},{8,12},{12,8},{9,1... | collective-permute-start | bytes 12296 | tf_op jit(solution)/shard_map/ppermute | solution.py:46
  21.5 8.5 %collective-permute-start.6 = (f32[64,512]{1,0:T(8,128)S(1)}, f32[64,512]{1,0:T(8,128)S(1)}, u32[]{:S(2)}, u32[]{:S(2)}) collective-permute-start(f32[64,512]{1,0:T(8,128)S(1)} %get-tuple-element.23.own_start), channel_id=1, source_target_pairs={{0,4},{4,0},{1,5},{5,1},{2,6},{6,2},{3,7},{7,3},{8,12},{12,8},{9,1... | collective-permute-start | bytes 393224 | tf_op jit(solution)/shard_map/ppermute | solution.py:46
  22.6 5.2 %collective-permute-start.4 = (f32[1,1024]{1,0:T(1,128)S(1)}, f32[1,1024]{1,0:T(1,128)S(1)}, u32[]{:S(2)}, u32[]{:S(2)}) collective-permute-start(f32[1,1024]{1,0:T(1,128)S(1)} %maximum_add_fusion), channel_id=1, source_target_pairs={{0,1},{1,0},{2,3},{3,2},{4,5},{5,4},{6,7},{7,6},{8,9},{9,8},{10,11... | collective-permute-start | bytes 12296 | tf_op jit(solution)/shard_map/ppermute | solution.py:50
  27.8 4.8 %collective-permute-start.5 = (f32[1,1024]{1,0:T(1,128)S(1)}, f32[1,1024]{1,0:T(1,128)S(1)}, u32[]{:S(2)}, u32[]{:S(2)}) collective-permute-start(f32[1,1024]{1,0:T(1,128)S(1)} %add.51.degree_ref), channel_id=1, source_target_pairs={{0,3},{1,2},{2,1},{3,0},{4,7},{5,6},{6,5},{7,4},{8,11},{9,10},{10,... | collective-permute-start | bytes 12296 | tf_op jit(solution)/shard_map/ppermute | solution.py:54
  33.0 10.2 %collective-permute-start.7 = (f32[64,256]{1,0:T(8,128)S(1)}, f32[64,256]{1,0:T(8,128)S(1)}, u32[]{:S(2)}, u32[]{:S(2)}) collective-permute-start(f32[64,256]{1,0:T(8,128)S(1)} %get-tuple-element.28), channel_id=1, source_target_pairs={{0,240},{1,17},{2,18},{3,243},{4,244},{5,21},{6,22},{7,247},{8,248... | collective-permute-start | bytes 196616 | tf_op jit(solution)/shard_map/ppermute | solution.py:42
  40.1 6.0 %collective-permute-start.8 = (f32[64,256]{1,0:T(8,128)S(1)}, f32[64,256]{1,0:T(8,128)S(1)}, u32[]{:S(2)}, u32[]{:S(2)}) collective-permute-start(f32[64,256]{1,0:T(8,128)S(1)} %get-tuple-element.29), channel_id=1, source_target_pairs={{0,8},{1,249},{2,250},{3,11},{4,12},{5,253},{6,254},{7,15},{8,16},... | collective-permute-start | bytes 196616 | tf_op jit(solution)/shard_map/ppermute | solution.py:42
  46.1 4.4 %collective-permute-start.9 = (f32[64,256]{1,0:T(8,128)S(1)}, f32[64,256]{1,0:T(8,128)S(1)}, u32[]{:S(2)}, u32[]{:S(2)}) collective-permute-start(f32[64,256]{1,0:T(8,128)S(1)} %select_add_fusion.1), channel_id=1, source_target_pairs={{0,1},{1,0},{2,3},{3,2},{4,5},{5,4},{6,7},{7,6},{8,9},{9,8},{10,11... | collective-permute-start | bytes 196616 | tf_op jit(solution)/shard_map/ppermute | solution.py:50
  50.5 5.6 %collective-permute-start.10 = (f32[64,256]{1,0:T(8,128)S(1)}, f32[64,256]{1,0:T(8,128)S(1)}, u32[]{:S(2)}, u32[]{:S(2)}) collective-permute-start(f32[64,256]{1,0:T(8,128)S(1)} %add.54), channel_id=1, source_target_pairs={{0,3},{1,2},{2,1},{3,0},{4,7},{5,6},{6,5},{7,4},{8,11},{9,10},{10,... | collective-permute-start | bytes 196616 | tf_op jit(solution)/shard_map/ppermute | solution.py:54
  56.1 1.4 %collective-permute-start.11 = (f32[64,512]{1,0:T(8,128)S(1)}, f32[64,512]{1,0:T(8,128)S(1)}, u32[]{:S(2)}, u32[]{:S(2)}) collective-permute-start(f32[64,512]{1,0:T(8,128)S(1)} %maximum_select_fusion.own_ref.first_ref), channel_id=1, source_target_pairs={{0,4},{4,0},{1,5},{5,1},{2,6},{6,2},{3,7},{7,3},{8,12},{12,8},{9,1... | collective-permute-start | bytes 393224 | tf_op jit(solution)/shard_map/ppermute | solution.py:46
  57.9 6.9 %collective-permute-start.12 = (f32[64,256]{1,0:T(8,128)S(1)}, f32[64,256]{1,0:T(8,128)S(1)}, u32[]{:S(2)}, u32[]{:S(2)}) collective-permute-start(f32[64,256]{1,0:T(8,128)S(1)} %get-tuple-element.31), channel_id=1, source_target_pairs={{0,240},{1,17},{2,18},{3,243},{4,244},{5,21},{6,22},{7,247},{8,248... | collective-permute-start | bytes 196616 | tf_op jit(solution)/shard_map/ppermute | solution.py:42
  62.4 4.3 %collective-permute-start.13 = (f32[64,256]{1,0:T(8,128)S(1)}, f32[64,256]{1,0:T(8,128)S(1)}, u32[]{:S(2)}, u32[]{:S(2)}) collective-permute-start(f32[64,256]{1,0:T(8,128)S(1)} %get-tuple-element.32), channel_id=1, source_target_pairs={{0,8},{1,249},{2,250},{3,11},{4,12},{5,253},{6,254},{7,15},{8,16},... | collective-permute-start | bytes 196616 | tf_op jit(solution)/shard_map/ppermute | solution.py:42
  66.7 4.4 %collective-permute-start.14 = (f32[64,256]{1,0:T(8,128)S(1)}, f32[64,256]{1,0:T(8,128)S(1)}, u32[]{:S(2)}, u32[]{:S(2)}) collective-permute-start(f32[64,256]{1,0:T(8,128)S(1)} %select_add_fusion), channel_id=1, source_target_pairs={{0,1},{1,0},{2,3},{3,2},{4,5},{5,4},{6,7},{7,6},{8,9},{9,8},{10,11... | collective-permute-start | bytes 196616 | tf_op jit(solution)/shard_map/ppermute | solution.py:50
  71.1 5.7 %collective-permute-start.15 = (f32[64,256]{1,0:T(8,128)S(1)}, f32[64,256]{1,0:T(8,128)S(1)}, u32[]{:S(2)}, u32[]{:S(2)}) collective-permute-start(f32[64,256]{1,0:T(8,128)S(1)} %add.57), channel_id=1, source_target_pairs={{0,3},{1,2},{2,1},{3,0},{4,7},{5,6},{6,5},{7,4},{8,11},{9,10},{10,... | collective-permute-start | bytes 196616 | tf_op jit(solution)/shard_map/ppermute | solution.py:54
  77.3 1.3 %collective-permute-start.16 = (f32[96,128]{1,0:T(8,128)S(1)}, f32[96,128]{1,0:T(8,128)S(1)}, u32[]{:S(2)}, u32[]{:S(2)}) collective-permute-start(f32[96,128]{1,0:T(8,128)S(1)} %get-tuple-element.34), channel_id=1, source_target_pairs={{0,4},{4,0},{1,5},{5,1},{2,6},{6,2},{3,7},{7,3},{8,12},{12,8},{9,1... | collective-permute-start | bytes 147464 | tf_op jit(solution)/shard_map/ppermute | solution.py:46
  78.6 7.3 %collective-permute-start.17 = (f32[96,128]{1,0:T(8,128)S(1)}, f32[96,128]{1,0:T(8,128)S(1)}, u32[]{:S(2)}, u32[]{:S(2)}) collective-permute-start(f32[96,128]{1,0:T(8,128)S(1)} %add.58), channel_id=1, source_target_pairs={{0,8},{8,0},{16,24},{24,16},{32,40},{40,32},{48,56},{56,48},{64,72... | collective-permute-start | bytes 147464 | tf_op jit(solution)/shard_map/ppermute | solution.py:275
  85.8 5.4 %collective-permute-start.18 = (f32[96,128]{1,0:T(8,128)S(1)}, f32[96,128]{1,0:T(8,128)S(1)}, u32[]{:S(2)}, u32[]{:S(2)}) collective-permute-start(f32[96,128]{1,0:T(8,128)S(1)} %add.59), channel_id=1, source_target_pairs={{0,16},{8,24},{16,0},{24,8},{32,48},{40,56},{48,32},{56,40},{64,80... | collective-permute-start | bytes 147464 | tf_op jit(solution)/shard_map/ppermute | solution.py:275
  91.3 8.4 %collective-permute-start.19 = (f32[96,128]{1,0:T(8,128)S(1)}, f32[96,128]{1,0:T(8,128)S(1)}, u32[]{:S(2)}, u32[]{:S(2)}) collective-permute-start(f32[96,128]{1,0:T(8,128)S(1)} %add.60), channel_id=1, source_target_pairs={{0,32},{8,40},{16,48},{24,56},{32,0},{40,8},{48,16},{56,24},{64,96... | collective-permute-start | bytes 147464 | tf_op jit(solution)/shard_map/ppermute | solution.py:275
  99.6 4.2 %collective-permute-start.20 = (f32[96,128]{1,0:T(8,128)S(1)}, f32[96,128]{1,0:T(8,128)S(1)}, u32[]{:S(2)}, u32[]{:S(2)}) collective-permute-start(f32[96,128]{1,0:T(8,128)S(1)} %add.61), channel_id=1, source_target_pairs={{0,64},{8,72},{16,80},{24,88},{32,96},{40,104},{48,112},{56,120},{... | collective-permute-start | bytes 147464 | tf_op jit(solution)/shard_map/ppermute | solution.py:275
  103.8 5.7 %collective-permute-start.21 = (f32[96,128]{1,0:T(8,128)S(1)}, f32[96,128]{1,0:T(8,128)S(1)}, u32[]{:S(2)}, u32[]{:S(2)}) collective-permute-start(f32[96,128]{1,0:T(8,128)S(1)} %add.62), channel_id=1, source_target_pairs={{0,128},{8,136},{16,144},{24,152},{32,160},{40,168},{48,176},{56,1... | collective-permute-start | bytes 147464 | tf_op jit(solution)/shard_map/ppermute | solution.py:275

commit v3 on v2

v3 whole, which is shorter than its diff:
```python
import functools
import math

import jax
import jax.numpy as jnp
from jax import lax
from jax.experimental import pallas as pl
from jax.experimental.pallas import tpu as pltpu
from jax.sharding import Mesh
from jax.sharding import PartitionSpec as P

WIDTH = 512
BASIS = 64
BLOCK = 512
HALF = BLOCK // 2
QUARTER = BLOCK // 4
DOCS = 32768
REACH = 5
CHUNK = 256
STEP = 8
EXPONENT = -math.log(BLOCK / 4) / (2 * WIDTH) * math.log2(math.e)
UNLISTED = -1e30
CHIPS = 32
CORES = 2
PAIRS = 4
PARITIES = (0, 1, 1, 0)
HALVES = (0, 0, 1, 1)
NEAR = (1, -1)
FAR = (-2, 2)
ALL_AXES = ("chip", "core", "pairs")
NT = (((1,), (1,)), ((), ()))
EXACT = lax.Precision.HIGHEST


def move(array, reaches, sign):
    moves = []
    for chip in range(CHIPS):
        for core in range(CORES):
            for pair in range(PAIRS):
                to_chip = (chip + sign * reaches[PARITIES[pair]]) % CHIPS
                source = (chip * CORES + core) * PAIRS + pair
                target = (to_chip * CORES + core) * PAIRS + pair
                moves.append((source, target))
    return lax.ppermute(array, ALL_AXES, moves)


def swap_core(array):
    return lax.ppermute(array, "core", [(0, 1), (1, 0)])


def other_chip(array, bits):
    return lax.ppermute(array, "chip", [(i, i ^ bits) for i in range(CHIPS)])


def other_planes(array):
    return [
        lax.ppermute(array, "pairs", [(i, step(i)) for i in range(PAIRS)])
        for step in (lambda i: i ^ 1, lambda i: PAIRS - 1 - i, lambda i: i ^ 2)
    ]


def place():
    pair = lax.axis_index("pairs")
    parity = jnp.where((pair == 1) | (pair == 2), 1, 0)
    return lax.axis_index("core"), parity, jnp.where(pair >= 2, 1, 0)


def pack_kernel(embeddings_ref, sent_ref, gate_ref, full_out):
    full_out[:BLOCK, :] = embeddings_ref[...].astype(jnp.bfloat16)
    full_out[BLOCK:, :] = sent_ref[HALF:, :]


def column_bias(reach, own_mask, mate_mask, other_mask, core):
    lane = lax.broadcasted_iota(jnp.int32, (1, 128), 1)
    found = []
    for mask, row_core in ((own_mask, core), (mate_mask, 1 - core)):
        offset = 2 * reach + core - row_core
        ahead = jnp.where((lane == offset) & (lane < REACH), mask, 0.0)
        behind = jnp.where((lane == -offset) & (lane > 0) & (lane < REACH), other_mask, 0.0)
        flag = jnp.sum(ahead + behind, axis=1, keepdims=True)
        found.append(jnp.where(flag > 0, 0.0, UNLISTED))
    return found


def mask_row(ref):
    return ref[ref.shape[0] - 16 :, :128].astype(jnp.float32)[:1]


def norms(array):
    return EXPONENT * jnp.sum(jnp.square(array.astype(jnp.float32)), axis=1, keepdims=True)


def write_tiles(row_refs, biases, cols, out_ref):
    count = cols.shape[0]
    cols_sq = jnp.broadcast_to(norms(cols), (count, 128)).T[:1]
    for part, (row_ref, bias) in enumerate(zip(row_refs, biases)):
        shift = cols_sq + bias
        for first in range(0, BLOCK, CHUNK):
            rows = row_ref[first : first + CHUNK, :]
            inner = lax.dot_general(rows, cols, NT, preferred_element_type=jnp.float32)
            tile = jnp.exp2(inner * (-2.0 * EXPONENT) + norms(rows) + shift)
            start = part * BLOCK + first
            out_ref[start : start + CHUNK, :] = tile.astype(jnp.bfloat16)
    ones = jnp.ones((8, count), jnp.bfloat16)
    return lax.dot_general(ones, out_ref[...], NT, preferred_element_type=jnp.float32)[:1]


def own_kernel(own_ref, mate_ref, own_out, sum_out):
    core, parity, half = place()
    masks = mask_row(own_ref), mask_row(mate_ref)
    bias = column_bias(0, *masks, masks[0], core)
    start = pl.multiple_of((2 * half + parity) * QUARTER, QUARTER)
    cols = own_ref[pl.ds(start, QUARTER), :]
    sum_out[...] = write_tiles((own_ref, mate_ref), bias, cols, own_out)


def reach_kernel(reaches, own_ref, mate_ref, reach_ref, sum_ref, tiles_out, sum_out):
    core, parity, _ = place()
    reach = jnp.where(parity == 0, reaches[0], reaches[1])
    masks = mask_row(own_ref), mask_row(mate_ref)
    bias = column_bias(reach, *masks, mask_row(reach_ref), core)
    rows = (own_ref, mate_ref)
    sum_out[...] = sum_ref[...] + write_tiles(rows, bias, reach_ref[:HALF, :], tiles_out)


def multiply(vectors, far_ref, near_ref, own_ref, far_out, near_out, own_out):
    for weights_ref, out_ref in ((far_ref, far_out), (near_ref, near_out), (own_ref, own_out)):
        found = jnp.dot(vectors, weights_ref[...], preferred_element_type=jnp.float32)
        if found.shape[0] > BASIS:
            found = found[:BASIS] + found[BASIS:]
        out_ref[...] = found


def first_kernel(
    sum_ref, same_ref, across_ref, both_ref, own_start, mate_start, far, near, own,
    far_out, near_out, own_out, root_out,
):
    degree = (sum_ref[...] + same_ref[...]) + (across_ref[...] + both_ref[...])
    root = lax.rsqrt(degree)
    root_out[...] = root
    scaled = jnp.concatenate(
        [own_start[...] * root[:, :BLOCK], mate_start[...] * root[:, BLOCK:]], axis=1
    )
    multiply(scaled.astype(jnp.bfloat16), far, near, own, far_out, near_out, own_out)


def second_kernel(root_ref, own_ref, mate_ref, far, near, own, far_out, near_out, own_out):
    root = root_ref[...]
    scaled = jnp.concatenate([own_ref[...], mate_ref[...]], axis=1) * root * root
    high = scaled.astype(jnp.bfloat16)
    low = (scaled - high.astype(jnp.float32)).astype(jnp.bfloat16)
    multiply(jnp.concatenate([high, low]), far, near, own, far_out, near_out, own_out)


def products_kernel(root_ref, first_ref, second_ref, image_out, products_out):
    root = root_ref[:, :BLOCK]
    image = second_ref[...] * root
    image_out[...] = image
    both = jnp.concatenate([first_ref[...] * root, image])
    found = lax.dot_general(both, both, NT, precision=EXACT, preferred_element_type=jnp.float32)
    row = lax.broadcasted_iota(jnp.int32, (BASIS, BASIS), 0)
    lane = lax.broadcasted_iota(jnp.int32, (BASIS, BASIS), 1)
    gram = found[BASIS:, BASIS:]
    square = jnp.where(row >= lane, found[:BASIS, :BASIS], gram)
    diagonal = jnp.sum(jnp.where(row == lane, gram, 0.0), axis=0, keepdims=True)
    products_out[:BASIS, :] = jnp.concatenate([square, found[:BASIS, BASIS:]], axis=1)
    products_out[BASIS:, :] = jnp.broadcast_to(
        jnp.concatenate([diagonal, diagonal], axis=1), (8, 2 * BASIS)
    )


def finish_kernel(products_ref, image_ref, basis_ref, projected_ref):
    square = products_ref[:BASIS, :BASIS]
    turned = square.T
    row = lax.broadcasted_iota(jnp.int32, (BASIS, BASIS), 0)
    lane = lax.broadcasted_iota(jnp.int32, (BASIS, BASIS), 1)
    first = jnp.where(row >= lane, square, turned)
    second = jnp.where(row > lane, turned, square)
    second = jnp.where(row == lane, products_ref[BASIS : BASIS + 1, :BASIS], second)
    work = jnp.concatenate([first, second], axis=1) * (1.0 / DOCS)
    row = lax.broadcasted_iota(jnp.int32, (BASIS, 128), 0)
    lane = lax.broadcasted_iota(jnp.int32, (BASIS, 128), 1)
    left = lane < BASIS
    for start in range(0, BASIS, STEP):
        columns = [
            jnp.take_along_axis(work, jnp.where(left, j, BASIS + j), axis=1)
            for j in range(start, start + STEP)
        ]
        rows = [work[j : j + 1, :] for j in range(start, start + STEP)]
        for k in range(STEP):
            j = start + k
            factor = jnp.where(row > j, columns[k] * (1.0 / columns[k][j : j + 1, :]), 0.0)
            pivot_row = rows[k] + jnp.where(lane[:1] % BASIS == j, 1.0, 0.0)
            for later in range(k + 1, STEP):
                columns[later] = columns[later] - factor * columns[later][j : j + 1, :]
                rows[later] = rows[later] - factor[start + later : start + later + 1, :] * pivot_row
            work = work - factor * pivot_row
    diagonal = lane % BASIS == row
    pivots = jnp.where(diagonal, work, 0.0)
    scale = jnp.where(
        left,
        jnp.sum(pivots[:, :BASIS], axis=1, keepdims=True),
        jnp.sum(pivots[:, BASIS:], axis=1, keepdims=True),
    )
    inverse = jnp.where(diagonal, 1.0, jnp.where(lane % BASIS < row, work, 0.0)) * lax.rsqrt(scale)
    cross = products_ref[:BASIS, BASIS:]
    first = inverse[:, :BASIS]
    half = jnp.dot(
        first, cross * (1.0 / DOCS), precision=EXACT, preferred_element_type=jnp.float32
    )
    projected_ref[...] = lax.dot_general(
        half, first, NT, precision=EXACT, preferred_element_type=jnp.float32
    )
    basis_ref[...] = jnp.dot(
        inverse[:, BASIS:], image_ref[...], precision=EXACT, preferred_element_type=jnp.float32
    )


def call(kernel, outs, operands, scratch=(), far_operands=0):
    spaces = [pl.ANY] * far_operands + [pltpu.VMEM] * (len(operands) - far_operands)
    limit = None if far_operands else 32 * 2**20
    return pl.pallas_call(
        kernel,
        out_shape=[jax.ShapeDtypeStruct(shape, dtype) for shape, dtype in outs],
        in_specs=[pl.BlockSpec(memory_space=space) for space in spaces],
        out_specs=[pl.BlockSpec(memory_space=pltpu.VMEM)] * len(outs),
        scratch_shapes=scratch,
        compiler_params=pltpu.CompilerParams(vmem_limit_bytes=limit),
    )(*operands)


def on_device(embeddings, start_basis, pair_mask):
    f32, bf16 = jnp.float32, jnp.bfloat16
    wide = 2 * BLOCK
    _, parity, half = place()

    own_start = start_basis.T
    mate_start = swap_core(own_start)
    rows = lax.dynamic_slice_in_dim(embeddings, half * HALF, HALF, 0).astype(bf16)
    mask = jnp.pad(pair_mask.astype(bf16), ((HALF, 15), (0, WIDTH - REACH)))
    sent = jnp.pad(rows, ((0, 16), (0, 0))) + mask
    far = move(sent, FAR, -1)
    (packed,) = call(
        pack_kernel, [((BLOCK + 16, WIDTH), bf16)], (embeddings, sent, mate_start)
    )
    mate = swap_core(packed)
    near = move(sent, NEAR, -1)
    tiles = [((wide, HALF), bf16), ((1, wide), f32)]
    own_weights, sums = call(
        own_kernel, [((wide, QUARTER), bf16), ((1, wide), f32)], (packed, mate)
    )
    far_kernel = functools.partial(reach_kernel, FAR)
    near_kernel = functools.partial(reach_kernel, NEAR)
    far_weights, sums = call(far_kernel, tiles, (packed, mate, far, sums))
    near_weights, sums = call(near_kernel, tiles, (packed, mate, near, sums))
    other = swap_core(sums)
    sums = sums + jnp.concatenate([other[:, BLOCK:], other[:, :BLOCK]], axis=1)
    plane_sums = [sums, *other_planes(sums)]
    weights = (far_weights, near_weights, own_weights)
    terms = [((BASIS, HALF), f32), ((BASIS, HALF), f32), ((BASIS, QUARTER), f32)]

    def collect(far_term, near_term, own_term):
        total = move(far_term, FAR, 1) + move(near_term, NEAR, 1)
        blank = jnp.zeros_like(own_term)
        total = total + jnp.where(
            parity == 0,
            jnp.concatenate([own_term, blank], axis=1),
            jnp.concatenate([blank, own_term], axis=1),
        )
        same, across, both = other_planes(total)
        total = total + same
        other = across + both
        return jnp.where(
            half == 0,
            jnp.concatenate([total, other], axis=1),
            jnp.concatenate([other, total], axis=1),
        )

    far_term, near_term, own_term, root = call(
        first_kernel,
        terms + [((1, wide), f32)],
        (*plane_sums, own_start, mate_start, *weights),
    )
    first = collect(far_term, near_term, own_term)
    second = collect(*call(second_kernel, terms, (root, first, swap_core(first), *weights)))
    image, products = call(
        products_kernel, [((BASIS, BLOCK), f32), ((BASIS + 8, 128), f32)], (root, first, second)
    )
    products = products + swap_core(products)
    for bits in (1, 2, 7, 8, 24):
        products = products + other_chip(products, bits)
    basis, projected = call(
        finish_kernel, [((BASIS, BLOCK), f32), ((BASIS, BASIS), f32)], (products, image)
    )
    return basis.T, projected


def solution(mesh):
    grid = Mesh(mesh.devices.reshape(CHIPS, CORES, PAIRS), ALL_AXES)
    rows = P(("chip", "core"), None)
    return jax.shard_map(
        on_device, mesh=grid, in_specs=(rows, rows, rows), out_specs=(rows, P()), check_vma=False
    )
```

time: 118 us -> 105 us (0.89); the launches traced: 117 us -> 105 us
  Pallas kernels: 11.3 us -> 6.59 us
  starting transfers between devices: 37.5 us -> 34.8 us
  local copies, waits for them, and re-layouts: 3.6 us -> 1.16 us
  waiting for transfers between devices: 63.3 us -> 61 us
    ppermute x11 -> x14, waiting for transfers between devices: 44.6 us -> 33.4 us  [the longest x5 22.9 us: other_chip(): return lax.ppermute(array, 'chip', [(i, i ^ bits) for i in range(CHIPS)])]
    ppermute x6, waiting for transfers between devices: 15.4 us -> 23.8 us  [move(): return lax.ppermute(array, ALL_AXES, moves)]
    ppermute x6, starting transfers between devices: 20.5 us -> 15.4 us  [move(): return lax.ppermute(array, ALL_AXES, moves)]
    pallas_call x7 -> x8, Pallas kernels: 11.3 us -> 6.59 us  [call(): pl.pallas_call(kernel, out_shape=[jax.ShapeDtypeStruct(shape, dtype) for...]
    unnamed x5 -> x4, local copies, waits for them, and re-layouts: 2.82 us -> 0.01 us
    ppermute x11 -> x14, starting transfers between devices: 16.2 us -> 18.6 us  [the longest x9 13.5 us: other_planes(): lax.ppermute(array, 'pairs', [(i, step(i)) for i in range(PAIRS)])]
  transfers between devices with their start and end apart: 22 -> 25, of which waited for: 18 -> 18; matrix products, arithmetic and copies ran while one was open for 0% -> 2% of each run, Pallas kernels for 2% -> 1%
where the time goes in v3:
time: 105 us
  waiting for transfers between devices  61 us (58%)
  starting transfers between devices  34.8 us (33%)
  Pallas kernels  6.59 us (6%)
  local copies, waits for them, and re-layouts  1.16 us (1%)
    ppermute x6, waiting for transfers between devices, move(): return lax.ppermute(array, ALL_AXES, moves)  23.8 us
    ppermute x5, waiting for transfers between devices, other_chip(): return lax.ppermute(array, 'chip', [(i, i ^ bits) for i in range(CHIPS)])  22.9 us
    ppermute x6, starting transfers between devices, move(): return lax.ppermute(array, ALL_AXES, moves)  15.4 us
    ppermute x9, starting transfers between devices, other_planes(): lax.ppermute(array, 'pairs', [(i, step(i)) for i in range(PAIRS)])  13.5 us
    ppermute x9, waiting for transfers between devices, other_planes(): lax.ppermute(array, 'pairs', [(i, step(i)) for i in range(PAIRS)])  10.5 us
    pallas_call x8, Pallas kernels, call(): pl.pallas_call(kernel, out_shape=[jax.ShapeDtypeStruct(shape, dtype) for...  6.59 us
    ppermute x5, starting transfers between devices, other_chip(): return lax.ppermute(array, 'chip', [(i, i ^ bits) for i in range(CHIPS)])  5.12 us
    ppermute x5, waiting for transfers between devices, swap_core(): return lax.ppermute(array, 'core', [(0, 1), (1, 0)])  3.69 us
  transfers between devices with their start and end apart: 25, of which 18 were waited for; matrix products, arithmetic and copies ran while one was open for 2% of the time, Pallas kernels for 1%

profile of v3, /device:TPU:32, one launch (start us, length us, event | category | flops | bytes accessed | tf_op | source)
XLA Modules:
  0.0 105.1 jit_solution(5880990875028510143)
XLA Ops:
  3.2 3.3 %collective-permute-start.3 = (bf16[272,512]{1,0:T(8,128)(2,1)S(1)}, bf16[272,512]{1,0:T(8,128)(2,1)S(1)}, u32[]{:S(2)}, u32[]{:S(2)}) collective-permute-start(bf16[272,512]{1,0:T(8,128)(2,1)S(1)} %pad_add_fusion.sent_ref), channel_id=1, source_target_pairs={{0,16},{1,241},{2,242},{3,19},{4,20},{5,245},{6,246},{7,23},{8,24}... | collective-permute-start | bytes 835592 | tf_op jit(solution)/shard_map/ppermute | solution.py:44
  7.2 16.5 %collective-permute-done.3.reach_ref = bf16[272,512]{1,0:T(8,128)(2,1)S(1)} collective-permute-done((bf16[272,512]{1,0:T(8,128)(2,1)S(1)}, bf16[272,512]{1,0:T(8,128)(2,1)S(1)}, u32[]{:S(2)}, u32[]{:S(2)}) %collective-permute-start.3) | collective-permute-done | bytes 278560 | tf_op jit(solution)/shard_map/ppermute | solution.py:44
  26.5 2.9 %collective-permute-start.6 = (f32[1,1024]{1,0:T(1,128)S(1)}, f32[1,1024]{1,0:T(1,128)S(1)}, u32[]{:S(2)}, u32[]{:S(2)}) collective-permute-start(f32[1,1024]{1,0:T(1,128)S(1)} %maximum_add_fusion.sum_ref), channel_id=1, source_target_pairs={{0,3},{1,2},{2,1},{3,0},{4,7},{5,6},{6,5},{7,4},{8,11},{9,10},{10,... | collective-permute-start | bytes 12296 | tf_op jit(solution)/shard_map/ppermute | solution.py:57
  31.5 1.6 %collective-permute-done.5.same_ref = f32[1,1024]{1,0:T(1,128)S(1)} collective-permute-done((f32[1,1024]{1,0:T(1,128)S(1)}, f32[1,1024]{1,0:T(1,128)S(1)}, u32[]{:S(2)}, u32[]{:S(2)}) %collective-permute-start.5) | collective-permute-done | bytes 4128 | tf_op jit(solution)/shard_map/ppermute | solution.py:57
  33.4 5.1 %collective-permute-start.8 = (f32[64,256]{1,0:T(8,128)S(1)}, f32[64,256]{1,0:T(8,128)S(1)}, u32[]{:S(2)}, u32[]{:S(2)}) collective-permute-start(f32[64,256]{1,0:T(8,128)S(1)} %get-tuple-element.26), channel_id=1, source_target_pairs={{0,240},{1,17},{2,18},{3,243},{4,244},{5,21},{6,22},{7,247},{8,248... | collective-permute-start | bytes 196616 | tf_op jit(solution)/shard_map/ppermute | solution.py:44
  38.6 1.9 %collective-permute-done.8 = f32[64,256]{1,0:T(8,128)S(1)} collective-permute-done((f32[64,256]{1,0:T(8,128)S(1)}, f32[64,256]{1,0:T(8,128)S(1)}, u32[]{:S(2)}, u32[]{:S(2)}) %collective-permute-start.8) | collective-permute-done | bytes 65568 | tf_op jit(solution)/shard_map/ppermute | solution.py:44
  40.5 3.6 %collective-permute-done.9 = f32[64,256]{1,0:T(8,128)S(1)} collective-permute-done((f32[64,256]{1,0:T(8,128)S(1)}, f32[64,256]{1,0:T(8,128)S(1)}, u32[]{:S(2)}, u32[]{:S(2)}) %collective-permute-start.9) | collective-permute-done | bytes 65568 | tf_op jit(solution)/shard_map/ppermute | solution.py:44
  44.1 3.5 %collective-permute-start.12 = (f32[64,256]{1,0:T(8,128)S(1)}, f32[64,256]{1,0:T(8,128)S(1)}, u32[]{:S(2)}, u32[]{:S(2)}) collective-permute-start(f32[64,256]{1,0:T(8,128)S(1)} %select_add_fusion.1), channel_id=1, source_target_pairs={{0,2},{1,3},{2,0},{3,1},{4,6},{5,7},{6,4},{7,5},{8,10},{9,11},{10,... | collective-permute-start | bytes 196616 | tf_op jit(solution)/shard_map/ppermute | solution.py:57
  48.8 1.7 %collective-permute-done.12 = f32[64,256]{1,0:T(8,128)S(1)} collective-permute-done((f32[64,256]{1,0:T(8,128)S(1)}, f32[64,256]{1,0:T(8,128)S(1)}, u32[]{:S(2)}, u32[]{:S(2)}) %collective-permute-start.12) | collective-permute-done | bytes 65568 | tf_op jit(solution)/shard_map/ppermute | solution.py:57
  50.6 2.5 %collective-permute-done.11 = f32[64,256]{1,0:T(8,128)S(1)} collective-permute-done((f32[64,256]{1,0:T(8,128)S(1)}, f32[64,256]{1,0:T(8,128)S(1)}, u32[]{:S(2)}, u32[]{:S(2)}) %collective-permute-start.11) | collective-permute-done | bytes 65568 | tf_op jit(solution)/shard_map/ppermute | solution.py:57
  53.2 1.3 %collective-permute-done.13.mate_ref = f32[64,512]{1,0:T(8,128)S(1)} collective-permute-done((f32[64,512]{1,0:T(8,128)S(1)}, f32[64,512]{1,0:T(8,128)S(1)}, u32[]{:S(2)}, u32[]{:S(2)}) %collective-permute-start.13) | collective-permute-done | bytes 131104 | tf_op jit(solution)/shard_map/ppermute | solution.py:48
  55.0 4.5 %collective-permute-start.14 = (f32[64,256]{1,0:T(8,128)S(1)}, f32[64,256]{1,0:T(8,128)S(1)}, u32[]{:S(2)}, u32[]{:S(2)}) collective-permute-start(f32[64,256]{1,0:T(8,128)S(1)} %get-tuple-element.29), channel_id=1, source_target_pairs={{0,240},{1,17},{2,18},{3,243},{4,244},{5,21},{6,22},{7,247},{8,248... | collective-permute-start | bytes 196616 | tf_op jit(solution)/shard_map/ppermute | solution.py:44
  59.5 2.4 %collective-permute-start.15 = (f32[64,256]{1,0:T(8,128)S(1)}, f32[64,256]{1,0:T(8,128)S(1)}, u32[]{:S(2)}, u32[]{:S(2)}) collective-permute-start(f32[64,256]{1,0:T(8,128)S(1)} %get-tuple-element.30), channel_id=1, source_target_pairs={{0,8},{1,249},{2,250},{3,11},{4,12},{5,253},{6,254},{7,15},{8,16},... | collective-permute-start | bytes 196616 | tf_op jit(solution)/shard_map/ppermute | solution.py:44
  61.8 1.9 %collective-permute-done.15 = f32[64,256]{1,0:T(8,128)S(1)} collective-permute-done((f32[64,256]{1,0:T(8,128)S(1)}, f32[64,256]{1,0:T(8,128)S(1)}, u32[]{:S(2)}, u32[]{:S(2)}) %collective-permute-start.15) | collective-permute-done | bytes 65568 | tf_op jit(solution)/shard_map/ppermute | solution.py:44
  63.9 2.7 %collective-permute-start.18 = (f32[64,256]{1,0:T(8,128)S(1)}, f32[64,256]{1,0:T(8,128)S(1)}, u32[]{:S(2)}, u32[]{:S(2)}) collective-permute-start(f32[64,256]{1,0:T(8,128)S(1)} %select_add_fusion), channel_id=1, source_target_pairs={{0,2},{1,3},{2,0},{3,1},{4,6},{5,7},{6,4},{7,5},{8,10},{9,11},{10,... | collective-permute-start | bytes 196616 | tf_op jit(solution)/shard_map/ppermute | solution.py:57
  66.5 2.0 %collective-permute-start.17 = (f32[64,256]{1,0:T(8,128)S(1)}, f32[64,256]{1,0:T(8,128)S(1)}, u32[]{:S(2)}, u32[]{:S(2)}) collective-permute-start(f32[64,256]{1,0:T(8,128)S(1)} %select_add_fusion), channel_id=1, source_target_pairs={{0,3},{1,2},{2,1},{3,0},{4,7},{5,6},{6,5},{7,4},{8,11},{9,10},{10,... | collective-permute-start | bytes 196616 | tf_op jit(solution)/shard_map/ppermute | solution.py:57
  69.8 2.2 %collective-permute-done.17 = f32[64,256]{1,0:T(8,128)S(1)} collective-permute-done((f32[64,256]{1,0:T(8,128)S(1)}, f32[64,256]{1,0:T(8,128)S(1)}, u32[]{:S(2)}, u32[]{:S(2)}) %collective-permute-start.17) | collective-permute-done | bytes 65568 | tf_op jit(solution)/shard_map/ppermute | solution.py:57
  73.8 5.1 %collective-permute-start.20 = (f32[72,128]{1,0:T(8,128)S(1)}, f32[72,128]{1,0:T(8,128)S(1)}, u32[]{:S(2)}, u32[]{:S(2)}) collective-permute-start(f32[72,128]{1,0:T(8,128)S(1)} %add.74), channel_id=1, source_target_pairs={{0,8},{8,0},{16,24},{24,16},{32,40},{40,32},{48,56},{56,48},{64,72... | collective-permute-start | bytes 110600 | tf_op jit(solution)/shard_map/ppermute | solution.py:52
  78.9 1.9 %collective-permute-done.20 = f32[72,128]{1,0:T(8,128)S(1)} collective-permute-done((f32[72,128]{1,0:T(8,128)S(1)}, f32[72,128]{1,0:T(8,128)S(1)}, u32[]{:S(2)}, u32[]{:S(2)}) %collective-permute-start.20) | collective-permute-done | bytes 36896 | tf_op jit(solution)/shard_map/ppermute | solution.py:52
  80.9 4.8 %collective-permute-done.21 = f32[72,128]{1,0:T(8,128)S(1)} collective-permute-done((f32[72,128]{1,0:T(8,128)S(1)}, f32[72,128]{1,0:T(8,128)S(1)}, u32[]{:S(2)}, u32[]{:S(2)}) %collective-permute-start.21) | collective-permute-done | bytes 36896 | tf_op jit(solution)/shard_map/ppermute | solution.py:52
  85.7 7.0 %collective-permute-done.22 = f32[72,128]{1,0:T(8,128)S(1)} collective-permute-done((f32[72,128]{1,0:T(8,128)S(1)}, f32[72,128]{1,0:T(8,128)S(1)}, u32[]{:S(2)}, u32[]{:S(2)}) %collective-permute-start.22) | collective-permute-done | bytes 36896 | tf_op jit(solution)/shard_map/ppermute | solution.py:52
  92.8 3.9 %collective-permute-done.23 = f32[72,128]{1,0:T(8,128)S(1)} collective-permute-done((f32[72,128]{1,0:T(8,128)S(1)}, f32[72,128]{1,0:T(8,128)S(1)}, u32[]{:S(2)}, u32[]{:S(2)}) %collective-permute-start.23) | collective-permute-done | bytes 36896 | tf_op jit(solution)/shard_map/ppermute | solution.py:52
  96.7 5.2 %collective-permute-done.24 = f32[72,128]{1,0:T(8,128)S(1)} collective-permute-done((f32[72,128]{1,0:T(8,128)S(1)}, f32[72,128]{1,0:T(8,128)S(1)}, u32[]{:S(2)}, u32[]{:S(2)}) %collective-permute-start.24) | collective-permute-done | bytes 36896 | tf_op jit(solution)/shard_map/ppermute | solution.py:52
  101.9 3.2 %shard_map.57 = (f32[64,512]{1,0:T(8,128)}, f32[64,64]{1,0:T(8,128)}) custom-call(f32[72,128]{1,0:T(8,128)S(1)} %add.79.products_ref, f32[64,512]{1,0:T(8,128)S(1)} %get-tuple-element.33.image_ref), custom_call_target="tpu_custom_call" | custom-call | tf_op jit(solution)/shard_map/pallas_call | solution.py:222
  (57 shorter events, 13.5 us)
Async XLA Ops:
  0.6 1.9 %collective-permute-start = (f32[64,512]{1,0:T(8,128)}, f32[64,512]{1,0:T(8,128)S(1)}, u32[]{:S(2)}, u32[]{:S(2)}) collective-permute-start(f32[64,512]{1,0:T(8,128)} %bitcast.2), channel_id=1, source_target_pairs={{0,4},{4,0},{1,5},{5,1},{2,6},{6,2},{3,7},{7,3},{8,12},{12,8},{9,1... | collective-permute-start | bytes 393224 | tf_op jit(solution)/shard_map/ppermute | solution.py:48
  2.7 3.9 %collective-permute-start.1 = (bf16[528,512]{1,0:T(8,128)(2,1)S(1)}, bf16[528,512]{1,0:T(8,128)(2,1)S(1)}, u32[]{:S(2)}, u32[]{:S(2)}) collective-permute-start(bf16[528,512]{1,0:T(8,128)(2,1)S(1)} %shard_map.50.own_ref), channel_id=1, source_target_pairs={{0,4},{4,0},{1,5},{5,1},{2,6},{6,2},{3,7},{7,3},{8,12},{12,8},{9,1... | collective-permute-start | bytes 1622024 | tf_op jit(solution)/shard_map/ppermute | solution.py:48
  3.2 20.5 %collective-permute-start.3 = (bf16[272,512]{1,0:T(8,128)(2,1)S(1)}, bf16[272,512]{1,0:T(8,128)(2,1)S(1)}, u32[]{:S(2)}, u32[]{:S(2)}) collective-permute-start(bf16[272,512]{1,0:T(8,128)(2,1)S(1)} %pad_add_fusion.sent_ref), channel_id=1, source_target_pairs={{0,16},{1,241},{2,242},{3,19},{4,20},{5,245},{6,246},{7,23},{8,24}... | collective-permute-start | bytes 835592 | tf_op jit(solution)/shard_map/ppermute | solution.py:44
  6.4 17.9 %collective-permute-start.2 = (bf16[272,512]{1,0:T(8,128)(2,1)S(1)}, bf16[272,512]{1,0:T(8,128)(2,1)S(1)}, u32[]{:S(2)}, u32[]{:S(2)}) collective-permute-start(bf16[272,512]{1,0:T(8,128)(2,1)S(1)} %pad_add_fusion.sent_ref), channel_id=1, source_target_pairs={{0,248},{1,9},{2,10},{3,251},{4,252},{5,13},{6,14},{7,255},{8,0},{... | collective-permute-start | bytes 835592 | tf_op jit(solution)/shard_map/ppermute | solution.py:44
  26.3 5.2 %collective-permute-start.7 = (f32[1,1024]{1,0:T(1,128)S(1)}, f32[1,1024]{1,0:T(1,128)S(1)}, u32[]{:S(2)}, u32[]{:S(2)}) collective-permute-start(f32[1,1024]{1,0:T(1,128)S(1)} %maximum_add_fusion.sum_ref), channel_id=1, source_target_pairs={{0,2},{1,3},{2,0},{3,1},{4,6},{5,7},{6,4},{7,5},{8,10},{9,11},{10,... | collective-permute-start | bytes 12296 | tf_op jit(solution)/shard_map/ppermute | solution.py:57
  26.5 4.9 %collective-permute-start.6 = (f32[1,1024]{1,0:T(1,128)S(1)}, f32[1,1024]{1,0:T(1,128)S(1)}, u32[]{:S(2)}, u32[]{:S(2)}) collective-permute-start(f32[1,1024]{1,0:T(1,128)S(1)} %maximum_add_fusion.sum_ref), channel_id=1, source_target_pairs={{0,3},{1,2},{2,1},{3,0},{4,7},{5,6},{6,5},{7,4},{8,11},{9,10},{10,... | collective-permute-start | bytes 12296 | tf_op jit(solution)/shard_map/ppermute | solution.py:57
  29.5 3.6 %collective-permute-start.5 = (f32[1,1024]{1,0:T(1,128)S(1)}, f32[1,1024]{1,0:T(1,128)S(1)}, u32[]{:S(2)}, u32[]{:S(2)}) collective-permute-start(f32[1,1024]{1,0:T(1,128)S(1)} %maximum_add_fusion.sum_ref), channel_id=1, source_target_pairs={{0,1},{1,0},{2,3},{3,2},{4,5},{5,4},{6,7},{7,6},{8,9},{9,8},{10,11... | collective-permute-start | bytes 12296 | tf_op jit(solution)/shard_map/ppermute | solution.py:57
  33.4 7.0 %collective-permute-start.8 = (f32[64,256]{1,0:T(8,128)S(1)}, f32[64,256]{1,0:T(8,128)S(1)}, u32[]{:S(2)}, u32[]{:S(2)}) collective-permute-start(f32[64,256]{1,0:T(8,128)S(1)} %get-tuple-element.26), channel_id=1, source_target_pairs={{0,240},{1,17},{2,18},{3,243},{4,244},{5,21},{6,22},{7,247},{8,248... | collective-permute-start | bytes 196616 | tf_op jit(solution)/shard_map/ppermute | solution.py:44
  38.6 5.5 %collective-permute-start.9 = (f32[64,256]{1,0:T(8,128)S(1)}, f32[64,256]{1,0:T(8,128)S(1)}, u32[]{:S(2)}, u32[]{:S(2)}) collective-permute-start(f32[64,256]{1,0:T(8,128)S(1)} %get-tuple-element.27), channel_id=1, source_target_pairs={{0,8},{1,249},{2,250},{3,11},{4,12},{5,253},{6,254},{7,15},{8,16},... | collective-permute-start | bytes 196616 | tf_op jit(solution)/shard_map/ppermute | solution.py:44
  44.0 4.8 %collective-permute-start.10 = (f32[64,256]{1,0:T(8,128)S(1)}, f32[64,256]{1,0:T(8,128)S(1)}, u32[]{:S(2)}, u32[]{:S(2)}) collective-permute-start(f32[64,256]{1,0:T(8,128)S(1)} %select_add_fusion.1), channel_id=1, source_target_pairs={{0,1},{1,0},{2,3},{3,2},{4,5},{5,4},{6,7},{7,6},{8,9},{9,8},{10,11... | collective-permute-start | bytes 196616 | tf_op jit(solution)/shard_map/ppermute | solution.py:57
  44.1 6.4 %collective-permute-start.12 = (f32[64,256]{1,0:T(8,128)S(1)}, f32[64,256]{1,0:T(8,128)S(1)}, u32[]{:S(2)}, u32[]{:S(2)}) collective-permute-start(f32[64,256]{1,0:T(8,128)S(1)} %select_add_fusion.1), channel_id=1, source_target_pairs={{0,2},{1,3},{2,0},{3,1},{4,6},{5,7},{6,4},{7,5},{8,10},{9,11},{10,... | collective-permute-start | bytes 196616 | tf_op jit(solution)/shard_map/ppermute | solution.py:57
  47.6 5.5 %collective-permute-start.11 = (f32[64,256]{1,0:T(8,128)S(1)}, f32[64,256]{1,0:T(8,128)S(1)}, u32[]{:S(2)}, u32[]{:S(2)}) collective-permute-start(f32[64,256]{1,0:T(8,128)S(1)} %select_add_fusion.1), channel_id=1, source_target_pairs={{0,3},{1,2},{2,1},{3,0},{4,7},{5,6},{6,5},{7,4},{8,11},{9,10},{10,... | collective-permute-start | bytes 196616 | tf_op jit(solution)/shard_map/ppermute | solution.py:57
  53.1 1.4 %collective-permute-start.13 = (f32[64,512]{1,0:T(8,128)S(1)}, f32[64,512]{1,0:T(8,128)S(1)}, u32[]{:S(2)}, u32[]{:S(2)}) collective-permute-start(f32[64,512]{1,0:T(8,128)S(1)} %maximum_select_fusion.own_ref.first_ref), channel_id=1, source_target_pairs={{0,4},{4,0},{1,5},{5,1},{2,6},{6,2},{3,7},{7,3},{8,12},{12,8},{9,1... | collective-permute-start | bytes 393224 | tf_op jit(solution)/shard_map/ppermute | solution.py:48
  55.0 6.9 %collective-permute-start.14 = (f32[64,256]{1,0:T(8,128)S(1)}, f32[64,256]{1,0:T(8,128)S(1)}, u32[]{:S(2)}, u32[]{:S(2)}) collective-permute-start(f32[64,256]{1,0:T(8,128)S(1)} %get-tuple-element.29), channel_id=1, source_target_pairs={{0,240},{1,17},{2,18},{3,243},{4,244},{5,21},{6,22},{7,247},{8,248... | collective-permute-start | bytes 196616 | tf_op jit(solution)/shard_map/ppermute | solution.py:44
  59.5 4.3 %collective-permute-start.15 = (f32[64,256]{1,0:T(8,128)S(1)}, f32[64,256]{1,0:T(8,128)S(1)}, u32[]{:S(2)}, u32[]{:S(2)}) collective-permute-start(f32[64,256]{1,0:T(8,128)S(1)} %get-tuple-element.30), channel_id=1, source_target_pairs={{0,8},{1,249},{2,250},{3,11},{4,12},{5,253},{6,254},{7,15},{8,16},... | collective-permute-start | bytes 196616 | tf_op jit(solution)/shard_map/ppermute | solution.py:44
  63.8 4.8 %collective-permute-start.16 = (f32[64,256]{1,0:T(8,128)S(1)}, f32[64,256]{1,0:T(8,128)S(1)}, u32[]{:S(2)}, u32[]{:S(2)}) collective-permute-start(f32[64,256]{1,0:T(8,128)S(1)} %select_add_fusion), channel_id=1, source_target_pairs={{0,1},{1,0},{2,3},{3,2},{4,5},{5,4},{6,7},{7,6},{8,9},{9,8},{10,11... | collective-permute-start | bytes 196616 | tf_op jit(solution)/shard_map/ppermute | solution.py:57
  63.9 6.0 %collective-permute-start.18 = (f32[64,256]{1,0:T(8,128)S(1)}, f32[64,256]{1,0:T(8,128)S(1)}, u32[]{:S(2)}, u32[]{:S(2)}) collective-permute-start(f32[64,256]{1,0:T(8,128)S(1)} %select_add_fusion), channel_id=1, source_target_pairs={{0,2},{1,3},{2,0},{3,1},{4,6},{5,7},{6,4},{7,5},{8,10},{9,11},{10,... | collective-permute-start | bytes 196616 | tf_op jit(solution)/shard_map/ppermute | solution.py:57
  66.5 5.5 %collective-permute-start.17 = (f32[64,256]{1,0:T(8,128)S(1)}, f32[64,256]{1,0:T(8,128)S(1)}, u32[]{:S(2)}, u32[]{:S(2)}) collective-permute-start(f32[64,256]{1,0:T(8,128)S(1)} %select_add_fusion), channel_id=1, source_target_pairs={{0,3},{1,2},{2,1},{3,0},{4,7},{5,6},{6,5},{7,4},{8,11},{9,10},{10,... | collective-permute-start | bytes 196616 | tf_op jit(solution)/shard_map/ppermute | solution.py:57
  72.6 1.2 %collective-permute-start.19 = (f32[72,128]{1,0:T(8,128)S(1)}, f32[72,128]{1,0:T(8,128)S(1)}, u32[]{:S(2)}, u32[]{:S(2)}) collective-permute-start(f32[72,128]{1,0:T(8,128)S(1)} %get-tuple-element.32), channel_id=1, source_target_pairs={{0,4},{4,0},{1,5},{5,1},{2,6},{6,2},{3,7},{7,3},{8,12},{12,8},{9,1... | collective-permute-start | bytes 110600 | tf_op jit(solution)/shard_map/ppermute | solution.py:48
  73.8 7.0 %collective-permute-start.20 = (f32[72,128]{1,0:T(8,128)S(1)}, f32[72,128]{1,0:T(8,128)S(1)}, u32[]{:S(2)}, u32[]{:S(2)}) collective-permute-start(f32[72,128]{1,0:T(8,128)S(1)} %add.74), channel_id=1, source_target_pairs={{0,8},{8,0},{16,24},{24,16},{32,40},{40,32},{48,56},{56,48},{64,72... | collective-permute-start | bytes 110600 | tf_op jit(solution)/shard_map/ppermute | solution.py:52
  80.9 4.9 %collective-permute-start.21 = (f32[72,128]{1,0:T(8,128)S(1)}, f32[72,128]{1,0:T(8,128)S(1)}, u32[]{:S(2)}, u32[]{:S(2)}) collective-permute-start(f32[72,128]{1,0:T(8,128)S(1)} %add.75), channel_id=1, source_target_pairs={{0,16},{8,24},{16,0},{24,8},{32,48},{40,56},{48,32},{56,40},{64,80... | collective-permute-start | bytes 110600 | tf_op jit(solution)/shard_map/ppermute | solution.py:52
  85.7 7.0 %collective-permute-start.22 = (f32[72,128]{1,0:T(8,128)S(1)}, f32[72,128]{1,0:T(8,128)S(1)}, u32[]{:S(2)}, u32[]{:S(2)}) collective-permute-start(f32[72,128]{1,0:T(8,128)S(1)} %add.76), channel_id=1, source_target_pairs={{0,56},{8,48},{16,40},{24,32},{32,24},{40,16},{48,8},{56,0},{64,12... | collective-permute-start | bytes 110600 | tf_op jit(solution)/shard_map/ppermute | solution.py:52
  92.8 4.0 %collective-permute-start.23 = (f32[72,128]{1,0:T(8,128)S(1)}, f32[72,128]{1,0:T(8,128)S(1)}, u32[]{:S(2)}, u32[]{:S(2)}) collective-permute-start(f32[72,128]{1,0:T(8,128)S(1)} %add.77), channel_id=1, source_target_pairs={{0,64},{8,72},{16,80},{24,88},{32,96},{40,104},{48,112},{56,120},{... | collective-permute-start | bytes 110600 | tf_op jit(solution)/shard_map/ppermute | solution.py:52
  96.7 5.2 %collective-permute-start.24 = (f32[72,128]{1,0:T(8,128)S(1)}, f32[72,128]{1,0:T(8,128)S(1)}, u32[]{:S(2)}, u32[]{:S(2)}) collective-permute-start(f32[72,128]{1,0:T(8,128)S(1)} %add.78), channel_id=1, source_target_pairs={{0,192},{8,200},{16,208},{24,216},{32,224},{40,232},{48,240},{56,2... | collective-permute-start | bytes 110600 | tf_op jit(solution)/shard_map/ppermute | solution.py:52
  (3 other events, 11.9 us)

commit v4 on v3

--- a/solution.py
+++ b/solution.py
@@ -48,8 +48,11 @@
     return lax.ppermute(array, "core", [(0, 1), (1, 0)])
 
 
-def other_chip(array, bits):
-    return lax.ppermute(array, "chip", [(i, i ^ bits) for i in range(CHIPS)])
+def other_chip(array, bits, core_bit=0):
+    count = CHIPS * CORES
+    return lax.ppermute(
+        array, ("chip", "core"), [(i, i ^ (CORES * bits + core_bit)) for i in range(count)]
+    )
 
 
 def other_planes(array):
@@ -114,13 +117,18 @@
     sum_out[...] = write_tiles((own_ref, mate_ref), bias, cols, own_out)
 
 
-def reach_kernel(reaches, own_ref, mate_ref, reach_ref, sum_ref, tiles_out, sum_out):
+def reach_kernel(
+    reaches, own_ref, mate_ref, reach_ref, sum_ref, tiles_out, sum_out, *turned_out
+):
     core, parity, _ = place()
     reach = jnp.where(parity == 0, reaches[0], reaches[1])
     masks = mask_row(own_ref), mask_row(mate_ref)
     bias = column_bias(reach, *masks, mask_row(reach_ref), core)
     rows = (own_ref, mate_ref)
-    sum_out[...] = sum_ref[...] + write_tiles(rows, bias, reach_ref[:HALF, :], tiles_out)
+    total = sum_ref[...] + write_tiles(rows, bias, reach_ref[:HALF, :], tiles_out)
+    sum_out[...] = total
+    for out_ref in turned_out:
+        out_ref[...] = jnp.concatenate([total[:, BLOCK:], total[:, :BLOCK]], axis=1)
 
 
 def multiply(vectors, far_ref, near_ref, own_ref, far_out, near_out, own_out):
@@ -245,16 +253,15 @@
     )
     mate = swap_core(packed)
     near = move(sent, NEAR, -1)
-    tiles = [((wide, HALF), bf16), ((1, wide), f32)]
+    tiles = [((wide, HALF), bf16), ((1, wide), f32), ((1, wide), f32)]
     own_weights, sums = call(
         own_kernel, [((wide, QUARTER), bf16), ((1, wide), f32)], (packed, mate)
     )
     far_kernel = functools.partial(reach_kernel, FAR)
     near_kernel = functools.partial(reach_kernel, NEAR)
-    far_weights, sums = call(far_kernel, tiles, (packed, mate, far, sums))
-    near_weights, sums = call(near_kernel, tiles, (packed, mate, near, sums))
-    other = swap_core(sums)
-    sums = sums + jnp.concatenate([other[:, BLOCK:], other[:, :BLOCK]], axis=1)
+    far_weights, sums = call(far_kernel, tiles[:2], (packed, mate, far, sums))
+    near_weights, sums, turned = call(near_kernel, tiles, (packed, mate, near, sums))
+    sums = sums + swap_core(turned)
     plane_sums = [sums, *other_planes(sums)]
     weights = (far_weights, near_weights, own_weights)
     terms = [((BASIS, HALF), f32), ((BASIS, HALF), f32), ((BASIS, QUARTER), f32)]
@@ -286,9 +293,12 @@
     image, products = call(
         products_kernel, [((BASIS, BLOCK), f32), ((BASIS + 8, 128), f32)], (root, first, second)
     )
-    products = products + swap_core(products)
-    for bits in (1, 2, 7, 8, 24):
-        products = products + other_chip(products, bits)
+    for group in ((8, 24, 16), (1, 2, 3)):
+        one, two, three = [other_chip(products, bits) for bits in group]
+        products = (products + one) + (two + three)
+    mate_products = swap_core(products)
+    one, two = other_chip(products, 7), other_chip(products, 7, 1)
+    products = (products + mate_products) + (one + two)
     basis, projected = call(
         finish_kernel, [((BASIS, BLOCK), f32), ((BASIS, BASIS), f32)], (products, image)
     )

time: 105 us -> 101 us (0.962)
  waiting for transfers between devices: 61 us -> 45.3 us
  starting transfers between devices: 34.8 us -> 45.6 us
    ppermute x5 -> x8, waiting for transfers between devices: 22.9 us -> 8.44 us  [other_chip(): lax.ppermute(array, ('chip', 'core'), [(i, i ^ CORES * bits + core_bit) f...]
    ppermute x5 -> x8, starting transfers between devices: 5.12 us -> 11.2 us  [other_chip(): lax.ppermute(array, ('chip', 'core'), [(i, i ^ CORES * bits + core_bit) f...]
    ppermute x5, starting transfers between devices: 0.74 us -> 5.54 us  [swap_core(): return lax.ppermute(array, 'core', [(0, 1), (1, 0)])]
    ppermute x5, waiting for transfers between devices: 3.69 us -> 2.5 us  [swap_core(): return lax.ppermute(array, 'core', [(0, 1), (1, 0)])]
  transfers between devices with their start and end apart: 25 -> 28, of which waited for: 18 -> 18; matrix products, arithmetic and copies ran while one was open for 2% -> 2% of each run, Pallas kernels for 1% -> 1%
where the time goes in v4:
time: 101 us; the launch traced here: 100 us
  starting transfers between devices  45.6 us (45%)
  waiting for transfers between devices  45.3 us (45%)
  Pallas kernels  6.6 us (7%)
  local copies, waits for them, and re-layouts  1.15 us (1%)
    ppermute x6, waiting for transfers between devices, move(): return lax.ppermute(array, ALL_AXES, moves)  23.8 us
    ppermute x6, starting transfers between devices, move(): return lax.ppermute(array, ALL_AXES, moves)  15.4 us
    ppermute x9, starting transfers between devices, other_planes(): lax.ppermute(array, 'pairs', [(i, step(i)) for i in range(PAIRS)])  13.4 us
    ppermute x8, starting transfers between devices, other_chip(): lax.ppermute(array, ('chip', 'core'), [(i, i ^ CORES * bits + core_bit) f...  11.2 us
    ppermute x9, waiting for transfers between devices, other_planes(): lax.ppermute(array, 'pairs', [(i, step(i)) for i in range(PAIRS)])  10.5 us
    ppermute x8, waiting for transfers between devices, other_chip(): lax.ppermute(array, ('chip', 'core'), [(i, i ^ CORES * bits + core_bit) f...  8.44 us
    pallas_call x8, Pallas kernels, call(): pl.pallas_call(kernel, out_shape=[jax.ShapeDtypeStruct(shape, dtype) for...  6.6 us
    ppermute x5, starting transfers between devices, swap_core(): return lax.ppermute(array, 'core', [(0, 1), (1, 0)])  5.54 us
  transfers between devices with their start and end apart: 28, of which 18 were waited for; matrix products, arithmetic and copies ran while one was open for 2% of the time, Pallas kernels for 1%

profile of v4, /device:TPU:32, one launch (start us, length us, event | category | flops | bytes accessed | tf_op | source)
XLA Modules:
  0.0 100.3 jit_solution(6003861820295397540)
XLA Ops:
  3.2 3.3 %collective-permute-start.3 = (bf16[272,512]{1,0:T(8,128)(2,1)S(1)}, bf16[272,512]{1,0:T(8,128)(2,1)S(1)}, u32[]{:S(2)}, u32[]{:S(2)}) collective-permute-start(bf16[272,512]{1,0:T(8,128)(2,1)S(1)} %pad_add_fusion.sent_ref), channel_id=1, source_target_pairs={{0,16},{1,241},{2,242},{3,19},{4,20},{5,245},{6,246},{7,23},{8,24}... | collective-permute-start | bytes 835592 | tf_op jit(solution)/shard_map/ppermute | solution.py:44
  7.2 16.5 %collective-permute-done.3.reach_ref = bf16[272,512]{1,0:T(8,128)(2,1)S(1)} collective-permute-done((bf16[272,512]{1,0:T(8,128)(2,1)S(1)}, bf16[272,512]{1,0:T(8,128)(2,1)S(1)}, u32[]{:S(2)}, u32[]{:S(2)}) %collective-permute-start.3) | collective-permute-done | bytes 278560 | tf_op jit(solution)/shard_map/ppermute | solution.py:44
  26.5 2.9 %collective-permute-start.6 = (f32[1,1024]{1,0:T(1,128)S(1)}, f32[1,1024]{1,0:T(1,128)S(1)}, u32[]{:S(2)}, u32[]{:S(2)}) collective-permute-start(f32[1,1024]{1,0:T(1,128)S(1)} %add.74.sum_ref), channel_id=1, source_target_pairs={{0,3},{1,2},{2,1},{3,0},{4,7},{5,6},{6,5},{7,4},{8,11},{9,10},{10,... | collective-permute-start | bytes 12296 | tf_op jit(solution)/shard_map/ppermute | solution.py:60
  31.5 1.6 %collective-permute-done.5.same_ref = f32[1,1024]{1,0:T(1,128)S(1)} collective-permute-done((f32[1,1024]{1,0:T(1,128)S(1)}, f32[1,1024]{1,0:T(1,128)S(1)}, u32[]{:S(2)}, u32[]{:S(2)}) %collective-permute-start.5) | collective-permute-done | bytes 4128 | tf_op jit(solution)/shard_map/ppermute | solution.py:60
  33.4 5.1 %collective-permute-start.8 = (f32[64,256]{1,0:T(8,128)S(1)}, f32[64,256]{1,0:T(8,128)S(1)}, u32[]{:S(2)}, u32[]{:S(2)}) collective-permute-start(f32[64,256]{1,0:T(8,128)S(1)} %get-tuple-element.28), channel_id=1, source_target_pairs={{0,240},{1,17},{2,18},{3,243},{4,244},{5,21},{6,22},{7,247},{8,248... | collective-permute-start | bytes 196616 | tf_op jit(solution)/shard_map/ppermute | solution.py:44
  38.6 1.9 %collective-permute-done.8 = f32[64,256]{1,0:T(8,128)S(1)} collective-permute-done((f32[64,256]{1,0:T(8,128)S(1)}, f32[64,256]{1,0:T(8,128)S(1)}, u32[]{:S(2)}, u32[]{:S(2)}) %collective-permute-start.8) | collective-permute-done | bytes 65568 | tf_op jit(solution)/shard_map/ppermute | solution.py:44
  40.5 3.6 %collective-permute-done.9 = f32[64,256]{1,0:T(8,128)S(1)} collective-permute-done((f32[64,256]{1,0:T(8,128)S(1)}, f32[64,256]{1,0:T(8,128)S(1)}, u32[]{:S(2)}, u32[]{:S(2)}) %collective-permute-start.9) | collective-permute-done | bytes 65568 | tf_op jit(solution)/shard_map/ppermute | solution.py:44
  44.1 3.5 %collective-permute-start.12 = (f32[64,256]{1,0:T(8,128)S(1)}, f32[64,256]{1,0:T(8,128)S(1)}, u32[]{:S(2)}, u32[]{:S(2)}) collective-permute-start(f32[64,256]{1,0:T(8,128)S(1)} %select_add_fusion.1), channel_id=1, source_target_pairs={{0,2},{1,3},{2,0},{3,1},{4,6},{5,7},{6,4},{7,5},{8,10},{9,11},{10,... | collective-permute-start | bytes 196616 | tf_op jit(solution)/shard_map/ppermute | solution.py:60
  48.8 1.7 %collective-permute-done.12 = f32[64,256]{1,0:T(8,128)S(1)} collective-permute-done((f32[64,256]{1,0:T(8,128)S(1)}, f32[64,256]{1,0:T(8,128)S(1)}, u32[]{:S(2)}, u32[]{:S(2)}) %collective-permute-start.12) | collective-permute-done | bytes 65568 | tf_op jit(solution)/shard_map/ppermute | solution.py:60
  50.6 2.5 %collective-permute-done.11 = f32[64,256]{1,0:T(8,128)S(1)} collective-permute-done((f32[64,256]{1,0:T(8,128)S(1)}, f32[64,256]{1,0:T(8,128)S(1)}, u32[]{:S(2)}, u32[]{:S(2)}) %collective-permute-start.11) | collective-permute-done | bytes 65568 | tf_op jit(solution)/shard_map/ppermute | solution.py:60
  55.0 4.5 %collective-permute-start.14 = (f32[64,256]{1,0:T(8,128)S(1)}, f32[64,256]{1,0:T(8,128)S(1)}, u32[]{:S(2)}, u32[]{:S(2)}) collective-permute-start(f32[64,256]{1,0:T(8,128)S(1)} %get-tuple-element.31), channel_id=1, source_target_pairs={{0,240},{1,17},{2,18},{3,243},{4,244},{5,21},{6,22},{7,247},{8,248... | collective-permute-start | bytes 196616 | tf_op jit(solution)/shard_map/ppermute | solution.py:44
  59.5 2.4 %collective-permute-start.15 = (f32[64,256]{1,0:T(8,128)S(1)}, f32[64,256]{1,0:T(8,128)S(1)}, u32[]{:S(2)}, u32[]{:S(2)}) collective-permute-start(f32[64,256]{1,0:T(8,128)S(1)} %get-tuple-element.32), channel_id=1, source_target_pairs={{0,8},{1,249},{2,250},{3,11},{4,12},{5,253},{6,254},{7,15},{8,16},... | collective-permute-start | bytes 196616 | tf_op jit(solution)/shard_map/ppermute | solution.py:44
  61.8 1.9 %collective-permute-done.15 = f32[64,256]{1,0:T(8,128)S(1)} collective-permute-done((f32[64,256]{1,0:T(8,128)S(1)}, f32[64,256]{1,0:T(8,128)S(1)}, u32[]{:S(2)}, u32[]{:S(2)}) %collective-permute-start.15) | collective-permute-done | bytes 65568 | tf_op jit(solution)/shard_map/ppermute | solution.py:44
  63.9 2.7 %collective-permute-start.18 = (f32[64,256]{1,0:T(8,128)S(1)}, f32[64,256]{1,0:T(8,128)S(1)}, u32[]{:S(2)}, u32[]{:S(2)}) collective-permute-start(f32[64,256]{1,0:T(8,128)S(1)} %select_add_fusion), channel_id=1, source_target_pairs={{0,2},{1,3},{2,0},{3,1},{4,6},{5,7},{6,4},{7,5},{8,10},{9,11},{10,... | collective-permute-start | bytes 196616 | tf_op jit(solution)/shard_map/ppermute | solution.py:60
  66.5 2.0 %collective-permute-start.17 = (f32[64,256]{1,0:T(8,128)S(1)}, f32[64,256]{1,0:T(8,128)S(1)}, u32[]{:S(2)}, u32[]{:S(2)}) collective-permute-start(f32[64,256]{1,0:T(8,128)S(1)} %select_add_fusion), channel_id=1, source_target_pairs={{0,3},{1,2},{2,1},{3,0},{4,7},{5,6},{6,5},{7,4},{8,11},{9,10},{10,... | collective-permute-start | bytes 196616 | tf_op jit(solution)/shard_map/ppermute | solution.py:60
  69.8 2.2 %collective-permute-done.17 = f32[64,256]{1,0:T(8,128)S(1)} collective-permute-done((f32[64,256]{1,0:T(8,128)S(1)}, f32[64,256]{1,0:T(8,128)S(1)}, u32[]{:S(2)}, u32[]{:S(2)}) %collective-permute-start.17) | collective-permute-done | bytes 65568 | tf_op jit(solution)/shard_map/ppermute | solution.py:60
  72.7 3.4 %collective-permute-start.19 = (f32[72,128]{1,0:T(8,128)S(1)}, f32[72,128]{1,0:T(8,128)S(1)}, u32[]{:S(2)}, u32[]{:S(2)}) collective-permute-start(f32[72,128]{1,0:T(8,128)S(1)} %get-tuple-element.34), channel_id=1, source_target_pairs={{0,64},{4,68},{8,72},{12,76},{16,80},{20,84},{24,88},{28,92},{32,9... | collective-permute-start | bytes 110600 | tf_op jit(solution)/shard_map/ppermute | solution.py:53
  76.1 2.1 %collective-permute-done.21 = f32[72,128]{1,0:T(8,128)S(1)} collective-permute-done((f32[72,128]{1,0:T(8,128)S(1)}, f32[72,128]{1,0:T(8,128)S(1)}, u32[]{:S(2)}, u32[]{:S(2)}) %collective-permute-start.21) | collective-permute-done | bytes 36896 | tf_op jit(solution)/shard_map/ppermute | solution.py:53
  78.3 2.4 %collective-permute-start.24 = (f32[72,128]{1,0:T(8,128)S(1)}, f32[72,128]{1,0:T(8,128)S(1)}, u32[]{:S(2)}, u32[]{:S(2)}) collective-permute-start(f32[72,128]{1,0:T(8,128)S(1)} %add_add_fusion.2), channel_id=1, source_target_pairs={{0,24},{4,28},{8,16},{12,20},{16,8},{20,12},{24,0},{28,4},{32,56},... | collective-permute-start | bytes 110600 | tf_op jit(solution)/shard_map/ppermute | solution.py:53
  80.7 5.1 %collective-permute-start.23 = (f32[72,128]{1,0:T(8,128)S(1)}, f32[72,128]{1,0:T(8,128)S(1)}, u32[]{:S(2)}, u32[]{:S(2)}) collective-permute-start(f32[72,128]{1,0:T(8,128)S(1)} %add_add_fusion.2), channel_id=1, source_target_pairs={{0,16},{4,20},{8,24},{12,28},{16,0},{20,4},{24,8},{28,12},{32,48},... | collective-permute-start | bytes 110600 | tf_op jit(solution)/shard_map/ppermute | solution.py:53
  85.8 2.3 %collective-permute-done.23 = f32[72,128]{1,0:T(8,128)S(1)} collective-permute-done((f32[72,128]{1,0:T(8,128)S(1)}, f32[72,128]{1,0:T(8,128)S(1)}, u32[]{:S(2)}, u32[]{:S(2)}) %collective-permute-start.23) | collective-permute-done | bytes 36896 | tf_op jit(solution)/shard_map/ppermute | solution.py:53
  88.2 1.6 %collective-permute-done.22 = f32[72,128]{1,0:T(8,128)S(1)} collective-permute-done((f32[72,128]{1,0:T(8,128)S(1)}, f32[72,128]{1,0:T(8,128)S(1)}, u32[]{:S(2)}, u32[]{:S(2)}) %collective-permute-start.22) | collective-permute-done | bytes 36896 | tf_op jit(solution)/shard_map/ppermute | solution.py:53
  90.0 4.8 %collective-permute-start.25 = (f32[72,128]{1,0:T(8,128)S(1)}, f32[72,128]{1,0:T(8,128)S(1)}, u32[]{:S(2)}, u32[]{:S(2)}) collective-permute-start(f32[72,128]{1,0:T(8,128)S(1)} %add_add_fusion.1), channel_id=1, source_target_pairs={{0,4},{4,0},{1,5},{5,1},{2,6},{6,2},{3,7},{7,3},{8,12},{12,8},{9,1... | collective-permute-start | bytes 110600 | tf_op jit(solution)/shard_map/ppermute | solution.py:48
  97.1 3.2 %shard_map.57 = (f32[64,512]{1,0:T(8,128)}, f32[64,64]{1,0:T(8,128)}) custom-call(f32[72,128]{1,0:T(8,128)S(1)} %add_add_fusion.products_ref, f32[64,512]{1,0:T(8,128)S(1)} %get-tuple-element.35.image_ref), custom_call_target="tpu_custom_call" | custom-call | tf_op jit(solution)/shard_map/pallas_call | solution.py:230
  (59 shorter events, 16.3 us)
Async XLA Ops:
  2.7 3.9 %collective-permute-start.1 = (bf16[528,512]{1,0:T(8,128)(2,1)S(1)}, bf16[528,512]{1,0:T(8,128)(2,1)S(1)}, u32[]{:S(2)}, u32[]{:S(2)}) collective-permute-start(bf16[528,512]{1,0:T(8,128)(2,1)S(1)} %shard_map.50.own_ref), channel_id=1, source_target_pairs={{0,4},{4,0},{1,5},{5,1},{2,6},{6,2},{3,7},{7,3},{8,12},{12,8},{9,1... | collective-permute-start | bytes 1622024 | tf_op jit(solution)/shard_map/ppermute | solution.py:48
  3.2 20.5 %collective-permute-start.3 = (bf16[272,512]{1,0:T(8,128)(2,1)S(1)}, bf16[272,512]{1,0:T(8,128)(2,1)S(1)}, u32[]{:S(2)}, u32[]{:S(2)}) collective-permute-start(bf16[272,512]{1,0:T(8,128)(2,1)S(1)} %pad_add_fusion.sent_ref), channel_id=1, source_target_pairs={{0,16},{1,241},{2,242},{3,19},{4,20},{5,245},{6,246},{7,23},{8,24}... | collective-permute-start | bytes 835592 | tf_op jit(solution)/shard_map/ppermute | solution.py:44
  6.4 17.9 %collective-permute-start.2 = (bf16[272,512]{1,0:T(8,128)(2,1)S(1)}, bf16[272,512]{1,0:T(8,128)(2,1)S(1)}, u32[]{:S(2)}, u32[]{:S(2)}) collective-permute-start(bf16[272,512]{1,0:T(8,128)(2,1)S(1)} %pad_add_fusion.sent_ref), channel_id=1, source_target_pairs={{0,248},{1,9},{2,10},{3,251},{4,252},{5,13},{6,14},{7,255},{8,0},{... | collective-permute-start | bytes 835592 | tf_op jit(solution)/shard_map/ppermute | solution.py:44
  26.4 5.1 %collective-permute-start.7 = (f32[1,1024]{1,0:T(1,128)S(1)}, f32[1,1024]{1,0:T(1,128)S(1)}, u32[]{:S(2)}, u32[]{:S(2)}) collective-permute-start(f32[1,1024]{1,0:T(1,128)S(1)} %add.74.sum_ref), channel_id=1, source_target_pairs={{0,2},{1,3},{2,0},{3,1},{4,6},{5,7},{6,4},{7,5},{8,10},{9,11},{10,... | collective-permute-start | bytes 12296 | tf_op jit(solution)/shard_map/ppermute | solution.py:60
  26.5 4.9 %collective-permute-start.6 = (f32[1,1024]{1,0:T(1,128)S(1)}, f32[1,1024]{1,0:T(1,128)S(1)}, u32[]{:S(2)}, u32[]{:S(2)}) collective-permute-start(f32[1,1024]{1,0:T(1,128)S(1)} %add.74.sum_ref), channel_id=1, source_target_pairs={{0,3},{1,2},{2,1},{3,0},{4,7},{5,6},{6,5},{7,4},{8,11},{9,10},{10,... | collective-permute-start | bytes 12296 | tf_op jit(solution)/shard_map/ppermute | solution.py:60
  33.4 7.0 %collective-permute-start.8 = (f32[64,256]{1,0:T(8,128)S(1)}, f32[64,256]{1,0:T(8,128)S(1)}, u32[]{:S(2)}, u32[]{:S(2)}) collective-permute-start(f32[64,256]{1,0:T(8,128)S(1)} %get-tuple-element.28), channel_id=1, source_target_pairs={{0,240},{1,17},{2,18},{3,243},{4,244},{5,21},{6,22},{7,247},{8,248... | collective-permute-start | bytes 196616 | tf_op jit(solution)/shard_map/ppermute | solution.py:44
  38.6 5.5 %collective-permute-start.9 = (f32[64,256]{1,0:T(8,128)S(1)}, f32[64,256]{1,0:T(8,128)S(1)}, u32[]{:S(2)}, u32[]{:S(2)}) collective-permute-start(f32[64,256]{1,0:T(8,128)S(1)} %get-tuple-element.29), channel_id=1, source_target_pairs={{0,8},{1,249},{2,250},{3,11},{4,12},{5,253},{6,254},{7,15},{8,16},... | collective-permute-start | bytes 196616 | tf_op jit(solution)/shard_map/ppermute | solution.py:44
  44.0 4.8 %collective-permute-start.10 = (f32[64,256]{1,0:T(8,128)S(1)}, f32[64,256]{1,0:T(8,128)S(1)}, u32[]{:S(2)}, u32[]{:S(2)}) collective-permute-start(f32[64,256]{1,0:T(8,128)S(1)} %select_add_fusion.1), channel_id=1, source_target_pairs={{0,1},{1,0},{2,3},{3,2},{4,5},{5,4},{6,7},{7,6},{8,9},{9,8},{10,11... | collective-permute-start | bytes 196616 | tf_op jit(solution)/shard_map/ppermute | solution.py:60
  44.1 6.4 %collective-permute-start.12 = (f32[64,256]{1,0:T(8,128)S(1)}, f32[64,256]{1,0:T(8,128)S(1)}, u32[]{:S(2)}, u32[]{:S(2)}) collective-permute-start(f32[64,256]{1,0:T(8,128)S(1)} %select_add_fusion.1), channel_id=1, source_target_pairs={{0,2},{1,3},{2,0},{3,1},{4,6},{5,7},{6,4},{7,5},{8,10},{9,11},{10,... | collective-permute-start | bytes 196616 | tf_op jit(solution)/shard_map/ppermute | solution.py:60
  47.6 5.5 %collective-permute-start.11 = (f32[64,256]{1,0:T(8,128)S(1)}, f32[64,256]{1,0:T(8,128)S(1)}, u32[]{:S(2)}, u32[]{:S(2)}) collective-permute-start(f32[64,256]{1,0:T(8,128)S(1)} %select_add_fusion.1), channel_id=1, source_target_pairs={{0,3},{1,2},{2,1},{3,0},{4,7},{5,6},{6,5},{7,4},{8,11},{9,10},{10,... | collective-permute-start | bytes 196616 | tf_op jit(solution)/shard_map/ppermute | solution.py:60
  55.0 6.9 %collective-permute-start.14 = (f32[64,256]{1,0:T(8,128)S(1)}, f32[64,256]{1,0:T(8,128)S(1)}, u32[]{:S(2)}, u32[]{:S(2)}) collective-permute-start(f32[64,256]{1,0:T(8,128)S(1)} %get-tuple-element.31), channel_id=1, source_target_pairs={{0,240},{1,17},{2,18},{3,243},{4,244},{5,21},{6,22},{7,247},{8,248... | collective-permute-start | bytes 196616 | tf_op jit(solution)/shard_map/ppermute | solution.py:44
  59.5 4.3 %collective-permute-start.15 = (f32[64,256]{1,0:T(8,128)S(1)}, f32[64,256]{1,0:T(8,128)S(1)}, u32[]{:S(2)}, u32[]{:S(2)}) collective-permute-start(f32[64,256]{1,0:T(8,128)S(1)} %get-tuple-element.32), channel_id=1, source_target_pairs={{0,8},{1,249},{2,250},{3,11},{4,12},{5,253},{6,254},{7,15},{8,16},... | collective-permute-start | bytes 196616 | tf_op jit(solution)/shard_map/ppermute | solution.py:44
  63.8 4.8 %collective-permute-start.16 = (f32[64,256]{1,0:T(8,128)S(1)}, f32[64,256]{1,0:T(8,128)S(1)}, u32[]{:S(2)}, u32[]{:S(2)}) collective-permute-start(f32[64,256]{1,0:T(8,128)S(1)} %select_add_fusion), channel_id=1, source_target_pairs={{0,1},{1,0},{2,3},{3,2},{4,5},{5,4},{6,7},{7,6},{8,9},{9,8},{10,11... | collective-permute-start | bytes 196616 | tf_op jit(solution)/shard_map/ppermute | solution.py:60
  63.9 6.0 %collective-permute-start.18 = (f32[64,256]{1,0:T(8,128)S(1)}, f32[64,256]{1,0:T(8,128)S(1)}, u32[]{:S(2)}, u32[]{:S(2)}) collective-permute-start(f32[64,256]{1,0:T(8,128)S(1)} %select_add_fusion), channel_id=1, source_target_pairs={{0,2},{1,3},{2,0},{3,1},{4,6},{5,7},{6,4},{7,5},{8,10},{9,11},{10,... | collective-permute-start | bytes 196616 | tf_op jit(solution)/shard_map/ppermute | solution.py:60
  66.5 5.5 %collective-permute-start.17 = (f32[64,256]{1,0:T(8,128)S(1)}, f32[64,256]{1,0:T(8,128)S(1)}, u32[]{:S(2)}, u32[]{:S(2)}) collective-permute-start(f32[64,256]{1,0:T(8,128)S(1)} %select_add_fusion), channel_id=1, source_target_pairs={{0,3},{1,2},{2,1},{3,0},{4,7},{5,6},{6,5},{7,4},{8,11},{9,10},{10,... | collective-permute-start | bytes 196616 | tf_op jit(solution)/shard_map/ppermute | solution.py:60
  72.6 5.6 %collective-permute-start.21 = (f32[72,128]{1,0:T(8,128)S(1)}, f32[72,128]{1,0:T(8,128)S(1)}, u32[]{:S(2)}, u32[]{:S(2)}) collective-permute-start(f32[72,128]{1,0:T(8,128)S(1)} %get-tuple-element.34), channel_id=1, source_target_pairs={{0,128},{4,132},{8,136},{12,140},{16,144},{20,148},{24,152},{28,15... | collective-permute-start | bytes 110600 | tf_op jit(solution)/shard_map/ppermute | solution.py:53
  72.6 5.7 %collective-permute-start.20 = (f32[72,128]{1,0:T(8,128)S(1)}, f32[72,128]{1,0:T(8,128)S(1)}, u32[]{:S(2)}, u32[]{:S(2)}) collective-permute-start(f32[72,128]{1,0:T(8,128)S(1)} %get-tuple-element.34), channel_id=1, source_target_pairs={{0,192},{4,196},{8,200},{12,204},{16,208},{20,212},{24,216},{28,22... | collective-permute-start | bytes 110600 | tf_op jit(solution)/shard_map/ppermute | solution.py:53
  72.7 5.6 %collective-permute-start.19 = (f32[72,128]{1,0:T(8,128)S(1)}, f32[72,128]{1,0:T(8,128)S(1)}, u32[]{:S(2)}, u32[]{:S(2)}) collective-permute-start(f32[72,128]{1,0:T(8,128)S(1)} %get-tuple-element.34), channel_id=1, source_target_pairs={{0,64},{4,68},{8,72},{12,76},{16,80},{20,84},{24,88},{28,92},{32,9... | collective-permute-start | bytes 110600 | tf_op jit(solution)/shard_map/ppermute | solution.py:53
  78.3 7.6 %collective-permute-start.24 = (f32[72,128]{1,0:T(8,128)S(1)}, f32[72,128]{1,0:T(8,128)S(1)}, u32[]{:S(2)}, u32[]{:S(2)}) collective-permute-start(f32[72,128]{1,0:T(8,128)S(1)} %add_add_fusion.2), channel_id=1, source_target_pairs={{0,24},{4,28},{8,16},{12,20},{16,8},{20,12},{24,0},{28,4},{32,56},... | collective-permute-start | bytes 110600 | tf_op jit(solution)/shard_map/ppermute | solution.py:53
  80.7 7.4 %collective-permute-start.23 = (f32[72,128]{1,0:T(8,128)S(1)}, f32[72,128]{1,0:T(8,128)S(1)}, u32[]{:S(2)}, u32[]{:S(2)}) collective-permute-start(f32[72,128]{1,0:T(8,128)S(1)} %add_add_fusion.2), channel_id=1, source_target_pairs={{0,16},{4,20},{8,24},{12,28},{16,0},{20,4},{24,8},{28,12},{32,48},... | collective-permute-start | bytes 110600 | tf_op jit(solution)/shard_map/ppermute | solution.py:53
  85.8 4.0 %collective-permute-start.22 = (f32[72,128]{1,0:T(8,128)S(1)}, f32[72,128]{1,0:T(8,128)S(1)}, u32[]{:S(2)}, u32[]{:S(2)}) collective-permute-start(f32[72,128]{1,0:T(8,128)S(1)} %add_add_fusion.2), channel_id=1, source_target_pairs={{0,8},{4,12},{8,0},{12,4},{16,24},{20,28},{24,16},{28,20},{32,40},... | collective-permute-start | bytes 110600 | tf_op jit(solution)/shard_map/ppermute | solution.py:53
  89.8 6.5 %collective-permute-start.27 = (f32[72,128]{1,0:T(8,128)S(1)}, f32[72,128]{1,0:T(8,128)S(1)}, u32[]{:S(2)}, u32[]{:S(2)}) collective-permute-start(f32[72,128]{1,0:T(8,128)S(1)} %add_add_fusion.1), channel_id=1, source_target_pairs={{0,60},{4,56},{8,52},{12,48},{16,44},{20,40},{24,36},{28,32},{32,2... | collective-permute-start | bytes 110600 | tf_op jit(solution)/shard_map/ppermute | solution.py:53
  89.9 7.2 %collective-permute-start.26 = (f32[72,128]{1,0:T(8,128)S(1)}, f32[72,128]{1,0:T(8,128)S(1)}, u32[]{:S(2)}, u32[]{:S(2)}) collective-permute-start(f32[72,128]{1,0:T(8,128)S(1)} %add_add_fusion.1), channel_id=1, source_target_pairs={{0,56},{4,60},{8,48},{12,52},{16,40},{20,44},{24,32},{28,36},{32,2... | collective-permute-start | bytes 110600 | tf_op jit(solution)/shard_map/ppermute | solution.py:53
  90.0 7.1 %collective-permute-start.25 = (f32[72,128]{1,0:T(8,128)S(1)}, f32[72,128]{1,0:T(8,128)S(1)}, u32[]{:S(2)}, u32[]{:S(2)}) collective-permute-start(f32[72,128]{1,0:T(8,128)S(1)} %add_add_fusion.1), channel_id=1, source_target_pairs={{0,4},{4,0},{1,5},{5,1},{2,6},{6,2},{3,7},{7,3},{8,12},{12,8},{9,1... | collective-permute-start | bytes 110600 | tf_op jit(solution)/shard_map/ppermute | solution.py:48
  (6 other events, 18.9 us)

commit v5 on v4

--- a/solution.py
+++ b/solution.py
@@ -18,6 +18,8 @@
 REACH = 5
 CHUNK = 256
 STEP = 8
+PIECE = 64
+MAIN = 192
 EXPONENT = -math.log(BLOCK / 4) / (2 * WIDTH) * math.log2(math.e)
 UNLISTED = -1e30
 CHIPS = 32
@@ -32,14 +34,15 @@
 EXACT = lax.Precision.HIGHEST
 
 
-def move(array, reaches, sign):
+def move(array, reaches, sign, across=0):
     moves = []
     for chip in range(CHIPS):
         for core in range(CORES):
             for pair in range(PAIRS):
-                to_chip = (chip + sign * reaches[PARITIES[pair]]) % CHIPS
+                to_pair = pair ^ across
+                to_chip = (chip + sign * reaches[PARITIES[to_pair]]) % CHIPS
                 source = (chip * CORES + core) * PAIRS + pair
-                target = (to_chip * CORES + core) * PAIRS + pair
+                target = (to_chip * CORES + core) * PAIRS + to_pair
                 moves.append((source, target))
     return lax.ppermute(array, ALL_AXES, moves)
 
@@ -68,9 +71,45 @@
     return lax.axis_index("core"), parity, jnp.where(pair >= 2, 1, 0)
 
 
-def pack_kernel(embeddings_ref, sent_ref, gate_ref, full_out):
-    full_out[:BLOCK, :] = embeddings_ref[...].astype(jnp.bfloat16)
-    full_out[BLOCK:, :] = sent_ref[HALF:, :]
+def mask_rows(mask_ref):
+    lane = lax.broadcasted_iota(jnp.int32, (16, WIDTH), 1)
+    row = jnp.zeros((16, WIDTH), jnp.float32)
+    for offset in range(REACH):
+        row = jnp.where(lane == offset, mask_ref[0, offset].astype(jnp.float32), row)
+    return row.astype(jnp.bfloat16)
+
+
+def send_kernel(
+    mask_ref, embeddings_ref, main_out, rest_out, sent_out, full_out,
+    mask, rows, mask_arrived, rows_arrived,
+):
+    half = place()[2]
+    mask_copy = pltpu.make_async_copy(mask_ref, mask, mask_arrived)
+    mask_copy.start()
+    pieces = HALF // PIECE
+    copies = []
+    for part in range(2 * pieces):
+        which = half if part < pieces else 1 - half
+        first = pl.multiple_of(which * HALF + part % pieces * PIECE, PIECE)
+        source = embeddings_ref.at[pl.ds(first, PIECE), :]
+        copies.append((first, pltpu.make_async_copy(source, rows.at[part], rows_arrived.at[part])))
+        copies[-1][1].start()
+    for part, (place_in_block, copy) in enumerate(copies):
+        copy.wait()
+        first = part * PIECE
+        piece = rows[part].astype(jnp.bfloat16)
+        full_out[pl.ds(place_in_block, PIECE), :] = piece
+        if part < pieces:
+            sent_out[first : first + PIECE, :] = piece
+            if first < MAIN:
+                main_out[first : first + PIECE, :] = piece
+            else:
+                rest_out[first - MAIN : first - MAIN + PIECE, :] = piece
+    mask_copy.wait()
+    row = mask_rows(mask)
+    sent_out[HALF:, :] = row
+    main_out[MAIN:, :] = row
+    full_out[BLOCK:, :] = row
 
 
 def column_bias(reach, own_mask, mate_mask, other_mask, core):
@@ -117,15 +156,15 @@
     sum_out[...] = write_tiles((own_ref, mate_ref), bias, cols, own_out)
 
 
-def reach_kernel(
-    reaches, own_ref, mate_ref, reach_ref, sum_ref, tiles_out, sum_out, *turned_out
-):
+def reach_kernel(reaches, count, own_ref, mate_ref, *refs):
+    parts, (sum_ref, tiles_out, sum_out, *turned_out) = refs[:count], refs[count:]
     core, parity, _ = place()
     reach = jnp.where(parity == 0, reaches[0], reaches[1])
     masks = mask_row(own_ref), mask_row(mate_ref)
-    bias = column_bias(reach, *masks, mask_row(reach_ref), core)
-    rows = (own_ref, mate_ref)
-    total = sum_ref[...] + write_tiles(rows, bias, reach_ref[:HALF, :], tiles_out)
+    bias = column_bias(reach, *masks, mask_row(parts[0]), core)
+    cols = [parts[0][: parts[0].shape[0] - 16, :]] + [ref[...] for ref in parts[1:]]
+    cols = jnp.concatenate(cols) if count > 1 else cols[0]
+    total = sum_ref[...] + write_tiles((own_ref, mate_ref), bias, cols, tiles_out)
     sum_out[...] = total
     for out_ref in turned_out:
         out_ref[...] = jnp.concatenate([total[:, BLOCK:], total[:, :BLOCK]], axis=1)
@@ -244,22 +283,32 @@
 
     own_start = start_basis.T
     mate_start = swap_core(own_start)
-    rows = lax.dynamic_slice_in_dim(embeddings, half * HALF, HALF, 0).astype(bf16)
-    mask = jnp.pad(pair_mask.astype(bf16), ((HALF, 15), (0, WIDTH - REACH)))
-    sent = jnp.pad(rows, ((0, 16), (0, 0))) + mask
-    far = move(sent, FAR, -1)
-    (packed,) = call(
-        pack_kernel, [((BLOCK + 16, WIDTH), bf16)], (embeddings, sent, mate_start)
-    )
+    main, rest, sent, packed = call(
+        send_kernel,
+        [
+            ((count, WIDTH), bf16)
+            for count in (MAIN + 16, HALF - MAIN, HALF + 16, BLOCK + 16)
+        ],
+        (pair_mask, embeddings),
+        scratch=[
+            pltpu.SMEM((1, REACH), jnp.int32),
+            pltpu.VMEM((BLOCK // PIECE, PIECE, WIDTH), f32),
+            pltpu.SemaphoreType.DMA,
+            pltpu.SemaphoreType.DMA((BLOCK // PIECE,)),
+        ],
+        far_operands=2,
+    )
+    far = move(main, FAR, -1)
+    far_rest = move(rest, FAR, -1, 1)
+    near = move(sent, NEAR, -1)
     mate = swap_core(packed)
-    near = move(sent, NEAR, -1)
     tiles = [((wide, HALF), bf16), ((1, wide), f32), ((1, wide), f32)]
     own_weights, sums = call(
         own_kernel, [((wide, QUARTER), bf16), ((1, wide), f32)], (packed, mate)
     )
-    far_kernel = functools.partial(reach_kernel, FAR)
-    near_kernel = functools.partial(reach_kernel, NEAR)
-    far_weights, sums = call(far_kernel, tiles[:2], (packed, mate, far, sums))
+    far_kernel = functools.partial(reach_kernel, FAR, 2)
+    near_kernel = functools.partial(reach_kernel, NEAR, 1)
+    far_weights, sums = call(far_kernel, tiles[:2], (packed, mate, far, far_rest, sums))
     near_weights, sums, turned = call(near_kernel, tiles, (packed, mate, near, sums))
     sums = sums + swap_core(turned)
     plane_sums = [sums, *other_planes(sums)]
@@ -267,7 +316,7 @@
     terms = [((BASIS, HALF), f32), ((BASIS, HALF), f32), ((BASIS, QUARTER), f32)]
 
     def collect(far_term, near_term, own_term):
-        total = move(far_term, FAR, 1) + move(near_term, NEAR, 1)
+        total = move(near_term, NEAR, 1) + move(far_term, FAR, 1)
         blank = jnp.zeros_like(own_term)
         total = total + jnp.where(
             parity == 0,
@@ -293,12 +342,11 @@
     image, products = call(
         products_kernel, [((BASIS, BLOCK), f32), ((BASIS + 8, 128), f32)], (root, first, second)
     )
-    for group in ((8, 24, 16), (1, 2, 3)):
-        one, two, three = [other_chip(products, bits) for bits in group]
-        products = (products + one) + (two + three)
-    mate_products = swap_core(products)
-    one, two = other_chip(products, 7), other_chip(products, 7, 1)
-    products = (products + mate_products) + (one + two)
+    products = products + swap_core(products)
+    for group in ((16, 24, 8), (3, 2, 1)):
+        three, two, one = [other_chip(products, bits) for bits in group]
+        products = (three + two) + (one + products)
+    products = products + other_chip(products, 7)
     basis, projected = call(
         finish_kernel, [((BASIS, BLOCK), f32), ((BASIS, BASIS), f32)], (products, image)
     )

time: 101 us -> 101 us (level)
  waiting for transfers between devices: 45.3 us -> 34.3 us
  starting transfers between devices: 45.6 us -> 55 us
  Pallas kernels: 6.6 us -> 8.98 us
    ppermute x6 -> x7, starting transfers between devices: 15.4 us -> 29.4 us  [move(): return lax.ppermute(array, ALL_AXES, moves)]
    ppermute x6 -> x7, waiting for transfers between devices: 23.8 us -> 11 us  [move(): return lax.ppermute(array, ALL_AXES, moves)]
    ppermute x5, starting transfers between devices: 5.54 us -> 0.34 us  [swap_core(): return lax.ppermute(array, 'core', [(0, 1), (1, 0)])]
    pallas_call x8, Pallas kernels: 6.6 us -> 8.98 us  [call(): pl.pallas_call(kernel, out_shape=[jax.ShapeDtypeStruct(shape, dtype) for...]
    ppermute x9, waiting for transfers between devices: 10.5 us -> 11.8 us  [other_planes(): lax.ppermute(array, 'pairs', [(i, step(i)) for i in range(PAIRS)])]
    ppermute x5, waiting for transfers between devices: 2.5 us -> 3.69 us  [swap_core(): return lax.ppermute(array, 'core', [(0, 1), (1, 0)])]
    convert_element_type x1 -> x0, local copies, waits for them, and re-layouts: 1.14 us -> none  [on_device(): lax.dynamic_slice_in_dim(embeddings, half * HALF, HALF, 0).astype(bf16)]
    unnamed x4, local copies, waits for them, and re-layouts: 0.01 us -> 1.05 us
  transfers between devices with their start and end apart: 28 -> 28, of which waited for: 18 -> 19; matrix products, arithmetic and copies ran while one was open for 2% -> 0% of each run, Pallas kernels for 1% -> 2%
where the time goes in v5:
time: 101 us; the launch traced here: 100 us
  starting transfers between devices  55 us (54%)
  waiting for transfers between devices  34.3 us (34%)
  Pallas kernels  8.98 us (9%)
  local copies, waits for them, and re-layouts  1.05 us (1%)
    ppermute x7, starting transfers between devices, move(): return lax.ppermute(array, ALL_AXES, moves)  29.4 us
    ppermute x9, starting transfers between devices, other_planes(): lax.ppermute(array, 'pairs', [(i, step(i)) for i in range(PAIRS)])  14.5 us
    ppermute x9, waiting for transfers between devices, other_planes(): lax.ppermute(array, 'pairs', [(i, step(i)) for i in range(PAIRS)])  11.8 us
    ppermute x7, waiting for transfers between devices, move(): return lax.ppermute(array, ALL_AXES, moves)  11 us
    ppermute x7, starting transfers between devices, other_chip(): lax.ppermute(array, ('chip', 'core'), [(i, i ^ CORES * bits + core_bit) f...  10.8 us
    pallas_call x8, Pallas kernels, call(): pl.pallas_call(kernel, out_shape=[jax.ShapeDtypeStruct(shape, dtype) for...  8.98 us
    ppermute x7, waiting for transfers between devices, other_chip(): lax.ppermute(array, ('chip', 'core'), [(i, i ^ CORES * bits + core_bit) f...  7.85 us
    ppermute x5, waiting for transfers between devices, swap_core(): return lax.ppermute(array, 'core', [(0, 1), (1, 0)])  3.69 us
  transfers between devices with their start and end apart: 28, of which 19 were waited for; matrix products, arithmetic and copies ran while one was open for 0% of the time, Pallas kernels for 2%

profile of v5, /device:TPU:32, one launch (start us, length us, event | category | flops | bytes accessed | tf_op | source)
XLA Modules:
  0.0 100.3 jit_solution(10943838581203183383)
XLA Ops:
  0.6 2.4 %shard_map.50 = (bf16[208,512]{1,0:T(8,128)(2,1)}, bf16[64,512]{1,0:T(8,128)(2,1)}, bf16[272,512]{1,0:T(8,128)(2,1)}, bf16[528,512]{1,0:T(8,128)(2,1)}) custom-call(s32[1,5]{1,0:T(1,128)} %mask_ref.1, f32[512,512]{1,0:T(8,128)} %embeddings_ref.1), custom_call_target="tpu_custom_call" | custom-call | tf_op jit(solution)/shard_map/pallas_call | solution.py:269
  3.1 1.9 %collective-permute-start.1 = (bf16[272,512]{1,0:T(8,128)(2,1)}, bf16[272,512]{1,0:T(8,128)(2,1)S(1)}, u32[]{:S(2)}, u32[]{:S(2)}) collective-permute-start(bf16[272,512]{1,0:T(8,128)(2,1)} %get-tuple-element.25), channel_id=1, source_target_pairs={{0,248},{1,9},{2,10},{3,251},{4,252},{5,13},{6,14},{7,255},{8,0},{... | collective-permute-start | bytes 835592 | tf_op jit(solution)/shard_map/ppermute | solution.py:47
  6.6 7.7 %collective-permute-start.3 = (bf16[64,512]{1,0:T(8,128)(2,1)}, bf16[64,512]{1,0:T(8,128)(2,1)S(1)}, u32[]{:S(2)}, u32[]{:S(2)}) collective-permute-start(bf16[64,512]{1,0:T(8,128)(2,1)} %get-tuple-element.27), channel_id=1, source_target_pairs={{0,241},{1,16},{2,19},{3,242},{4,245},{5,20},{6,23},{7,246},{8,249... | collective-permute-start | bytes 196616 | tf_op jit(solution)/shard_map/ppermute | solution.py:47
  16.0 5.0 %collective-permute-done.3.refs_1_ = bf16[64,512]{1,0:T(8,128)(2,1)S(1)} collective-permute-done((bf16[64,512]{1,0:T(8,128)(2,1)}, bf16[64,512]{1,0:T(8,128)(2,1)S(1)}, u32[]{:S(2)}, u32[]{:S(2)}) %collective-permute-start.3) | collective-permute-done | bytes 65568 | tf_op jit(solution)/shard_map/ppermute | solution.py:47
  23.8 2.2 %collective-permute-start.6 = (f32[1,1024]{1,0:T(1,128)S(1)}, f32[1,1024]{1,0:T(1,128)S(1)}, u32[]{:S(2)}, u32[]{:S(2)}) collective-permute-start(f32[1,1024]{1,0:T(1,128)S(1)} %add.59.sum_ref), channel_id=1, source_target_pairs={{0,3},{1,2},{2,1},{3,0},{4,7},{5,6},{6,5},{7,4},{8,11},{9,10},{10,... | collective-permute-start | bytes 12296 | tf_op jit(solution)/shard_map/ppermute | solution.py:63
  26.0 1.9 %collective-permute-start.7 = (f32[1,1024]{1,0:T(1,128)S(1)}, f32[1,1024]{1,0:T(1,128)S(1)}, u32[]{:S(2)}, u32[]{:S(2)}) collective-permute-start(f32[1,1024]{1,0:T(1,128)S(1)} %add.59.sum_ref), channel_id=1, source_target_pairs={{0,2},{1,3},{2,0},{3,1},{4,6},{5,7},{6,4},{7,5},{8,10},{9,11},{10,... | collective-permute-start | bytes 12296 | tf_op jit(solution)/shard_map/ppermute | solution.py:63
  28.7 2.4 %collective-permute-done.7.both_ref = f32[1,1024]{1,0:T(1,128)S(1)} collective-permute-done((f32[1,1024]{1,0:T(1,128)S(1)}, f32[1,1024]{1,0:T(1,128)S(1)}, u32[]{:S(2)}, u32[]{:S(2)}) %collective-permute-start.7) | collective-permute-done | bytes 4128 | tf_op jit(solution)/shard_map/ppermute | solution.py:63
  31.4 5.1 %collective-permute-start.10 = (f32[64,256]{1,0:T(8,128)S(1)}, f32[64,256]{1,0:T(8,128)S(1)}, u32[]{:S(2)}, u32[]{:S(2)}) collective-permute-start(f32[64,256]{1,0:T(8,128)S(1)} %get-tuple-element.37), channel_id=1, source_target_pairs={{0,240},{1,17},{2,18},{3,243},{4,244},{5,21},{6,22},{7,247},{8,248... | collective-permute-start | bytes 196616 | tf_op jit(solution)/shard_map/ppermute | solution.py:47
  36.6 2.8 %collective-permute-start.9 = (f32[64,256]{1,0:T(8,128)S(1)}, f32[64,256]{1,0:T(8,128)S(1)}, u32[]{:S(2)}, u32[]{:S(2)}) collective-permute-start(f32[64,256]{1,0:T(8,128)S(1)} %get-tuple-element.36), channel_id=1, source_target_pairs={{0,8},{1,249},{2,250},{3,11},{4,12},{5,253},{6,254},{7,15},{8,16},... | collective-permute-start | bytes 196616 | tf_op jit(solution)/shard_map/ppermute | solution.py:47
  39.4 4.0 %collective-permute-done.9 = f32[64,256]{1,0:T(8,128)S(1)} collective-permute-done((f32[64,256]{1,0:T(8,128)S(1)}, f32[64,256]{1,0:T(8,128)S(1)}, u32[]{:S(2)}, u32[]{:S(2)}) %collective-permute-start.9) | collective-permute-done | bytes 65568 | tf_op jit(solution)/shard_map/ppermute | solution.py:47
  44.6 2.9 %collective-permute-start.13 = (f32[64,256]{1,0:T(8,128)S(1)}, f32[64,256]{1,0:T(8,128)S(1)}, u32[]{:S(2)}, u32[]{:S(2)}) collective-permute-start(f32[64,256]{1,0:T(8,128)S(1)} %select_add_fusion.1), channel_id=1, source_target_pairs={{0,2},{1,3},{2,0},{3,1},{4,6},{5,7},{6,4},{7,5},{8,10},{9,11},{10,... | collective-permute-start | bytes 196616 | tf_op jit(solution)/shard_map/ppermute | solution.py:63
  52.6 10.1 %collective-permute-start.16 = (f32[64,256]{1,0:T(8,128)S(1)}, f32[64,256]{1,0:T(8,128)S(1)}, u32[]{:S(2)}, u32[]{:S(2)}) collective-permute-start(f32[64,256]{1,0:T(8,128)S(1)} %get-tuple-element.40), channel_id=1, source_target_pairs={{0,240},{1,17},{2,18},{3,243},{4,244},{5,21},{6,22},{7,247},{8,248... | collective-permute-start | bytes 196616 | tf_op jit(solution)/shard_map/ppermute | solution.py:47
  62.7 1.9 %collective-permute-done.16 = f32[64,256]{1,0:T(8,128)S(1)} collective-permute-done((f32[64,256]{1,0:T(8,128)S(1)}, f32[64,256]{1,0:T(8,128)S(1)}, u32[]{:S(2)}, u32[]{:S(2)}) %collective-permute-start.16) | collective-permute-done | bytes 65568 | tf_op jit(solution)/shard_map/ppermute | solution.py:47
  64.6 4.0 %collective-permute-start.17 = (f32[64,256]{1,0:T(8,128)S(1)}, f32[64,256]{1,0:T(8,128)S(1)}, u32[]{:S(2)}, u32[]{:S(2)}) collective-permute-start(f32[64,256]{1,0:T(8,128)S(1)} %select_add_fusion), channel_id=1, source_target_pairs={{0,1},{1,0},{2,3},{3,2},{4,5},{5,4},{6,7},{7,6},{8,9},{9,8},{10,11... | collective-permute-start | bytes 196616 | tf_op jit(solution)/shard_map/ppermute | solution.py:63
  68.6 2.2 %collective-permute-start.18 = (f32[64,256]{1,0:T(8,128)S(1)}, f32[64,256]{1,0:T(8,128)S(1)}, u32[]{:S(2)}, u32[]{:S(2)}) collective-permute-start(f32[64,256]{1,0:T(8,128)S(1)} %select_add_fusion), channel_id=1, source_target_pairs={{0,3},{1,2},{2,1},{3,0},{4,7},{5,6},{6,5},{7,4},{8,11},{9,10},{10,... | collective-permute-start | bytes 196616 | tf_op jit(solution)/shard_map/ppermute | solution.py:63
  70.9 3.2 %collective-permute-done.18 = f32[64,256]{1,0:T(8,128)S(1)} collective-permute-done((f32[64,256]{1,0:T(8,128)S(1)}, f32[64,256]{1,0:T(8,128)S(1)}, u32[]{:S(2)}, u32[]{:S(2)}) %collective-permute-start.18) | collective-permute-done | bytes 65568 | tf_op jit(solution)/shard_map/ppermute | solution.py:63
  74.1 2.5 %collective-permute-done.19 = f32[64,256]{1,0:T(8,128)S(1)} collective-permute-done((f32[64,256]{1,0:T(8,128)S(1)}, f32[64,256]{1,0:T(8,128)S(1)}, u32[]{:S(2)}, u32[]{:S(2)}) %collective-permute-start.19) | collective-permute-done | bytes 65568 | tf_op jit(solution)/shard_map/ppermute | solution.py:63
  78.5 3.4 %collective-permute-start.23 = (f32[72,128]{1,0:T(8,128)S(1)}, f32[72,128]{1,0:T(8,128)S(1)}, u32[]{:S(2)}, u32[]{:S(2)}) collective-permute-start(f32[72,128]{1,0:T(8,128)S(1)} %add.68), channel_id=1, source_target_pairs={{0,64},{4,68},{8,72},{12,76},{16,80},{20,84},{24,88},{28,92},{32,9... | collective-permute-start | bytes 110600 | tf_op jit(solution)/shard_map/ppermute | solution.py:56
  81.9 2.2 %collective-permute-done.21 = f32[72,128]{1,0:T(8,128)S(1)} collective-permute-done((f32[72,128]{1,0:T(8,128)S(1)}, f32[72,128]{1,0:T(8,128)S(1)}, u32[]{:S(2)}, u32[]{:S(2)}) %collective-permute-start.21) | collective-permute-done | bytes 36896 | tf_op jit(solution)/shard_map/ppermute | solution.py:56
  84.2 1.6 %collective-permute-start.25 = (f32[72,128]{1,0:T(8,128)S(1)}, f32[72,128]{1,0:T(8,128)S(1)}, u32[]{:S(2)}, u32[]{:S(2)}) collective-permute-start(f32[72,128]{1,0:T(8,128)S(1)} %add_add_fusion.1), channel_id=1, source_target_pairs={{0,16},{4,20},{8,24},{12,28},{16,0},{20,4},{24,8},{28,12},{32,48},... | collective-permute-start | bytes 110600 | tf_op jit(solution)/shard_map/ppermute | solution.py:56
  85.8 1.8 %collective-permute-start.26 = (f32[72,128]{1,0:T(8,128)S(1)}, f32[72,128]{1,0:T(8,128)S(1)}, u32[]{:S(2)}, u32[]{:S(2)}) collective-permute-start(f32[72,128]{1,0:T(8,128)S(1)} %add_add_fusion.1), channel_id=1, source_target_pairs={{0,8},{4,12},{8,0},{12,4},{16,24},{20,28},{24,16},{28,20},{32,40},... | collective-permute-start | bytes 110600 | tf_op jit(solution)/shard_map/ppermute | solution.py:56
  90.0 3.7 %collective-permute-start.27 = (f32[72,128]{1,0:T(8,128)S(1)}, f32[72,128]{1,0:T(8,128)S(1)}, u32[]{:S(2)}, u32[]{:S(2)}) collective-permute-start(f32[72,128]{1,0:T(8,128)S(1)} %add_add_fusion), channel_id=1, source_target_pairs={{0,56},{4,60},{8,48},{12,52},{16,40},{20,44},{24,32},{28,36},{32,2... | collective-permute-start | bytes 110600 | tf_op jit(solution)/shard_map/ppermute | solution.py:56
  93.7 3.3 %collective-permute-done.27 = f32[72,128]{1,0:T(8,128)S(1)} collective-permute-done((f32[72,128]{1,0:T(8,128)S(1)}, f32[72,128]{1,0:T(8,128)S(1)}, u32[]{:S(2)}, u32[]{:S(2)}) %collective-permute-start.27) | collective-permute-done | bytes 36896 | tf_op jit(solution)/shard_map/ppermute | solution.py:56
  97.0 3.2 %shard_map.57 = (f32[64,512]{1,0:T(8,128)}, f32[64,64]{1,0:T(8,128)}) custom-call(f32[72,128]{1,0:T(8,128)S(1)} %add.75.products_ref, f32[64,512]{1,0:T(8,128)S(1)} %get-tuple-element.43.image_ref), custom_call_target="tpu_custom_call" | custom-call | tf_op jit(solution)/shard_map/pallas_call | solution.py:269
  (57 shorter events, 17.8 us)
Async XLA Ops:
  3.0 11.3 %collective-permute-start = (bf16[528,512]{1,0:T(8,128)(2,1)}, bf16[528,512]{1,0:T(8,128)(2,1)S(1)}, u32[]{:S(2)}, u32[]{:S(2)}) collective-permute-start(bf16[528,512]{1,0:T(8,128)(2,1)} %get-tuple-element.24.own_ref), channel_id=1, source_target_pairs={{0,4},{4,0},{1,5},{5,1},{2,6},{6,2},{3,7},{7,3},{8,12},{12,8},{9,1... | collective-permute-start | bytes 1622024 | tf_op jit(solution)/shard_map/ppermute | solution.py:51
  3.1 18.6 %collective-permute-start.1 = (bf16[272,512]{1,0:T(8,128)(2,1)}, bf16[272,512]{1,0:T(8,128)(2,1)S(1)}, u32[]{:S(2)}, u32[]{:S(2)}) collective-permute-start(bf16[272,512]{1,0:T(8,128)(2,1)} %get-tuple-element.25), channel_id=1, source_target_pairs={{0,248},{1,9},{2,10},{3,251},{4,252},{5,13},{6,14},{7,255},{8,0},{... | collective-permute-start | bytes 835592 | tf_op jit(solution)/shard_map/ppermute | solution.py:47
  5.1 16.0 %collective-permute-start.2 = (bf16[208,512]{1,0:T(8,128)(2,1)}, bf16[208,512]{1,0:T(8,128)(2,1)S(1)}, u32[]{:S(2)}, u32[]{:S(2)}) collective-permute-start(bf16[208,512]{1,0:T(8,128)(2,1)} %get-tuple-element.26), channel_id=1, source_target_pairs={{0,16},{1,241},{2,242},{3,19},{4,20},{5,245},{6,246},{7,23},{8,24}... | collective-permute-start | bytes 638984 | tf_op jit(solution)/shard_map/ppermute | solution.py:47
  6.6 21.3 %collective-permute-start.8 = (f32[64,512]{1,0:T(8,128)S(1)}, f32[64,512]{1,0:T(8,128)S(1)}, u32[]{:S(2)}, u32[]{:S(2)}) collective-permute-start(f32[64,512]{1,0:T(8,128)S(1)} %bitcast.2), channel_id=1, source_target_pairs={{0,4},{4,0},{1,5},{5,1},{2,6},{6,2},{3,7},{7,3},{8,12},{12,8},{9,1... | collective-permute-start | bytes 393224 | tf_op jit(solution)/shard_map/ppermute | solution.py:51
  6.6 14.4 %collective-permute-start.3 = (bf16[64,512]{1,0:T(8,128)(2,1)}, bf16[64,512]{1,0:T(8,128)(2,1)S(1)}, u32[]{:S(2)}, u32[]{:S(2)}) collective-permute-start(bf16[64,512]{1,0:T(8,128)(2,1)} %get-tuple-element.27), channel_id=1, source_target_pairs={{0,241},{1,16},{2,19},{3,242},{4,245},{5,20},{6,23},{7,246},{8,249... | collective-permute-start | bytes 196616 | tf_op jit(solution)/shard_map/ppermute | solution.py:47
  23.8 4.9 %collective-permute-start.6 = (f32[1,1024]{1,0:T(1,128)S(1)}, f32[1,1024]{1,0:T(1,128)S(1)}, u32[]{:S(2)}, u32[]{:S(2)}) collective-permute-start(f32[1,1024]{1,0:T(1,128)S(1)} %add.59.sum_ref), channel_id=1, source_target_pairs={{0,3},{1,2},{2,1},{3,0},{4,7},{5,6},{6,5},{7,4},{8,11},{9,10},{10,... | collective-permute-start | bytes 12296 | tf_op jit(solution)/shard_map/ppermute | solution.py:63
  26.0 5.1 %collective-permute-start.7 = (f32[1,1024]{1,0:T(1,128)S(1)}, f32[1,1024]{1,0:T(1,128)S(1)}, u32[]{:S(2)}, u32[]{:S(2)}) collective-permute-start(f32[1,1024]{1,0:T(1,128)S(1)} %add.59.sum_ref), channel_id=1, source_target_pairs={{0,2},{1,3},{2,0},{3,1},{4,6},{5,7},{6,4},{7,5},{8,10},{9,11},{10,... | collective-permute-start | bytes 12296 | tf_op jit(solution)/shard_map/ppermute | solution.py:63
  31.4 7.9 %collective-permute-start.10 = (f32[64,256]{1,0:T(8,128)S(1)}, f32[64,256]{1,0:T(8,128)S(1)}, u32[]{:S(2)}, u32[]{:S(2)}) collective-permute-start(f32[64,256]{1,0:T(8,128)S(1)} %get-tuple-element.37), channel_id=1, source_target_pairs={{0,240},{1,17},{2,18},{3,243},{4,244},{5,21},{6,22},{7,247},{8,248... | collective-permute-start | bytes 196616 | tf_op jit(solution)/shard_map/ppermute | solution.py:47
  36.6 6.8 %collective-permute-start.9 = (f32[64,256]{1,0:T(8,128)S(1)}, f32[64,256]{1,0:T(8,128)S(1)}, u32[]{:S(2)}, u32[]{:S(2)}) collective-permute-start(f32[64,256]{1,0:T(8,128)S(1)} %get-tuple-element.36), channel_id=1, source_target_pairs={{0,8},{1,249},{2,250},{3,11},{4,12},{5,253},{6,254},{7,15},{8,16},... | collective-permute-start | bytes 196616 | tf_op jit(solution)/shard_map/ppermute | solution.py:47
  43.4 4.4 %collective-permute-start.11 = (f32[64,256]{1,0:T(8,128)S(1)}, f32[64,256]{1,0:T(8,128)S(1)}, u32[]{:S(2)}, u32[]{:S(2)}) collective-permute-start(f32[64,256]{1,0:T(8,128)S(1)} %select_add_fusion.1), channel_id=1, source_target_pairs={{0,1},{1,0},{2,3},{3,2},{4,5},{5,4},{6,7},{7,6},{8,9},{9,8},{10,11... | collective-permute-start | bytes 196616 | tf_op jit(solution)/shard_map/ppermute | solution.py:63
  43.5 5.6 %collective-permute-start.12 = (f32[64,256]{1,0:T(8,128)S(1)}, f32[64,256]{1,0:T(8,128)S(1)}, u32[]{:S(2)}, u32[]{:S(2)}) collective-permute-start(f32[64,256]{1,0:T(8,128)S(1)} %select_add_fusion.1), channel_id=1, source_target_pairs={{0,3},{1,2},{2,1},{3,0},{4,7},{5,6},{6,5},{7,4},{8,11},{9,10},{10,... | collective-permute-start | bytes 196616 | tf_op jit(solution)/shard_map/ppermute | solution.py:63
  44.6 5.8 %collective-permute-start.13 = (f32[64,256]{1,0:T(8,128)S(1)}, f32[64,256]{1,0:T(8,128)S(1)}, u32[]{:S(2)}, u32[]{:S(2)}) collective-permute-start(f32[64,256]{1,0:T(8,128)S(1)} %select_add_fusion.1), channel_id=1, source_target_pairs={{0,2},{1,3},{2,0},{3,1},{4,6},{5,7},{6,4},{7,5},{8,10},{9,11},{10,... | collective-permute-start | bytes 196616 | tf_op jit(solution)/shard_map/ppermute | solution.py:63
  52.3 10.4 %collective-permute-start.15 = (f32[64,256]{1,0:T(8,128)S(1)}, f32[64,256]{1,0:T(8,128)S(1)}, u32[]{:S(2)}, u32[]{:S(2)}) collective-permute-start(f32[64,256]{1,0:T(8,128)S(1)} %get-tuple-element.39), channel_id=1, source_target_pairs={{0,8},{1,249},{2,250},{3,11},{4,12},{5,253},{6,254},{7,15},{8,16},... | collective-permute-start | bytes 196616 | tf_op jit(solution)/shard_map/ppermute | solution.py:47
  52.6 12.0 %collective-permute-start.16 = (f32[64,256]{1,0:T(8,128)S(1)}, f32[64,256]{1,0:T(8,128)S(1)}, u32[]{:S(2)}, u32[]{:S(2)}) collective-permute-start(f32[64,256]{1,0:T(8,128)S(1)} %get-tuple-element.40), channel_id=1, source_target_pairs={{0,240},{1,17},{2,18},{3,243},{4,244},{5,21},{6,22},{7,247},{8,248... | collective-permute-start | bytes 196616 | tf_op jit(solution)/shard_map/ppermute | solution.py:47
  64.6 6.3 %collective-permute-start.17 = (f32[64,256]{1,0:T(8,128)S(1)}, f32[64,256]{1,0:T(8,128)S(1)}, u32[]{:S(2)}, u32[]{:S(2)}) collective-permute-start(f32[64,256]{1,0:T(8,128)S(1)} %select_add_fusion), channel_id=1, source_target_pairs={{0,1},{1,0},{2,3},{3,2},{4,5},{5,4},{6,7},{7,6},{8,9},{9,8},{10,11... | collective-permute-start | bytes 196616 | tf_op jit(solution)/shard_map/ppermute | solution.py:63
  68.6 5.5 %collective-permute-start.18 = (f32[64,256]{1,0:T(8,128)S(1)}, f32[64,256]{1,0:T(8,128)S(1)}, u32[]{:S(2)}, u32[]{:S(2)}) collective-permute-start(f32[64,256]{1,0:T(8,128)S(1)} %select_add_fusion), channel_id=1, source_target_pairs={{0,3},{1,2},{2,1},{3,0},{4,7},{5,6},{6,5},{7,4},{8,11},{9,10},{10,... | collective-permute-start | bytes 196616 | tf_op jit(solution)/shard_map/ppermute | solution.py:63
  70.8 5.8 %collective-permute-start.19 = (f32[64,256]{1,0:T(8,128)S(1)}, f32[64,256]{1,0:T(8,128)S(1)}, u32[]{:S(2)}, u32[]{:S(2)}) collective-permute-start(f32[64,256]{1,0:T(8,128)S(1)} %select_add_fusion), channel_id=1, source_target_pairs={{0,2},{1,3},{2,0},{3,1},{4,6},{5,7},{6,4},{7,5},{8,10},{9,11},{10,... | collective-permute-start | bytes 196616 | tf_op jit(solution)/shard_map/ppermute | solution.py:63
  78.4 5.7 %collective-permute-start.21 = (f32[72,128]{1,0:T(8,128)S(1)}, f32[72,128]{1,0:T(8,128)S(1)}, u32[]{:S(2)}, u32[]{:S(2)}) collective-permute-start(f32[72,128]{1,0:T(8,128)S(1)} %add.68), channel_id=1, source_target_pairs={{0,128},{4,132},{8,136},{12,140},{16,144},{20,148},{24,152},{28,15... | collective-permute-start | bytes 110600 | tf_op jit(solution)/shard_map/ppermute | solution.py:56
  78.4 5.7 %collective-permute-start.22 = (f32[72,128]{1,0:T(8,128)S(1)}, f32[72,128]{1,0:T(8,128)S(1)}, u32[]{:S(2)}, u32[]{:S(2)}) collective-permute-start(f32[72,128]{1,0:T(8,128)S(1)} %add.68), channel_id=1, source_target_pairs={{0,192},{4,196},{8,200},{12,204},{16,208},{20,212},{24,216},{28,22... | collective-permute-start | bytes 110600 | tf_op jit(solution)/shard_map/ppermute | solution.py:56
  78.5 5.6 %collective-permute-start.23 = (f32[72,128]{1,0:T(8,128)S(1)}, f32[72,128]{1,0:T(8,128)S(1)}, u32[]{:S(2)}, u32[]{:S(2)}) collective-permute-start(f32[72,128]{1,0:T(8,128)S(1)} %add.68), channel_id=1, source_target_pairs={{0,64},{4,68},{8,72},{12,76},{16,80},{20,84},{24,88},{28,92},{32,9... | collective-permute-start | bytes 110600 | tf_op jit(solution)/shard_map/ppermute | solution.py:56
  84.1 4.2 %collective-permute-start.24 = (f32[72,128]{1,0:T(8,128)S(1)}, f32[72,128]{1,0:T(8,128)S(1)}, u32[]{:S(2)}, u32[]{:S(2)}) collective-permute-start(f32[72,128]{1,0:T(8,128)S(1)} %add_add_fusion.1), channel_id=1, source_target_pairs={{0,24},{4,28},{8,16},{12,20},{16,8},{20,12},{24,0},{28,4},{32,56},... | collective-permute-start | bytes 110600 | tf_op jit(solution)/shard_map/ppermute | solution.py:56
  84.2 4.9 %collective-permute-start.25 = (f32[72,128]{1,0:T(8,128)S(1)}, f32[72,128]{1,0:T(8,128)S(1)}, u32[]{:S(2)}, u32[]{:S(2)}) collective-permute-start(f32[72,128]{1,0:T(8,128)S(1)} %add_add_fusion.1), channel_id=1, source_target_pairs={{0,16},{4,20},{8,24},{12,28},{16,0},{20,4},{24,8},{28,12},{32,48},... | collective-permute-start | bytes 110600 | tf_op jit(solution)/shard_map/ppermute | solution.py:56
  85.8 4.2 %collective-permute-start.26 = (f32[72,128]{1,0:T(8,128)S(1)}, f32[72,128]{1,0:T(8,128)S(1)}, u32[]{:S(2)}, u32[]{:S(2)}) collective-permute-start(f32[72,128]{1,0:T(8,128)S(1)} %add_add_fusion.1), channel_id=1, source_target_pairs={{0,8},{4,12},{8,0},{12,4},{16,24},{20,28},{24,16},{28,20},{32,40},... | collective-permute-start | bytes 110600 | tf_op jit(solution)/shard_map/ppermute | solution.py:56
  90.0 7.1 %collective-permute-start.27 = (f32[72,128]{1,0:T(8,128)S(1)}, f32[72,128]{1,0:T(8,128)S(1)}, u32[]{:S(2)}, u32[]{:S(2)}) collective-permute-start(f32[72,128]{1,0:T(8,128)S(1)} %add_add_fusion), channel_id=1, source_target_pairs={{0,56},{4,60},{8,48},{12,52},{16,40},{20,44},{24,32},{28,36},{32,2... | collective-permute-start | bytes 110600 | tf_op jit(solution)/shard_map/ppermute | solution.py:56
  (6 other events, 15.1 us)

commit v6 on v5

--- a/solution.py
+++ b/solution.py
@@ -1,4 +1,3 @@
-import functools
 import math
 
 import jax
@@ -17,7 +16,7 @@
 DOCS = 32768
 REACH = 5
 CHUNK = 256
-STEP = 8
+STEP = 16
 PIECE = 64
 MAIN = 192
 EXPONENT = -math.log(BLOCK / 4) / (2 * WIDTH) * math.log2(math.e)
@@ -156,18 +155,21 @@
     sum_out[...] = write_tiles((own_ref, mate_ref), bias, cols, own_out)
 
 
-def reach_kernel(reaches, count, own_ref, mate_ref, *refs):
-    parts, (sum_ref, tiles_out, sum_out, *turned_out) = refs[:count], refs[count:]
+def reach_kernel(
+    own_ref, mate_ref, main_ref, rest_ref, near_ref, sum_ref, far_out, near_out, sum_out, turned_out
+):
     core, parity, _ = place()
-    reach = jnp.where(parity == 0, reaches[0], reaches[1])
     masks = mask_row(own_ref), mask_row(mate_ref)
-    bias = column_bias(reach, *masks, mask_row(parts[0]), core)
-    cols = [parts[0][: parts[0].shape[0] - 16, :]] + [ref[...] for ref in parts[1:]]
-    cols = jnp.concatenate(cols) if count > 1 else cols[0]
-    total = sum_ref[...] + write_tiles((own_ref, mate_ref), bias, cols, tiles_out)
+    rows = (own_ref, mate_ref)
+    reach = jnp.where(parity == 0, NEAR[0], NEAR[1])
+    bias = column_bias(reach, *masks, mask_row(near_ref), core)
+    total = sum_ref[...] + write_tiles(rows, bias, near_ref[:HALF, :], near_out)
+    reach = jnp.where(parity == 0, FAR[0], FAR[1])
+    bias = column_bias(reach, *masks, mask_row(main_ref), core)
+    cols = jnp.concatenate([main_ref[:MAIN, :], rest_ref[...]])
+    total = total + write_tiles(rows, bias, cols, far_out)
     sum_out[...] = total
-    for out_ref in turned_out:
-        out_ref[...] = jnp.concatenate([total[:, BLOCK:], total[:, :BLOCK]], axis=1)
+    turned_out[...] = jnp.concatenate([total[:, BLOCK:], total[:, :BLOCK]], axis=1)
 
 
 def multiply(vectors, far_ref, near_ref, own_ref, far_out, near_out, own_out):
@@ -302,14 +304,15 @@
     far_rest = move(rest, FAR, -1, 1)
     near = move(sent, NEAR, -1)
     mate = swap_core(packed)
-    tiles = [((wide, HALF), bf16), ((1, wide), f32), ((1, wide), f32)]
     own_weights, sums = call(
         own_kernel, [((wide, QUARTER), bf16), ((1, wide), f32)], (packed, mate)
     )
-    far_kernel = functools.partial(reach_kernel, FAR, 2)
-    near_kernel = functools.partial(reach_kernel, NEAR, 1)
-    far_weights, sums = call(far_kernel, tiles[:2], (packed, mate, far, far_rest, sums))
-    near_weights, sums, turned = call(near_kernel, tiles, (packed, mate, near, sums))
+    tiles = ((wide, HALF), bf16)
+    far_weights, near_weights, sums, turned = call(
+        reach_kernel,
+        [tiles, tiles, ((1, wide), f32), ((1, wide), f32)],
+        (packed, mate, far, far_rest, near, sums),
+    )
     sums = sums + swap_core(turned)
     plane_sums = [sums, *other_planes(sums)]
     weights = (far_weights, near_weights, own_weights)

time: 101 us -> 100 us (0.990)
    pallas_call x8 -> x7, Pallas kernels: 8.98 us -> 8.44 us  [call(): pl.pallas_call(kernel, out_shape=[jax.ShapeDtypeStruct(shape, dtype) for...]
where the time goes in v6:
time: 100 us; the launch traced here: 99.7 us
  starting transfers between devices  55 us (55%)
  waiting for transfers between devices  34.3 us (34%)
  Pallas kernels  8.44 us (8%)
  local copies, waits for them, and re-layouts  1.05 us (1%)
    ppermute x7, starting transfers between devices, move(): return lax.ppermute(array, ALL_AXES, moves)  29.4 us
    ppermute x9, starting transfers between devices, other_planes(): lax.ppermute(array, 'pairs', [(i, step(i)) for i in range(PAIRS)])  14.4 us
    ppermute x9, waiting for transfers between devices, other_planes(): lax.ppermute(array, 'pairs', [(i, step(i)) for i in range(PAIRS)])  11.8 us
    ppermute x7, waiting for transfers between devices, move(): return lax.ppermute(array, ALL_AXES, moves)  11 us
    ppermute x7, starting transfers between devices, other_chip(): lax.ppermute(array, ('chip', 'core'), [(i, i ^ CORES * bits + core_bit) f...  10.8 us
    pallas_call x7, Pallas kernels, call(): pl.pallas_call(kernel, out_shape=[jax.ShapeDtypeStruct(shape, dtype) for...  8.44 us
    ppermute x7, waiting for transfers between devices, other_chip(): lax.ppermute(array, ('chip', 'core'), [(i, i ^ CORES * bits + core_bit) f...  7.85 us
    ppermute x5, waiting for transfers between devices, swap_core(): return lax.ppermute(array, 'core', [(0, 1), (1, 0)])  3.69 us
  transfers between devices with their start and end apart: 28, of which 19 were waited for; matrix products, arithmetic and copies ran while one was open for 0% of the time, Pallas kernels for 2%

profile of v6, /device:TPU:32, one launch (start us, length us, event | category | flops | bytes accessed | tf_op | source)
XLA Modules:
  0.0 99.7 jit_solution(4679773858937194312)
XLA Ops:
  0.6 2.4 %shard_map.50 = (bf16[208,512]{1,0:T(8,128)(2,1)}, bf16[64,512]{1,0:T(8,128)(2,1)}, bf16[272,512]{1,0:T(8,128)(2,1)}, bf16[528,512]{1,0:T(8,128)(2,1)}) custom-call(s32[1,5]{1,0:T(1,128)} %mask_ref.1, f32[512,512]{1,0:T(8,128)} %embeddings_ref.1), custom_call_target="tpu_custom_call" | custom-call | tf_op jit(solution)/shard_map/pallas_call | solution.py:271
  3.1 1.9 %collective-permute-start.3 = (bf16[272,512]{1,0:T(8,128)(2,1)}, bf16[272,512]{1,0:T(8,128)(2,1)S(1)}, u32[]{:S(2)}, u32[]{:S(2)}) collective-permute-start(bf16[272,512]{1,0:T(8,128)(2,1)} %get-tuple-element.26), channel_id=1, source_target_pairs={{0,248},{1,9},{2,10},{3,251},{4,252},{5,13},{6,14},{7,255},{8,0},{... | collective-permute-start | bytes 835592 | tf_op jit(solution)/shard_map/ppermute | solution.py:46
  6.6 7.7 %collective-permute-start.2 = (bf16[64,512]{1,0:T(8,128)(2,1)}, bf16[64,512]{1,0:T(8,128)(2,1)S(1)}, u32[]{:S(2)}, u32[]{:S(2)}) collective-permute-start(bf16[64,512]{1,0:T(8,128)(2,1)} %get-tuple-element.25), channel_id=1, source_target_pairs={{0,241},{1,16},{2,19},{3,242},{4,245},{5,20},{6,23},{7,246},{8,249... | collective-permute-start | bytes 196616 | tf_op jit(solution)/shard_map/ppermute | solution.py:46
  16.0 5.1 %collective-permute-done.2.rest_ref = bf16[64,512]{1,0:T(8,128)(2,1)S(1)} collective-permute-done((bf16[64,512]{1,0:T(8,128)(2,1)}, bf16[64,512]{1,0:T(8,128)(2,1)S(1)}, u32[]{:S(2)}, u32[]{:S(2)}) %collective-permute-start.2) | collective-permute-done | bytes 65568 | tf_op jit(solution)/shard_map/ppermute | solution.py:46
  23.7 2.2 %collective-permute-start.6 = (f32[1,1024]{1,0:T(1,128)S(1)}, f32[1,1024]{1,0:T(1,128)S(1)}, u32[]{:S(2)}, u32[]{:S(2)}) collective-permute-start(f32[1,1024]{1,0:T(1,128)S(1)} %add.59.sum_ref), channel_id=1, source_target_pairs={{0,3},{1,2},{2,1},{3,0},{4,7},{5,6},{6,5},{7,4},{8,11},{9,10},{10,... | collective-permute-start | bytes 12296 | tf_op jit(solution)/shard_map/ppermute | solution.py:62
  25.8 1.9 %collective-permute-start.7 = (f32[1,1024]{1,0:T(1,128)S(1)}, f32[1,1024]{1,0:T(1,128)S(1)}, u32[]{:S(2)}, u32[]{:S(2)}) collective-permute-start(f32[1,1024]{1,0:T(1,128)S(1)} %add.59.sum_ref), channel_id=1, source_target_pairs={{0,2},{1,3},{2,0},{3,1},{4,6},{5,7},{6,4},{7,5},{8,10},{9,11},{10,... | collective-permute-start | bytes 12296 | tf_op jit(solution)/shard_map/ppermute | solution.py:62
  28.6 2.4 %collective-permute-done.7.both_ref = f32[1,1024]{1,0:T(1,128)S(1)} collective-permute-done((f32[1,1024]{1,0:T(1,128)S(1)}, f32[1,1024]{1,0:T(1,128)S(1)}, u32[]{:S(2)}, u32[]{:S(2)}) %collective-permute-start.7) | collective-permute-done | bytes 4128 | tf_op jit(solution)/shard_map/ppermute | solution.py:62
  31.3 5.2 %collective-permute-start.10 = (f32[64,256]{1,0:T(8,128)S(1)}, f32[64,256]{1,0:T(8,128)S(1)}, u32[]{:S(2)}, u32[]{:S(2)}) collective-permute-start(f32[64,256]{1,0:T(8,128)S(1)} %get-tuple-element.35), channel_id=1, source_target_pairs={{0,240},{1,17},{2,18},{3,243},{4,244},{5,21},{6,22},{7,247},{8,248... | collective-permute-start | bytes 196616 | tf_op jit(solution)/shard_map/ppermute | solution.py:46
  36.5 2.8 %collective-permute-start.9 = (f32[64,256]{1,0:T(8,128)S(1)}, f32[64,256]{1,0:T(8,128)S(1)}, u32[]{:S(2)}, u32[]{:S(2)}) collective-permute-start(f32[64,256]{1,0:T(8,128)S(1)} %get-tuple-element.34), channel_id=1, source_target_pairs={{0,8},{1,249},{2,250},{3,11},{4,12},{5,253},{6,254},{7,15},{8,16},... | collective-permute-start | bytes 196616 | tf_op jit(solution)/shard_map/ppermute | solution.py:46
  39.3 4.0 %collective-permute-done.9 = f32[64,256]{1,0:T(8,128)S(1)} collective-permute-done((f32[64,256]{1,0:T(8,128)S(1)}, f32[64,256]{1,0:T(8,128)S(1)}, u32[]{:S(2)}, u32[]{:S(2)}) %collective-permute-start.9) | collective-permute-done | bytes 65568 | tf_op jit(solution)/shard_map/ppermute | solution.py:46
  44.5 2.9 %collective-permute-start.13 = (f32[64,256]{1,0:T(8,128)S(1)}, f32[64,256]{1,0:T(8,128)S(1)}, u32[]{:S(2)}, u32[]{:S(2)}) collective-permute-start(f32[64,256]{1,0:T(8,128)S(1)} %select_add_fusion.1), channel_id=1, source_target_pairs={{0,2},{1,3},{2,0},{3,1},{4,6},{5,7},{6,4},{7,5},{8,10},{9,11},{10,... | collective-permute-start | bytes 196616 | tf_op jit(solution)/shard_map/ppermute | solution.py:62
  52.4 10.1 %collective-permute-start.16 = (f32[64,256]{1,0:T(8,128)S(1)}, f32[64,256]{1,0:T(8,128)S(1)}, u32[]{:S(2)}, u32[]{:S(2)}) collective-permute-start(f32[64,256]{1,0:T(8,128)S(1)} %get-tuple-element.38), channel_id=1, source_target_pairs={{0,240},{1,17},{2,18},{3,243},{4,244},{5,21},{6,22},{7,247},{8,248... | collective-permute-start | bytes 196616 | tf_op jit(solution)/shard_map/ppermute | solution.py:46
  62.6 1.9 %collective-permute-done.16 = f32[64,256]{1,0:T(8,128)S(1)} collective-permute-done((f32[64,256]{1,0:T(8,128)S(1)}, f32[64,256]{1,0:T(8,128)S(1)}, u32[]{:S(2)}, u32[]{:S(2)}) %collective-permute-start.16) | collective-permute-done | bytes 65568 | tf_op jit(solution)/shard_map/ppermute | solution.py:46
  64.5 4.0 %collective-permute-start.17 = (f32[64,256]{1,0:T(8,128)S(1)}, f32[64,256]{1,0:T(8,128)S(1)}, u32[]{:S(2)}, u32[]{:S(2)}) collective-permute-start(f32[64,256]{1,0:T(8,128)S(1)} %select_add_fusion), channel_id=1, source_target_pairs={{0,1},{1,0},{2,3},{3,2},{4,5},{5,4},{6,7},{7,6},{8,9},{9,8},{10,11... | collective-permute-start | bytes 196616 | tf_op jit(solution)/shard_map/ppermute | solution.py:62
  68.5 2.2 %collective-permute-start.18 = (f32[64,256]{1,0:T(8,128)S(1)}, f32[64,256]{1,0:T(8,128)S(1)}, u32[]{:S(2)}, u32[]{:S(2)}) collective-permute-start(f32[64,256]{1,0:T(8,128)S(1)} %select_add_fusion), channel_id=1, source_target_pairs={{0,3},{1,2},{2,1},{3,0},{4,7},{5,6},{6,5},{7,4},{8,11},{9,10},{10,... | collective-permute-start | bytes 196616 | tf_op jit(solution)/shard_map/ppermute | solution.py:62
  70.8 3.2 %collective-permute-done.18 = f32[64,256]{1,0:T(8,128)S(1)} collective-permute-done((f32[64,256]{1,0:T(8,128)S(1)}, f32[64,256]{1,0:T(8,128)S(1)}, u32[]{:S(2)}, u32[]{:S(2)}) %collective-permute-start.18) | collective-permute-done | bytes 65568 | tf_op jit(solution)/shard_map/ppermute | solution.py:62
  74.0 2.5 %collective-permute-done.19 = f32[64,256]{1,0:T(8,128)S(1)} collective-permute-done((f32[64,256]{1,0:T(8,128)S(1)}, f32[64,256]{1,0:T(8,128)S(1)}, u32[]{:S(2)}, u32[]{:S(2)}) %collective-permute-start.19) | collective-permute-done | bytes 65568 | tf_op jit(solution)/shard_map/ppermute | solution.py:62
  78.4 3.4 %collective-permute-start.23 = (f32[72,128]{1,0:T(8,128)S(1)}, f32[72,128]{1,0:T(8,128)S(1)}, u32[]{:S(2)}, u32[]{:S(2)}) collective-permute-start(f32[72,128]{1,0:T(8,128)S(1)} %add.68), channel_id=1, source_target_pairs={{0,64},{4,68},{8,72},{12,76},{16,80},{20,84},{24,88},{28,92},{32,9... | collective-permute-start | bytes 110600 | tf_op jit(solution)/shard_map/ppermute | solution.py:55
  81.7 2.2 %collective-permute-done.21 = f32[72,128]{1,0:T(8,128)S(1)} collective-permute-done((f32[72,128]{1,0:T(8,128)S(1)}, f32[72,128]{1,0:T(8,128)S(1)}, u32[]{:S(2)}, u32[]{:S(2)}) %collective-permute-start.21) | collective-permute-done | bytes 36896 | tf_op jit(solution)/shard_map/ppermute | solution.py:55
  84.1 1.6 %collective-permute-start.25 = (f32[72,128]{1,0:T(8,128)S(1)}, f32[72,128]{1,0:T(8,128)S(1)}, u32[]{:S(2)}, u32[]{:S(2)}) collective-permute-start(f32[72,128]{1,0:T(8,128)S(1)} %add_add_fusion.1), channel_id=1, source_target_pairs={{0,16},{4,20},{8,24},{12,28},{16,0},{20,4},{24,8},{28,12},{32,48},... | collective-permute-start | bytes 110600 | tf_op jit(solution)/shard_map/ppermute | solution.py:55
  85.7 1.8 %collective-permute-start.26 = (f32[72,128]{1,0:T(8,128)S(1)}, f32[72,128]{1,0:T(8,128)S(1)}, u32[]{:S(2)}, u32[]{:S(2)}) collective-permute-start(f32[72,128]{1,0:T(8,128)S(1)} %add_add_fusion.1), channel_id=1, source_target_pairs={{0,8},{4,12},{8,0},{12,4},{16,24},{20,28},{24,16},{28,20},{32,40},... | collective-permute-start | bytes 110600 | tf_op jit(solution)/shard_map/ppermute | solution.py:55
  89.9 3.7 %collective-permute-start.27 = (f32[72,128]{1,0:T(8,128)S(1)}, f32[72,128]{1,0:T(8,128)S(1)}, u32[]{:S(2)}, u32[]{:S(2)}) collective-permute-start(f32[72,128]{1,0:T(8,128)S(1)} %add_add_fusion), channel_id=1, source_target_pairs={{0,56},{4,60},{8,48},{12,52},{16,40},{20,44},{24,32},{28,36},{32,2... | collective-permute-start | bytes 110600 | tf_op jit(solution)/shard_map/ppermute | solution.py:55
  93.6 3.3 %collective-permute-done.27 = f32[72,128]{1,0:T(8,128)S(1)} collective-permute-done((f32[72,128]{1,0:T(8,128)S(1)}, f32[72,128]{1,0:T(8,128)S(1)}, u32[]{:S(2)}, u32[]{:S(2)}) %collective-permute-start.27) | collective-permute-done | bytes 36896 | tf_op jit(solution)/shard_map/ppermute | solution.py:55
  96.9 2.8 %shard_map.56 = (f32[64,512]{1,0:T(8,128)}, f32[64,64]{1,0:T(8,128)}) custom-call(f32[72,128]{1,0:T(8,128)S(1)} %add.75.products_ref, f32[64,512]{1,0:T(8,128)S(1)} %get-tuple-element.41.image_ref), custom_call_target="tpu_custom_call" | custom-call | tf_op jit(solution)/shard_map/pallas_call | solution.py:271
  (56 shorter events, 17.8 us)
Async XLA Ops:
  3.0 11.3 %collective-permute-start = (bf16[528,512]{1,0:T(8,128)(2,1)}, bf16[528,512]{1,0:T(8,128)(2,1)S(1)}, u32[]{:S(2)}, u32[]{:S(2)}) collective-permute-start(bf16[528,512]{1,0:T(8,128)(2,1)} %get-tuple-element.23.own_ref), channel_id=1, source_target_pairs={{0,4},{4,0},{1,5},{5,1},{2,6},{6,2},{3,7},{7,3},{8,12},{12,8},{9,1... | collective-permute-start | bytes 1622024 | tf_op jit(solution)/shard_map/ppermute | solution.py:50
  3.1 17.9 %collective-permute-start.3 = (bf16[272,512]{1,0:T(8,128)(2,1)}, bf16[272,512]{1,0:T(8,128)(2,1)S(1)}, u32[]{:S(2)}, u32[]{:S(2)}) collective-permute-start(bf16[272,512]{1,0:T(8,128)(2,1)} %get-tuple-element.26), channel_id=1, source_target_pairs={{0,248},{1,9},{2,10},{3,251},{4,252},{5,13},{6,14},{7,255},{8,0},{... | collective-permute-start | bytes 835592 | tf_op jit(solution)/shard_map/ppermute | solution.py:46
  5.1 16.0 %collective-permute-start.1 = (bf16[208,512]{1,0:T(8,128)(2,1)}, bf16[208,512]{1,0:T(8,128)(2,1)S(1)}, u32[]{:S(2)}, u32[]{:S(2)}) collective-permute-start(bf16[208,512]{1,0:T(8,128)(2,1)} %get-tuple-element.24), channel_id=1, source_target_pairs={{0,16},{1,241},{2,242},{3,19},{4,20},{5,245},{6,246},{7,23},{8,24}... | collective-permute-start | bytes 638984 | tf_op jit(solution)/shard_map/ppermute | solution.py:46
  6.6 21.2 %collective-permute-start.8 = (f32[64,512]{1,0:T(8,128)S(1)}, f32[64,512]{1,0:T(8,128)S(1)}, u32[]{:S(2)}, u32[]{:S(2)}) collective-permute-start(f32[64,512]{1,0:T(8,128)S(1)} %bitcast.2), channel_id=1, source_target_pairs={{0,4},{4,0},{1,5},{5,1},{2,6},{6,2},{3,7},{7,3},{8,12},{12,8},{9,1... | collective-permute-start | bytes 393224 | tf_op jit(solution)/shard_map/ppermute | solution.py:50
  6.6 14.4 %collective-permute-start.2 = (bf16[64,512]{1,0:T(8,128)(2,1)}, bf16[64,512]{1,0:T(8,128)(2,1)S(1)}, u32[]{:S(2)}, u32[]{:S(2)}) collective-permute-start(bf16[64,512]{1,0:T(8,128)(2,1)} %get-tuple-element.25), channel_id=1, source_target_pairs={{0,241},{1,16},{2,19},{3,242},{4,245},{5,20},{6,23},{7,246},{8,249... | collective-permute-start | bytes 196616 | tf_op jit(solution)/shard_map/ppermute | solution.py:46
  23.7 4.9 %collective-permute-start.6 = (f32[1,1024]{1,0:T(1,128)S(1)}, f32[1,1024]{1,0:T(1,128)S(1)}, u32[]{:S(2)}, u32[]{:S(2)}) collective-permute-start(f32[1,1024]{1,0:T(1,128)S(1)} %add.59.sum_ref), channel_id=1, source_target_pairs={{0,3},{1,2},{2,1},{3,0},{4,7},{5,6},{6,5},{7,4},{8,11},{9,10},{10,... | collective-permute-start | bytes 12296 | tf_op jit(solution)/shard_map/ppermute | solution.py:62
  25.8 5.1 %collective-permute-start.7 = (f32[1,1024]{1,0:T(1,128)S(1)}, f32[1,1024]{1,0:T(1,128)S(1)}, u32[]{:S(2)}, u32[]{:S(2)}) collective-permute-start(f32[1,1024]{1,0:T(1,128)S(1)} %add.59.sum_ref), channel_id=1, source_target_pairs={{0,2},{1,3},{2,0},{3,1},{4,6},{5,7},{6,4},{7,5},{8,10},{9,11},{10,... | collective-permute-start | bytes 12296 | tf_op jit(solution)/shard_map/ppermute | solution.py:62
  31.3 7.9 %collective-permute-start.10 = (f32[64,256]{1,0:T(8,128)S(1)}, f32[64,256]{1,0:T(8,128)S(1)}, u32[]{:S(2)}, u32[]{:S(2)}) collective-permute-start(f32[64,256]{1,0:T(8,128)S(1)} %get-tuple-element.35), channel_id=1, source_target_pairs={{0,240},{1,17},{2,18},{3,243},{4,244},{5,21},{6,22},{7,247},{8,248... | collective-permute-start | bytes 196616 | tf_op jit(solution)/shard_map/ppermute | solution.py:46
  36.5 6.8 %collective-permute-start.9 = (f32[64,256]{1,0:T(8,128)S(1)}, f32[64,256]{1,0:T(8,128)S(1)}, u32[]{:S(2)}, u32[]{:S(2)}) collective-permute-start(f32[64,256]{1,0:T(8,128)S(1)} %get-tuple-element.34), channel_id=1, source_target_pairs={{0,8},{1,249},{2,250},{3,11},{4,12},{5,253},{6,254},{7,15},{8,16},... | collective-permute-start | bytes 196616 | tf_op jit(solution)/shard_map/ppermute | solution.py:46
  43.3 4.4 %collective-permute-start.11 = (f32[64,256]{1,0:T(8,128)S(1)}, f32[64,256]{1,0:T(8,128)S(1)}, u32[]{:S(2)}, u32[]{:S(2)}) collective-permute-start(f32[64,256]{1,0:T(8,128)S(1)} %select_add_fusion.1), channel_id=1, source_target_pairs={{0,1},{1,0},{2,3},{3,2},{4,5},{5,4},{6,7},{7,6},{8,9},{9,8},{10,11... | collective-permute-start | bytes 196616 | tf_op jit(solution)/shard_map/ppermute | solution.py:62
  43.4 5.6 %collective-permute-start.12 = (f32[64,256]{1,0:T(8,128)S(1)}, f32[64,256]{1,0:T(8,128)S(1)}, u32[]{:S(2)}, u32[]{:S(2)}) collective-permute-start(f32[64,256]{1,0:T(8,128)S(1)} %select_add_fusion.1), channel_id=1, source_target_pairs={{0,3},{1,2},{2,1},{3,0},{4,7},{5,6},{6,5},{7,4},{8,11},{9,10},{10,... | collective-permute-start | bytes 196616 | tf_op jit(solution)/shard_map/ppermute | solution.py:62
  44.5 5.8 %collective-permute-start.13 = (f32[64,256]{1,0:T(8,128)S(1)}, f32[64,256]{1,0:T(8,128)S(1)}, u32[]{:S(2)}, u32[]{:S(2)}) collective-permute-start(f32[64,256]{1,0:T(8,128)S(1)} %select_add_fusion.1), channel_id=1, source_target_pairs={{0,2},{1,3},{2,0},{3,1},{4,6},{5,7},{6,4},{7,5},{8,10},{9,11},{10,... | collective-permute-start | bytes 196616 | tf_op jit(solution)/shard_map/ppermute | solution.py:62
  52.2 10.4 %collective-permute-start.15 = (f32[64,256]{1,0:T(8,128)S(1)}, f32[64,256]{1,0:T(8,128)S(1)}, u32[]{:S(2)}, u32[]{:S(2)}) collective-permute-start(f32[64,256]{1,0:T(8,128)S(1)} %get-tuple-element.37), channel_id=1, source_target_pairs={{0,8},{1,249},{2,250},{3,11},{4,12},{5,253},{6,254},{7,15},{8,16},... | collective-permute-start | bytes 196616 | tf_op jit(solution)/shard_map/ppermute | solution.py:46
  52.4 12.0 %collective-permute-start.16 = (f32[64,256]{1,0:T(8,128)S(1)}, f32[64,256]{1,0:T(8,128)S(1)}, u32[]{:S(2)}, u32[]{:S(2)}) collective-permute-start(f32[64,256]{1,0:T(8,128)S(1)} %get-tuple-element.38), channel_id=1, source_target_pairs={{0,240},{1,17},{2,18},{3,243},{4,244},{5,21},{6,22},{7,247},{8,248... | collective-permute-start | bytes 196616 | tf_op jit(solution)/shard_map/ppermute | solution.py:46
  64.5 6.3 %collective-permute-start.17 = (f32[64,256]{1,0:T(8,128)S(1)}, f32[64,256]{1,0:T(8,128)S(1)}, u32[]{:S(2)}, u32[]{:S(2)}) collective-permute-start(f32[64,256]{1,0:T(8,128)S(1)} %select_add_fusion), channel_id=1, source_target_pairs={{0,1},{1,0},{2,3},{3,2},{4,5},{5,4},{6,7},{7,6},{8,9},{9,8},{10,11... | collective-permute-start | bytes 196616 | tf_op jit(solution)/shard_map/ppermute | solution.py:62
  68.5 5.5 %collective-permute-start.18 = (f32[64,256]{1,0:T(8,128)S(1)}, f32[64,256]{1,0:T(8,128)S(1)}, u32[]{:S(2)}, u32[]{:S(2)}) collective-permute-start(f32[64,256]{1,0:T(8,128)S(1)} %select_add_fusion), channel_id=1, source_target_pairs={{0,3},{1,2},{2,1},{3,0},{4,7},{5,6},{6,5},{7,4},{8,11},{9,10},{10,... | collective-permute-start | bytes 196616 | tf_op jit(solution)/shard_map/ppermute | solution.py:62
  70.7 5.8 %collective-permute-start.19 = (f32[64,256]{1,0:T(8,128)S(1)}, f32[64,256]{1,0:T(8,128)S(1)}, u32[]{:S(2)}, u32[]{:S(2)}) collective-permute-start(f32[64,256]{1,0:T(8,128)S(1)} %select_add_fusion), channel_id=1, source_target_pairs={{0,2},{1,3},{2,0},{3,1},{4,6},{5,7},{6,4},{7,5},{8,10},{9,11},{10,... | collective-permute-start | bytes 196616 | tf_op jit(solution)/shard_map/ppermute | solution.py:62
  78.3 5.7 %collective-permute-start.21 = (f32[72,128]{1,0:T(8,128)S(1)}, f32[72,128]{1,0:T(8,128)S(1)}, u32[]{:S(2)}, u32[]{:S(2)}) collective-permute-start(f32[72,128]{1,0:T(8,128)S(1)} %add.68), channel_id=1, source_target_pairs={{0,128},{4,132},{8,136},{12,140},{16,144},{20,148},{24,152},{28,15... | collective-permute-start | bytes 110600 | tf_op jit(solution)/shard_map/ppermute | solution.py:55
  78.3 5.7 %collective-permute-start.22 = (f32[72,128]{1,0:T(8,128)S(1)}, f32[72,128]{1,0:T(8,128)S(1)}, u32[]{:S(2)}, u32[]{:S(2)}) collective-permute-start(f32[72,128]{1,0:T(8,128)S(1)} %add.68), channel_id=1, source_target_pairs={{0,192},{4,196},{8,200},{12,204},{16,208},{20,212},{24,216},{28,22... | collective-permute-start | bytes 110600 | tf_op jit(solution)/shard_map/ppermute | solution.py:55
  78.4 5.6 %collective-permute-start.23 = (f32[72,128]{1,0:T(8,128)S(1)}, f32[72,128]{1,0:T(8,128)S(1)}, u32[]{:S(2)}, u32[]{:S(2)}) collective-permute-start(f32[72,128]{1,0:T(8,128)S(1)} %add.68), channel_id=1, source_target_pairs={{0,64},{4,68},{8,72},{12,76},{16,80},{20,84},{24,88},{28,92},{32,9... | collective-permute-start | bytes 110600 | tf_op jit(solution)/shard_map/ppermute | solution.py:55
  84.0 4.2 %collective-permute-start.24 = (f32[72,128]{1,0:T(8,128)S(1)}, f32[72,128]{1,0:T(8,128)S(1)}, u32[]{:S(2)}, u32[]{:S(2)}) collective-permute-start(f32[72,128]{1,0:T(8,128)S(1)} %add_add_fusion.1), channel_id=1, source_target_pairs={{0,24},{4,28},{8,16},{12,20},{16,8},{20,12},{24,0},{28,4},{32,56},... | collective-permute-start | bytes 110600 | tf_op jit(solution)/shard_map/ppermute | solution.py:55
  84.1 4.9 %collective-permute-start.25 = (f32[72,128]{1,0:T(8,128)S(1)}, f32[72,128]{1,0:T(8,128)S(1)}, u32[]{:S(2)}, u32[]{:S(2)}) collective-permute-start(f32[72,128]{1,0:T(8,128)S(1)} %add_add_fusion.1), channel_id=1, source_target_pairs={{0,16},{4,20},{8,24},{12,28},{16,0},{20,4},{24,8},{28,12},{32,48},... | collective-permute-start | bytes 110600 | tf_op jit(solution)/shard_map/ppermute | solution.py:55
  85.7 4.2 %collective-permute-start.26 = (f32[72,128]{1,0:T(8,128)S(1)}, f32[72,128]{1,0:T(8,128)S(1)}, u32[]{:S(2)}, u32[]{:S(2)}) collective-permute-start(f32[72,128]{1,0:T(8,128)S(1)} %add_add_fusion.1), channel_id=1, source_target_pairs={{0,8},{4,12},{8,0},{12,4},{16,24},{20,28},{24,16},{28,20},{32,40},... | collective-permute-start | bytes 110600 | tf_op jit(solution)/shard_map/ppermute | solution.py:55
  89.9 7.1 %collective-permute-start.27 = (f32[72,128]{1,0:T(8,128)S(1)}, f32[72,128]{1,0:T(8,128)S(1)}, u32[]{:S(2)}, u32[]{:S(2)}) collective-permute-start(f32[72,128]{1,0:T(8,128)S(1)} %add_add_fusion), channel_id=1, source_target_pairs={{0,56},{4,60},{8,48},{12,52},{16,40},{20,44},{24,32},{28,36},{32,2... | collective-permute-start | bytes 110600 | tf_op jit(solution)/shard_map/ppermute | solution.py:55
  (6 other events, 15.1 us)
